TPU v7x, 256 devices: a whole 4x4x8 slice. The times are simulated.
256 devices in a mesh: genome: 128 (over y_lo, x, z, core), chan: 2 (over y_hi).
Axes of the slice: x: 4, y: 4 (y_hi: 2, y_lo: 2; y = y_hi * 2 + y_lo), z: 8, core: 2. Of those that a mesh axis runs over, the one named last changes fastest.
Arguments:
- embeddings: bfloat16 [4096, 512], P('genome'), may hold values from -6 to 6
- bin_mask: int32 [4096], P('genome'), may hold values 0 or 1
- target: float32 [4096, 256], P('genome'), may hold values from -6 to 6
- proj_weight: bfloat16 [512, 64], P(None, 'chan'), may hold values from -0.25 to 0.25
- dist_bias: bfloat16 [64, 256], P('chan'), may hold values from -3 to 3
- pair_kernel: bfloat16 [9, 64, 64], P(None, 'chan'), may hold values from -0.25 to 0.25
- head_kernel: bfloat16 [9, 64], P(None, 'chan'), may hold values from -0.25 to 0.25
- dilations: int32 [2], replicated, may hold values from 1 to 4, as said below
Outputs:
- emb_grad: float32 [4096, 512], P('genome', 'chan')
- proj_grad: float32 [512, 64], P(None, 'chan')
- pair_grad: float32 [9, 64, 64], P(None, 'chan')
- head_grad: float32 [9, 64], P(None, 'chan')
Inputs may be any that keep to these rules, and one draw needn't show every extreme that they name: `dilations`: one of the two rates is 4.
All inputs are finite; a program needn't handle non-finite values. No bound on the sum of `bin_mask` on one device may be relied on, other than what follows from the above.
Results may differ from a plain program's by a relative error of at most 0.0075.
Values may be sent and summed in bfloat16 or wider, within the bound.
No kernel may reach another device: no remote copies, remote signals or barrier semaphores. Data moves between devices by JAX's collectives and lax.ppermute only.
A program may use at most 64 MiB of HBM per device.

v0:
```python
import jax
import jax.numpy as jnp
from jax import lax
from jax.sharding import PartitionSpec as P

MAXDIL = 4


tap_pairs = ((-1, -1), (-1, 0), (-1, 1), (0, -1), (0, 0), (0, 1), (1, -1), (1, 0), (1, 1))


def passed_along(value, axis, by):
    length = lax.axis_size(axis)
    pairs = [(i, i + by) for i in range(length) if 0 <= i + by < length]
    return lax.ppermute(value, axis, pairs)


def padded_2(value, sides, width):
    for axis, dim in sides:
        size, length = (lax.axis_size(axis), value.shape[dim])
        up = [(i, (i + 1) % size) for i in range(size - 1)]
        down = [(j, i) for i, j in up]
        last = lax.slice_in_dim(value, length - width, length, axis=dim)
        leading = lax.slice_in_dim(value, 0, width, axis=dim)
        before = lax.ppermute(last, axis, up)
        after = lax.ppermute(leading, axis, down)
        value = jnp.concatenate([before, value, after], axis=dim)
    return value


def silu_slope(values):
    sigma = jax.nn.sigmoid(values)
    return sigma * (1.0 + values * (1.0 - sigma))


def pad_columns(values):
    return jnp.pad(values, ((0, 0), (0, 0), (2 * MAXDIL, 2 * MAXDIL)))


def tap_view(padded, row_count, rate, row_tap, col_tap, orient):
    zero_start = jnp.zeros((), jnp.int32)
    row_first = MAXDIL + orient * row_tap * rate
    col_first = 2 * MAXDIL + orient * (col_tap - row_tap) * rate
    return lax.dynamic_slice(
        padded,
        (zero_start, row_first, col_first),
        (padded.shape[0], row_count, padded.shape[2] - 4 * MAXDIL),
    )


def pair_inputs(extended, first, amount, band_cols):
    offsets = (
        first
        + jnp.arange(amount, dtype=jnp.int32)[:, None]
        + jnp.arange(band_cols, dtype=jnp.int32)[None, :]
    )
    partners = extended[offsets]
    own_rows = lax.dynamic_slice_in_dim(extended, first, amount, 0)
    product = (own_rows[:, None, :].astype(jnp.float32) * partners.astype(jnp.float32)).astype(
        jnp.bfloat16
    )
    return (product, partners, own_rows, offsets)


def project(extended, weight, bias_rows, inside, row_count, band_cols):
    block_rows = min(16, row_count)

    def forward_block(index, carried):
        hidden, deriv = carried
        first = (index * block_rows).astype(jnp.int32)
        product, partners, own_rows, offsets = pair_inputs(extended, first, block_rows, band_cols)
        pre = jnp.einsum("tde,ec->ctd", product, weight, preferred_element_type=jnp.float32)
        pre = pre + bias_rows.astype(jnp.float32)[:, None, :]
        near = lax.dynamic_slice_in_dim(inside, first, block_rows, 0)
        value = (jax.nn.silu(pre) * near[None]).astype(jnp.bfloat16)
        slope_value = silu_slope(pre) * near[None]
        hidden = lax.dynamic_update_slice_in_dim(hidden, value, first, 1)
        deriv = lax.dynamic_update_slice_in_dim(deriv, slope_value, first, 1)
        return (hidden, deriv)

    start_hidden = (
        jnp.zeros((weight.shape[1], row_count, band_cols), jnp.bfloat16),
        jnp.zeros((weight.shape[1], row_count, band_cols), jnp.float32),
    )
    return lax.fori_loop(0, row_count // block_rows, forward_block, start_hidden)


def local(
    embeddings, bin_mask, target, proj_weight, dist_bias, pair_kernel, head_kernel, dilations
):
    row_count = embeddings.shape[0]
    band_cols = target.shape[1]
    channels_own = proj_weight.shape[1]
    reach = band_cols // row_count
    total_bins = row_count * lax.axis_size("genome")
    first_row = lax.axis_index("genome") * row_count
    rate_pair = dilations[0]
    rate_head = dilations[1]
    arrived = [
        passed_along((embeddings, bin_mask), "genome", -distance)
        for distance in range(1, reach + 1)
    ]
    extended = jnp.concatenate([embeddings] + [entry[0] for entry in arrived], 0)
    mask_ext = jnp.concatenate([bin_mask] + [entry[1] for entry in arrived], 0)
    local_index = (
        jnp.arange(row_count, dtype=jnp.int32)[:, None]
        + jnp.arange(band_cols, dtype=jnp.int32)[None, :]
    )
    inside = (first_row + local_index < total_bins).astype(jnp.float32)
    loss_mask = bin_mask[:, None].astype(jnp.float32) * mask_ext[local_index].astype(jnp.float32)
    hidden_own, deriv_zero = project(extended, proj_weight, dist_bias, inside, row_count, band_cols)
    source_rim = padded_2(hidden_own, (("genome", 1),), MAXDIL)
    hidden_full = lax.all_gather(source_rim, "chan", axis=0, tiled=True)
    padded_zero = pad_columns(hidden_full)
    pre_pair = jnp.zeros((channels_own, row_count, band_cols), jnp.float32)
    for tap, (row_tap, col_tap) in enumerate(tap_pairs):
        view = tap_view(padded_zero, row_count, rate_pair, row_tap, col_tap, 1)
        pre_pair = pre_pair + jnp.einsum(
            "oc,cid->oid", pair_kernel[tap], view, preferred_element_type=jnp.float32
        )
    hidden_one = (jax.nn.silu(pre_pair) * inside[None]).astype(jnp.bfloat16)
    deriv_one = silu_slope(pre_pair) * inside[None]
    padded_one = pad_columns(padded_2(hidden_one, (("genome", 1),), MAXDIL))
    partial_pred = jnp.zeros((row_count, band_cols), jnp.float32)
    for tap, (row_tap, col_tap) in enumerate(tap_pairs):
        view = tap_view(padded_one, row_count, rate_head, row_tap, col_tap, 1)
        partial_pred = partial_pred + jnp.einsum(
            "c,cid->id", head_kernel[tap], view, preferred_element_type=jnp.float32
        )
    prediction = lax.psum(partial_pred, "chan")
    residual_grad = loss_mask * (prediction - target) / band_cols
    grad_rows = padded_2(residual_grad, (("genome", 0),), MAXDIL)
    padded_grad = pad_columns(grad_rows[None])
    head_terms = []
    hidden_grad = jnp.zeros((channels_own, row_count, band_cols), jnp.float32)
    for tap, (row_tap, col_tap) in enumerate(tap_pairs):
        view = tap_view(padded_one, row_count, rate_head, row_tap, col_tap, 1)
        head_terms.append(jnp.einsum("cid,id->c", view.astype(jnp.float32), residual_grad))
        back_view = tap_view(padded_grad, row_count, rate_head, row_tap, col_tap, -1)
        hidden_grad = hidden_grad + head_kernel[tap].astype(jnp.float32)[:, None, None] * back_view
    head_acc = jnp.stack(head_terms)
    slope_one = (hidden_grad * deriv_one).astype(jnp.bfloat16)
    pair_terms = []
    for tap, (row_tap, col_tap) in enumerate(tap_pairs):
        view = tap_view(padded_zero, row_count, rate_pair, row_tap, col_tap, 1)
        pair_terms.append(
            jnp.einsum("oid,cid->oc", slope_one, view, preferred_element_type=jnp.float32)
        )
    pair_acc = jnp.stack(pair_terms)
    slope_rim = padded_2(slope_one, (("genome", 1),), MAXDIL)
    padded_slope = pad_columns(slope_rim)
    totals = jnp.zeros((channels_own * lax.axis_size("chan"), row_count, band_cols), jnp.float32)
    for tap, (row_tap, col_tap) in enumerate(tap_pairs):
        kernel_cols = pair_kernel[tap]
        back_view = tap_view(padded_slope, row_count, rate_pair, row_tap, col_tap, -1)
        totals = totals + jnp.einsum(
            "oc,oid->cid", kernel_cols, back_view, preferred_element_type=jnp.float32
        )
    zero_grad = lax.psum_scatter(totals, "chan", scatter_dimension=0, tiled=True)
    slope_zero = (zero_grad * deriv_zero).astype(jnp.bfloat16)
    block_rows = min(16, row_count)

    def backward_block(index, carried):
        proj_acc, grad_ext = carried
        first = (index * block_rows).astype(jnp.int32)
        product, partners, own_rows, offsets = pair_inputs(extended, first, block_rows, band_cols)
        piece_rows = lax.dynamic_slice_in_dim(slope_zero, first, block_rows, 1)
        proj_acc = proj_acc + jnp.einsum(
            "tde,ctd->ec", product, piece_rows, preferred_element_type=jnp.float32
        )
        slope = jnp.einsum(
            "ctd,ec->tde", piece_rows, proj_weight, preferred_element_type=jnp.float32
        )
        own_term = jnp.sum(slope * partners.astype(jnp.float32), axis=1)
        grad_ext = grad_ext.at[offsets].add(slope * own_rows.astype(jnp.float32)[:, None, :])
        current = lax.dynamic_slice_in_dim(grad_ext, first, block_rows, 0)
        grad_ext = lax.dynamic_update_slice_in_dim(grad_ext, current + own_term, first, 0)
        return (proj_acc, grad_ext)

    start_state = (
        jnp.zeros((embeddings.shape[1], channels_own), jnp.float32),
        jnp.zeros((row_count + band_cols, embeddings.shape[1]), jnp.float32),
    )
    proj_acc, grad_ext = lax.fori_loop(0, row_count // block_rows, backward_block, start_state)
    own_half, partner_half = (
        lax.psum_scatter(grad_ext[:row_count], "chan", scatter_dimension=1, tiled=True),
        lax.psum_scatter(grad_ext[row_count:], "chan", scatter_dimension=1, tiled=True),
    )
    blocks_back = [
        partner_half[distance * row_count : (distance + 1) * row_count] for distance in range(reach)
    ]
    for distance in range(1, reach + 1):
        own_half = own_half + passed_along(blocks_back[distance - 1], "genome", distance)
    summed = lax.psum((proj_acc, pair_acc, head_acc), "genome")
    inverse = 1.0 / total_bins
    return (own_half, summed[0] * inverse, summed[1] * inverse, summed[2] * inverse)


def solution(mesh):
    return jax.shard_map(
        local,
        mesh=mesh,
        in_specs=(
            P("genome", None),
            P("genome"),
            P("genome", None),
            P(None, "chan"),
            P("chan", None),
            P(None, "chan", None),
            P(None, "chan"),
            P(),
        ),
        out_specs=(P("genome", "chan"), P(None, "chan"), P(None, "chan", None), P(None, "chan")),
        check_vma=False,
    )
```

profile of v0, /device:TPU:1, one launch (start us, length us, event | category | flops | bytes accessed | tf_op | source)
XLA Modules:
  0.0 1651.0 jit_solution(14922035784763464290)
XLA Ops:
  7.2 5.2 collective-permute-start
  22.8 3.3 collective-permute-done.4
  27.9 4.2 collective-permute-done.6
  33.9 42.5 %while.31 = (s32[]{:T(128)}, bf16[32,32,256]{2,0,1:T(8,128)(2,1)S(1)}, f32[32,32,256]{2,0,1:T(8,128)S(1)}, bf16[288,512]{1,0:T(8,128)(2,1)S(1)}, bf16[512,32]{0,...) while((s32[]{:T(128)}, ...), condition=%wide.region_1.2_spmd, body=%wide.region_0.1_spmd.sunk | while | flops 142512144 | bytes 14778704 | solution.py:85
  34.1 17.3 %gather_fusion = bf16[4096,512]{1,0:T(8,128)(2,1)} fusion(bf16[288,512]{1,0:T(8,128)(2,1)S(1)} %get-tuple-element.449, s32[4096]{0:T(1024)S(1)} %broadcast_clamp_fusion.5), kind=kCustom, calls=%fused_computation.clone.1 | custom fusion | bytes 8404992 | tf_op jit(solution)/shard_map/while/body/eval_jaxpr/gather | solution.py:57
  51.4 3.6 fusion.266
  55.3 17.3 %gather_fusion = bf16[4096,512]{1,0:T(8,128)(2,1)} fusion(bf16[288,512]{1,0:T(8,128)(2,1)S(1)} %get-tuple-element.449, s32[4096]{0:T(1024)S(1)} %broadcast_clamp_fusion.5), kind=kCustom, calls=%fused_computation.clone.1 | custom fusion | bytes 8404992 | tf_op jit(solution)/shard_map/while/body/eval_jaxpr/gather | solution.py:57
  72.6 3.6 fusion.266
  76.5 5.6 collective-permute-start.16
  84.0 3.6 collective-permute-done.17
  109.6 7.7 collective-permute-done.15
  117.5 51.2 %gather_fusion.2 = s32[8192]{0:T(1024)S(1)} fusion(s32[288]{0:T(512)S(1)} %concatenate.19, s32[8192]{0:T(1024)S(1)} %broadcast_clamp_fusion.2), kind=kCustom, calls=%fused_computation.2 | custom fusion | bytes 98304 | tf_op jit(solution)/shard_map/gather | solution.py:110
  175.8 6.6 collective-permute-start.18
  184.6 3.5 collective-permute-done.19
  191.3 8.9 psum.28
  200.3 3.9 collective-permute-start.20
  229.2 301.4 %psum.31 = f32[9,32]{1,0:T(8,128)} all-reduce(f32[9,32]{1,0:T(8,128)S(1)} %stack.79), channel_id=1, replica_groups=mesh['genome'=128,'chan'=2] {'genome'}, use_global_device_ids=true, to_apply=%region_12.13 | all-reduce | flops 288 | bytes 2304 | tf_op jit(solution)/shard_map/psum | solution.py:194
  535.3 105.8 %while.32 = (s32[]{:T(128)}, f32[512,32]{0,1:T(8,128)S(1)}, f32[288,512]{1,0:T(8,128)S(1)}, bf16[288,512]{1,0:T(8,128)(2,1)S(1)}, bf16[32,32,256]{2,0,1:T(8,128)...) while((s32[]{:T(128)}, f32[512,32]{0,1:T(8,128)S(1)}, ...), condition=%wide.region_7.8_spmd.clone, body=%wide.region_4.7_spmd.clone.sunk | while | flops 285274144 | bytes 51380560 | solution.py:184
  535.5 17.3 %gather_fusion.1 = bf16[4096,512]{1,0:T(8,128)(2,1)} fusion(bf16[288,512]{1,0:T(8,128)(2,1)S(1)} %get-tuple-element.483, s32[4096]{0:T(1024)S(1)} %broadcast_clamp_fusion.6), kind=kCustom, calls=%fused_computation.1.clone.clone.1 | custom fusion | bytes 8404992 | tf_op jit(solution)/shard_map/while/body/eval_jaxpr/gather | solution.py:57
  552.7 6.9 fusion.271
  559.6 25.4 %scatter_fusion = f32[288,512]{1,0:T(8,128)S(1)} fusion(f32[288,512]{1,0:T(8,128)S(1)} %get-tuple-element.471, s32[4096]{0:T(1024)S(1)} %bitcast.346, f32[4096,512]{1,0:T(8,128)} %bitcast.342), kind=kCustom, calls=%fused_computation.3.clone.clone.1 | custom fusion | flops 2097152 | bytes 25182208 | tf_op jit(solution)/shard_map/while/body/eval_jaxpr/scatter-add | solution.py:175
  585.0 3.2 fusion.270
  588.4 17.3 %gather_fusion.1 = bf16[4096,512]{1,0:T(8,128)(2,1)} fusion(bf16[288,512]{1,0:T(8,128)(2,1)S(1)} %get-tuple-element.483, s32[4096]{0:T(1024)S(1)} %broadcast_clamp_fusion.6), kind=kCustom, calls=%fused_computation.1.clone.clone.1 | custom fusion | bytes 8404992 | tf_op jit(solution)/shard_map/while/body/eval_jaxpr/gather | solution.py:57
  605.7 6.9 fusion.271
  612.5 25.4 %scatter_fusion = f32[288,512]{1,0:T(8,128)S(1)} fusion(f32[288,512]{1,0:T(8,128)S(1)} %get-tuple-element.471, s32[4096]{0:T(1024)S(1)} %bitcast.346, f32[4096,512]{1,0:T(8,128)} %bitcast.342), kind=kCustom, calls=%fused_computation.3.clone.clone.1 | custom fusion | flops 2097152 | bytes 25182208 | tf_op jit(solution)/shard_map/while/body/eval_jaxpr/scatter-add | solution.py:175
  638.0 3.2 fusion.270
  649.1 29.4 %reduce-scatter.8.cloned.1.call-done = f32[256,256]{1,0:T(8,128)} async-done(((f32[256,512]{1,0:T(8,128)}), f32[256,256]{1,0:T(8,128)}) %reduce-scatter.8.cloned.1.call-update) | async-done | bytes 262160 | tf_op jit(solution)/shard_map/reduce_scatter | solution.py:187
  679.4 3.8 collective-permute-start.24
  683.2 3.2 collective-permute-start.25
  686.4 3.2 collective-permute-start.26
  689.6 938.7 %all-reduce.7.cloned.1.call-done = (f32[512,32]{0,1:T(8,128)}, f32[9,32,64]{2,1,0:T(8,128)}) async-done(((f32[512,32]{0,1:T(8,128)}, f32[9,32,64]{2,1,0:T(8,128)}), (f32[512,32]{0,1:T(8,128)}, f32[9,32,64]{2,1,0:T(8,128)})) %all-reduce.7.cloned.1.call-update) | async-done | bytes 139280 | tf_op jit(solution)/shard_map/psum | solution.py:194
  1637.8 5.2 reduce-scatter.6.cloned.1.call-done
  (215 shorter events, 90.9 us)
Async XLA Ops:
  7.2 161.6 %all-gather.2.cloned.1.call-start = ((), (), s32[]{:S(2)}) async-start(), calls=%async_computation.3 | async-start | bytes 1966080 | tf_op jit(solution)/shard_map/all_gather | solution.py:113
  7.2 11.1 collective-permute-start
  12.4 7.3 collective-permute-start.1
  13.7 7.3 collective-permute-start.2
  15.0 7.8 collective-permute-start.3
  16.3 9.9 collective-permute-start.4
  18.4 9.5 collective-permute-start.5
  19.7 12.4 collective-permute-start.6
  21.0 12.7 collective-permute-start.7
  76.5 7.5 collective-permute-start.16
  88.6 444.2 %reduce-scatter.4.cloned.1.call-start = ((), (), s32[]{:S(2)}) async-start(), calls=%async_computation.4 | async-start | bytes 3145728 | tf_op jit(solution)/shard_map/reduce_scatter | solution.py:159
  88.7 16.4 collective-permute-start.10
  90.0 16.4 collective-permute-start.11
  91.3 17.0 %collective-permute-start.12 = (s32[32]{0:T(128)S(1)}, s32[32]{0:T(128)S(1)}, u32[]{:S(2)}, u32[]{:S(2)}) collective-permute-start(s32[32]{0:T(128)S(1)} %copy-done.16), channel_id=1, source_target_pairs={{10,0},{12,2},{14,4},{16,6},{18,8},{20,10},{22,12},{24,14},{26,16}... | collective-permute-start | bytes 392 | tf_op jit(solution)/shard_map/ppermute | solution.py:15
  92.6 17.0 %collective-permute-start.13 = (s32[32]{0:T(128)S(1)}, s32[32]{0:T(128)S(1)}, u32[]{:S(2)}, u32[]{:S(2)}) collective-permute-start(s32[32]{0:T(128)S(1)} %copy-done.16), channel_id=1, source_target_pairs={{12,0},{14,2},{16,4},{18,6},{20,8},{22,10},{24,12},{26,14},{28,16}... | collective-permute-start | bytes 392 | tf_op jit(solution)/shard_map/ppermute | solution.py:15
  93.9 15.7 collective-permute-start.14
  105.0 12.3 collective-permute-start.15
  106.4 11.0 collective-permute-start.8
  108.3 9.1 collective-permute-start.9
  175.8 8.8 collective-permute-start.18
  200.3 6.0 collective-permute-start.20
  226.2 452.3 %reduce-scatter.8.cloned.1.call-start = ((), (), s32[]{:S(2)}) async-start(), calls=%async_computation.6 | async-start | bytes 786432 | tf_op jit(solution)/shard_map/reduce_scatter | solution.py:187
  642.0 986.2 %all-reduce.7.cloned.1.call-start = ((), (), s32[]{:S(2)}) async-start(), calls=%async_computation.7 | async-start | bytes 425984 | tf_op jit(solution)/shard_map/psum | solution.py:194
  647.7 995.3 %reduce-scatter.6.cloned.1.call-start = ((), (), s32[]{:S(2)}) async-start(), calls=%async_computation.5 | async-start | bytes 98304 | tf_op jit(solution)/shard_map/reduce_scatter | solution.py:186
  679.4 953.0 %collective-permute-start.24 = (f32[32,256]{1,0:T(8,128)S(1)}, f32[32,256]{1,0:T(8,128)S(1)}, u32[]{:S(2)}, u32[]{:S(2)}) collective-permute-start(f32[32,256]{1,0:T(8,128)S(1)} %get-tuple-element.302), channel_id=1, source_target_pairs={{0,2},{2,4},{4,6},{6,8},{8,10},{10,12},{12,14},{14,16},{16,18},{18... | collective-permute-start | bytes 98312 | tf_op jit(solution)/shard_map/ppermute | solution.py:15
  683.2 950.6 %collective-permute-start.25 = (f32[32,256]{1,0:T(8,128)S(1)}, f32[32,256]{1,0:T(8,128)S(1)}, u32[]{:S(2)}, u32[]{:S(2)}) collective-permute-start(f32[32,256]{1,0:T(8,128)S(1)} %get-tuple-element.309), channel_id=1, source_target_pairs={{0,4},{2,6},{4,8},{6,10},{8,12},{10,14},{12,16},{14,18},{16,20},{1... | collective-permute-start | bytes 98312 | tf_op jit(solution)/shard_map/ppermute | solution.py:15
  686.4 948.7 %collective-permute-start.26 = (f32[32,256]{1,0:T(8,128)S(1)}, f32[32,256]{1,0:T(8,128)S(1)}, u32[]{:S(2)}, u32[]{:S(2)}) collective-permute-start(f32[32,256]{1,0:T(8,128)S(1)} %get-tuple-element.308), channel_id=1, source_target_pairs={{0,6},{2,8},{4,10},{6,12},{8,14},{10,16},{12,18},{14,20},{16,22},{... | collective-permute-start | bytes 98312 | tf_op jit(solution)/shard_map/ppermute | solution.py:15
  1629.8 13.2 collective-permute-start.27
  1631.1 11.9 collective-permute-start.28
  1632.4 10.6 collective-permute-start.29
  1633.7 9.3 collective-permute-start.30
  1635.1 8.0 collective-permute-start.31
  (22 other events, 782.5 us)
Sparse Core Ops, SparseCore 0:
  88.7 46.0 all-gather.1
  226.3 74.0 reduce-scatter.3
  642.1 36.3 reduce-scatter.7
  681.6 946.5 all-reduce.6
  1630.7 12.3 reduce-scatter.5
where the time goes:
time: 1670 us; the launch traced here: 1650 us
  waiting for transfers between devices  1010 us (60%)
  blocking collectives  310 us (19%)
  local copies, waits for them, and re-layouts  125 us (7%)
  starting transfers between devices  68.3 us (4%)
  other arithmetic  62.8 us (4%)
  matrix products  54.6 us (3%)
  between operations  23.9 us (1%)
    psum x1, waiting for transfers between devices, local(): summed = lax.psum((proj_acc, pair_acc, head_acc), 'genome')  939 us
    psum x1, blocking collectives, local(): summed = lax.psum((proj_acc, pair_acc, head_acc), 'genome')  301 us
    gather x4, local copies, waits for them, and re-layouts, pair_inputs(): partners = extended[offsets]  69.1 us
    gather x1, local copies, waits for them, and re-layouts, local(): mask_ext[local_index].astype(jnp.float32)  51.2 us
    scatter-add x2, other arithmetic, backward_block(): grad_ext.at[offsets].add(slope * own_rows.astype(jnp.float32)[:, None, :])  50.8 us
    ppermute x24, starting transfers between devices, passed_along(): return lax.ppermute(value, axis, pairs)  41.7 us
  transfers between devices with their start and end apart: 37, of which 13 were waited for; matrix products, arithmetic and copies ran while one was open for 4% of the time, Pallas kernels for 0%

commit v1 on v0

v1 whole, which is shorter than its diff:
```python
import functools

import jax
import jax.numpy as jnp
from jax import lax
from jax.experimental import pallas as pl
from jax.experimental.pallas import tpu as pltpu
from jax.sharding import Mesh, PartitionSpec as P

F32 = jnp.float32
BF16 = jnp.bfloat16
EMB = 512
CH = 64
BAND = 256
BINS = 4096
OWN = 16
HALO = 16
ROWS = OWN + 2 * HALO
WIDE = 384
GENOME = ("yl", "x", "z", "core")
CHIPS = ("yl", "x", "z")
NT = (((1,), (1,)), ((), ()))
TN = (((0,), (0,)), ((), ()))


def dot(a, b, dims=(((1,), (0,)), ((), ()))):
    return lax.dot_general(a, b, dims, preferred_element_type=F32)


def sigmoid(v):
    return 0.5 * jnp.tanh(0.5 * v) + 0.5


def kernel(
    scalars, win, wt, bias, kf, kb, hk, hkt, tgt,
    g_out, w_out,
    et, ef, mrow, cmask, pre, hz, d0, h1, d1, s1, s1b, sz, aown, q, rgb, tgw, pacc, g1, pg, hg,
):
    r0 = scalars[0]
    r1 = scalars[1]
    w0 = scalars[2]
    col = lax.broadcasted_iota(jnp.int32, (1, WIDE), 1)

    def band(r):
        high = jnp.where(w0 + r >= 0, jnp.minimum(r + BAND, BINS - w0), 0)
        return jnp.where((col >= r) & (col < high), 1.0, 0.0).astype(F32)

    def back_roll(v, by):
        return pltpu.roll(v, WIDE - by, 1)

    wide = win[:, :EMB].astype(F32)
    et[...] = wide.T.astype(BF16)
    ef[...] = wide[:ROWS]
    marks = win[:, EMB:].astype(F32)
    mrow[...] = marks[:ROWS]
    cmask[...] = marks.T[:8]
    padded = jnp.concatenate([tgt[...], jnp.zeros((32, WIDE - BAND), F32)], 1)
    tgw[...] = pltpu.roll(padded, 8, 1, stride=1, stride_axis=0)

    def forward(b, _):
        e8 = ef[pl.ds(pl.multiple_of(b * 8, 8), 8), :]
        w = wt[...].astype(F32)
        a = jnp.concatenate([(w * e8[k : k + 1]).astype(BF16) for k in range(8)], 0)

        @pl.when((b >= 2) & (b < 4))
        def _():
            aown[pl.ds(pl.multiple_of((b - 2) * 512, 512), 512), :] = a

        pre[...] = dot(a, et[...])

        def row(k, _):
            r = b * 8 + k
            v = pre[pl.ds(pl.multiple_of(k * CH, CH), CH), :] + pltpu.roll(bias[...], r, 1)
            s = sigmoid(v)
            m = band(r)
            hz[r] = (v * s * m).astype(BF16)

            @pl.when((r >= HALO) & (r < HALO + OWN))
            def _():
                d0[r - HALO] = s * (1.0 + v * (1.0 - s)) * m

            return 0

        lax.fori_loop(0, 8, row, 0)
        return 0

    lax.fori_loop(0, ROWS // 8, forward, 0)

    def second(n, _):
        for k in range(4):
            r = 4 + n * 4 + k
            near = jnp.concatenate([hz[r - r0], hz[r], hz[r + r0]], 0)
            p = dot(kf[...], near)
            v = pltpu.roll(p[:CH], r0, 1) + p[CH : 2 * CH] + back_roll(p[2 * CH :], r0)
            s = sigmoid(v)
            m = band(r)
            one = (v * s * m).astype(BF16)
            h1[r] = one
            d1[r] = s * (1.0 + v * (1.0 - s)) * m
            p9 = dot(hk[...], one)
            q[r] = pltpu.roll(p9[:8], r1, 1) + p9[8:16] + back_roll(p9[16:24], r1)
        return 0

    lax.fori_loop(0, 10, second, 0)

    which = lax.broadcasted_iota(jnp.int32, (8, WIDE), 0)

    def residual(n, _):
        for k in range(4):
            r = 8 + n * 4 + k
            pred = q[r - r1][0:1] + q[r][1:2] + q[r + r1][2:3]
            mark = mrow[pl.ds(r, 1), :]
            lm = jnp.concatenate([mark] * (WIDE // 128), 1) * cmask[0:1] * band(r)
            rg = lm * (pred - tgw[pl.ds(r - 8, 1), :]) * (1.0 / BAND)
            rg = jnp.broadcast_to(rg, (8, WIDE))
            taps = jnp.where(
                which == 0,
                back_roll(rg, r1),
                jnp.where(which == 1, rg, jnp.where(which == 2, pltpu.roll(rg, r1, 1), 0.0)),
            )
            high = taps.astype(BF16).astype(F32)
            rgb[r] = jnp.concatenate([high, taps - high], 0).astype(BF16)
        return 0

    lax.fori_loop(0, 8, residual, 0)

    def slope(n, _):
        for k in range(4):
            r = 12 + n * 4 + k
            near = jnp.concatenate([rgb[r + r1], rgb[r], rgb[r - r1]], 0)
            s = (dot(hkt[...], near) * d1[r]).astype(BF16)
            s1[r] = s

            @pl.when((r >= HALO) & (r < HALO + OWN))
            def _():
                sf = s.astype(F32)
                s1b[r - HALO] = jnp.concatenate(
                    [back_roll(sf, r0).astype(BF16), s, pltpu.roll(sf, r0, 1).astype(BF16)], 0
                )

        return 0

    lax.fori_loop(0, 6, slope, 0)

    pg[...] = jnp.zeros_like(pg)
    hg[...] = jnp.zeros_like(hg)

    def grads(n, _):
        psum, hsum = 0.0, 0.0
        for k in range(4):
            i = n * 4 + k
            r = HALO + i
            near = jnp.concatenate([hz[r - r0], hz[r], hz[r + r0]], 0)
            psum = psum + dot(s1b[i], near, NT)
            near = jnp.concatenate([h1[r - r1], h1[r], h1[r + r1]], 0)
            hsum = hsum + dot(rgb[r], near, NT)
            near = jnp.concatenate([s1[r + r0], s1[r], s1[r - r0]], 0)
            p = dot(kb[...], near)
            zg = back_roll(p[:CH], r0) + p[CH : 2 * CH] + pltpu.roll(p[2 * CH :], r0, 1)
            sz[pl.ds(pl.multiple_of(i * CH, CH), CH), :] = (zg * d0[i]).astype(BF16)
        pg[...] += psum
        hg[...] += hsum
        return 0

    lax.fori_loop(0, 4, grads, 0)

    pacc[...] = jnp.zeros_like(pacc)

    def back(n, _):
        t = dot(sz[pl.ds(pl.multiple_of(n * 256, 256), 256), :], win[:, :EMB])
        w = wt[...].astype(F32)
        acc = pacc[...]
        for k in range(4):
            tr = t[k * CH : (k + 1) * CH]
            g1[pl.ds(n * 4 + k, 1), :] = jnp.sum(w * tr, axis=0, keepdims=True)
            acc = acc + tr * ef[pl.ds(HALO + n * 4 + k, 1), :]
        pacc[...] = acc
        return 0

    lax.fori_loop(0, 4, back, 0)
    g = dot(sz[...], aown[...], TN)
    g_out[...] = g.astype(BF16)
    g_out[HALO : HALO + OWN, :] = (g[HALO : HALO + OWN] + g1[...]).astype(BF16)

    w_out[...] = jnp.zeros_like(w_out)
    heads = hg[0:8] + hg[8:16]
    for half in range(2):
        t = 0
        for a in range(4):
            for b in range(4):
                w_out[half, t] = pacc[half * 32 + a * 8 : half * 32 + a * 8 + 8, b * 128 : b * 128 + 128]
                t += 1
        for b in range(3):
            for a in range(4):
                rows = pg[b * CH + half * 32 + a * 8 : b * CH + half * 32 + a * 8 + 8, :]
                w_out[half, t] = rows[:, :128]
                w_out[half, t + 1, :, : 3 * CH - 128] = rows[:, 128:]
                t += 2
        w_out[half, t] = heads[:, :128]
        w_out[half, t + 1, :, : 3 * CH - 128] = heads[:, 128:]


def run_kernel(scalars, win, wt, bias, kf, kb, hk, hkt, tgt):
    vmem = pl.BlockSpec(memory_space=pltpu.VMEM)
    return pl.pallas_call(
        kernel,
        out_shape=(
            jax.ShapeDtypeStruct((WIDE, EMB), BF16),
            jax.ShapeDtypeStruct((2, 64, 8, 128), F32),
        ),
        in_specs=[pl.BlockSpec(memory_space=pltpu.SMEM)] + [vmem] * 8,
        out_specs=(vmem, vmem),
        scratch_shapes=[
            pltpu.VMEM((EMB, WIDE), BF16),
            pltpu.VMEM((ROWS, EMB), F32),
            pltpu.VMEM((ROWS, 128), F32),
            pltpu.VMEM((8, WIDE), F32),
            pltpu.VMEM((8 * CH, WIDE), F32),
            pltpu.VMEM((ROWS, CH, WIDE), BF16),
            pltpu.VMEM((OWN, CH, WIDE), F32),
            pltpu.VMEM((ROWS, CH, WIDE), BF16),
            pltpu.VMEM((ROWS, CH, WIDE), F32),
            pltpu.VMEM((ROWS, CH, WIDE), BF16),
            pltpu.VMEM((OWN, 3 * CH, WIDE), BF16),
            pltpu.VMEM((OWN * CH, WIDE), BF16),
            pltpu.VMEM((OWN * CH, EMB), BF16),
            pltpu.VMEM((ROWS, 8, WIDE), F32),
            pltpu.VMEM((ROWS, 16, WIDE), BF16),
            pltpu.VMEM((32, WIDE), F32),
            pltpu.VMEM((CH, EMB), F32),
            pltpu.VMEM((OWN, EMB), F32),
            pltpu.VMEM((3 * CH, 3 * CH), F32),
            pltpu.VMEM((16, 3 * CH), F32),
        ],
        compiler_params=pltpu.CompilerParams(vmem_limit_bytes=48 * 1024 * 1024),
    )(scalars, win, wt, bias, kf, kb, hk, hkt, tgt)


def both(value, chan):
    other = lax.ppermute(value, "chan", [(0, 1), (1, 0)])
    return jnp.where(chan == 0, jnp.stack([value, other]), jnp.stack([other, value]))


def swap(value, axis):
    return lax.ppermute(value, axis, [(0, 1), (1, 0)])


def local(sizes, embeddings, bin_mask, target, proj_weight, dist_bias, pair_kernel, head_kernel, dilations):
    chips = sizes["yl"] * sizes["x"] * sizes["z"]
    chan = lax.axis_index("chan")
    core = lax.axis_index("core")
    first = (lax.axis_index(GENOME) * 2 + chan) * OWN

    packed = jnp.concatenate(
        [
            proj_weight.T.reshape(-1, 128),
            dist_bias.reshape(-1, 128),
            pair_kernel.transpose(1, 0, 2).reshape(-1, 128),
            jnp.pad(head_kernel.T.reshape(-1), (0, 96)).reshape(-1, 128),
        ],
        0,
    )
    pair = both(packed, chan)
    at = 0

    def take(rows, shape):
        nonlocal at
        piece = pair[:, at : at + rows]
        at += rows
        return piece.reshape((2,) + shape)

    wt = take(128, (32, EMB)).reshape(CH, EMB)
    bias = take(64, (32, BAND)).reshape(CH, BAND)
    kernels = take(144, (32, 3, 3, CH)).reshape(CH, 3, 3, CH)
    heads = pair[:, at : at + 3].reshape(2, 384)[:, :288].reshape(CH, 3, 3)
    bias = jnp.pad(bias.astype(F32), ((0, 0), (0, WIDE - BAND)))
    kf = kernels.transpose(2, 0, 1, 3).reshape(3 * CH, 3 * CH)
    kb = kernels.transpose(2, 3, 1, 0).reshape(3 * CH, 3 * CH)
    hk = jnp.pad(heads.transpose(2, 1, 0), ((0, 0), (0, 5), (0, 0))).reshape(24, CH)
    hkt = jnp.pad(heads, ((0, 0), (0, 0), (0, 5)))
    hkt = jnp.concatenate([hkt, hkt], 2).reshape(CH, 48)

    marked = jnp.concatenate(
        [embeddings, jnp.broadcast_to(bin_mask.astype(BF16)[:, None], (2 * OWN, 128))], 1
    )

    def ahead(value, by):
        return lax.ppermute(value, CHIPS, [(i, i - by) for i in range(by, chips)])

    same = [marked] + [ahead(marked, n) for n in range(1, 5)]
    flat = lambda chip, c, h: (chip * 2 + c) * 2 + h
    rim_pairs = [(flat(i, 1, 0), flat(i + 1, 0, 0)) for i in range(chips - 1)]
    rim_pairs += [(flat(i, 0, 1), flat(i - 5, 1, 1)) for i in range(5, chips)]
    rim = lax.ppermute(
        jnp.where(core == 0, marked[:OWN], marked[OWN:]), GENOME + ("chan",), rim_pairs
    )
    sibling = [swap(value, "core") for value in same]
    zero_half = jnp.zeros((OWN, marked.shape[1]), BF16)
    window_even = []
    for a, b in zip(same, sibling):
        window_even += [a, b]
    window_odd = [same[0]]
    for n in range(1, 5):
        window_odd += [sibling[n], same[n]]
    even = jnp.concatenate(window_even[:9], 0)
    odd = jnp.concatenate(window_odd, 0)
    main = jnp.where(core == 0, even, odd)
    before = jnp.where(core == 0, rim, sibling[0][OWN:])
    after = jnp.where(core == 0, sibling[4][:OWN], rim)
    fill = jnp.zeros((WIDE - 304, marked.shape[1]), BF16)
    win = jnp.where(
        chan == 0,
        jnp.concatenate([before, main, fill], 0),
        jnp.concatenate([main, after, fill], 0),
    )

    genome = chips * 2
    target_pairs = [(2 * i, 2 * i + 2) for i in range(genome - 1)]
    target_pairs += [(2 * i + 1, 2 * i - 1) for i in range(1, genome)]
    rim_target = lax.ppermute(
        jnp.where(chan == 0, target[24:], target[:8]), GENOME + ("chan",), target_pairs
    )
    tgt = jnp.where(
        chan == 0,
        jnp.concatenate([rim_target, target[:24]], 0),
        jnp.concatenate([target[8:], rim_target], 0),
    )

    scalars = jnp.stack([dilations[0], dilations[1], first - HALO]).astype(jnp.int32)
    g, w = run_kernel(scalars, win, wt, bias, kf, kb, hk, hkt, tgt)

    lead = jnp.zeros((OWN, EMB), BF16)
    blocks = jnp.where(
        chan == 0, g[HALO : HALO + 288], jnp.concatenate([lead, g[HALO : HALO + 272]], 0)
    ).reshape(9, 2 * OWN, EMB)
    kept = blocks[0::2].astype(F32)
    given = swap(blocks[1::2], "core").astype(F32)
    none = jnp.zeros((1, 2 * OWN, EMB), F32)
    kept = kept + jnp.where(
        core == 0, jnp.concatenate([none, given], 0), jnp.concatenate([given, none], 0)
    )
    mine = jnp.where(chan == 0, kept[..., :256], kept[..., 256:])
    others = jnp.where(chan == 0, kept[..., 256:], kept[..., :256]).astype(BF16)
    mine = mine + swap(others, "chan").astype(F32)
    total = mine[0]
    for n in range(1, 5):
        moved = lax.ppermute(
            mine[n].astype(BF16), CHIPS, [(i, i + n) for i in range(chips - n)]
        )
        total = total + moved.astype(F32)

    mine_w = jnp.where(chan == 0, w[0], w[1])
    other_w = jnp.where(chan == 0, w[1], w[0])
    mine_w = mine_w + swap(other_w, "chan")
    tiles = 64
    mine_w = mine_w + swap(mine_w, "core")
    pieces = lax.all_to_all(mine_w.reshape(chips, tiles // chips * 8, 128), CHIPS, 0, 0, tiled=True)
    piece = jnp.sum(pieces, axis=0, keepdims=True)
    whole = lax.all_to_all(
        jnp.broadcast_to(piece, (chips,) + piece.shape[1:]), CHIPS, 0, 0, tiled=True
    ).reshape(tiles, 8, 128)
    whole = whole * (1.0 / BINS)
    proj = whole[:16].reshape(4, 4, 8, 128).transpose(1, 3, 0, 2).reshape(EMB, 32)
    conv = whole[16:40].reshape(3, 4, 2, 8, 128).transpose(0, 1, 3, 2, 4).reshape(3, 32, 256)
    conv = conv[:, :, : 3 * CH].reshape(3, 32, 3, CH)
    conv = conv.transpose(2, 0, 1, 3).reshape(9, 32, CH)
    head = whole[40:42].transpose(1, 0, 2).reshape(8, 256)[:3, : 3 * CH].reshape(3, 3, CH)
    head = head.transpose(1, 0, 2).reshape(9, CH)
    head = jnp.where(chan == 0, head[:, :32], head[:, 32:])
    return total, proj, conv, head


def solution(mesh):
    split = mesh.devices.reshape(2, 4, 8, 2, 2)
    sizes = dict(yl=2, x=4, z=8, core=2, chan=2)
    fine = Mesh(split, ("yl", "x", "z", "core", "chan"))
    return jax.shard_map(
        functools.partial(local, sizes),
        mesh=fine,
        in_specs=(
            P(GENOME, None),
            P(GENOME),
            P(GENOME, None),
            P(None, "chan"),
            P("chan", None),
            P(None, "chan", None),
            P(None, "chan"),
            P(),
        ),
        out_specs=(P(GENOME, "chan"), P(None, "chan"), P(None, "chan", None), P(None, "chan")),
        check_vma=False,
    )
```

time: 1670 us -> 149 us (0.09)
  the two profiles are of different devices: /device:TPU:1 before, /device:TPU:24 now
where the time goes in v1:
time: 149 us; the launch traced here: 148 us
  starting transfers between devices  64.2 us (43%)
  Pallas kernels  36.3 us (24%)
  waiting for transfers between devices  32.5 us (22%)
  local copies, waits for them, and re-layouts  10 us (7%)
  other arithmetic  4.27 us (3%)
    pallas_call x1, Pallas kernels, run_kernel(): pl.pallas_call(kernel, out_shape=(jax.ShapeDtypeStruct((WIDE, EMB), BF16)...  36.3 us
    ppermute x4, starting transfers between devices, ahead(): return lax.ppermute(value, CHIPS, [(i, i - by) for i in range(by, chips)])  23.2 us
    ppermute x4, starting transfers between devices, local(): lax.ppermute(mine[n].astype(BF16), CHIPS, [(i, i + n) for i in range(chip...  17.5 us
    all_to_all x1, waiting for transfers between devices, local(): lax.all_to_all(mine_w.reshape(chips, tiles // chips * 8, 128), CHIPS, 0,...  13 us
    ppermute x9, waiting for transfers between devices, swap(): return lax.ppermute(value, axis, [(0, 1), (1, 0)])  9.79 us
    all_to_all x1, starting transfers between devices, local(): lax.all_to_all(mine_w.reshape(chips, tiles // chips * 8, 128), CHIPS, 0,...  8.61 us
    ppermute x4, waiting for transfers between devices, local(): lax.ppermute(mine[n].astype(BF16), CHIPS, [(i, i + n) for i in range(chip...  7.41 us
    all_to_all x1, starting transfers between devices, local(): lax.all_to_all(jnp.broadcast_to(piece, (chips,) + piece.shape[1:]), CHIPS...  4.87 us
  transfers between devices with their start and end apart: 22, of which 9 were waited for; matrix products, arithmetic and copies ran while one was open for 2% of the time, Pallas kernels for 0%

profile of v1, /device:TPU:24, one launch (start us, length us, event | category | flops | bytes accessed | tf_op | source)
XLA Modules:
  0.0 148.5 jit_solution(3528604745549884480)
XLA Ops:
  0.6 0.7 convert_element_type.55
  1.4 0.8 pad_maximum_fusion.1
  2.1 10.1 %collective-permute-start.2 = (bf16[32,640]{1,0:T(8,128)(2,1)S(1)}, bf16[32,640]{1,0:T(8,128)(2,1)S(1)}, u32[]{:S(2)}, u32[]{:S(2)}) collective-permute-start(bf16[32,640]{1,0:T(8,128)(2,1)S(1)} %get-tuple-element.24), channel_id=1, source_target_pairs={{4,0},{8,4},{12,8},{16,12},{20,16},{24,20},{28,24},{32,28},{36,32}... | collective-permute-start | bytes 122888 | tf_op jit(solution)/shard_map/ppermute | solution.py:288
  12.4 3.4 %collective-permute-start.4 = (bf16[32,640]{1,0:T(8,128)(2,1)S(1)}, bf16[32,640]{1,0:T(8,128)(2,1)S(1)}, u32[]{:S(2)}, u32[]{:S(2)}) collective-permute-start(bf16[32,640]{1,0:T(8,128)(2,1)S(1)} %get-tuple-element.24), channel_id=1, source_target_pairs={{8,0},{12,4},{16,8},{20,12},{24,16},{28,20},{32,24},{36,28},{40,32... | collective-permute-start | bytes 122888 | tf_op jit(solution)/shard_map/ppermute | solution.py:288
  15.7 2.4 %collective-permute-start.6 = (bf16[32,640]{1,0:T(8,128)(2,1)S(1)}, bf16[32,640]{1,0:T(8,128)(2,1)S(1)}, u32[]{:S(2)}, u32[]{:S(2)}) collective-permute-start(bf16[32,640]{1,0:T(8,128)(2,1)S(1)} %get-tuple-element.24), channel_id=1, source_target_pairs={{12,0},{16,4},{20,8},{24,12},{28,16},{32,20},{36,24},{40,28},{44,3... | collective-permute-start | bytes 122888 | tf_op jit(solution)/shard_map/ppermute | solution.py:288
  18.1 2.3 %collective-permute-start.11 = (f32[8,256]{1,0:T(8,128)S(1)}, f32[8,256]{1,0:T(8,128)S(1)}, u32[]{:S(2)}, u32[]{:S(2)}) collective-permute-start(f32[8,256]{1,0:T(8,128)S(1)} %slice_select_fusion.3), channel_id=1, source_target_pairs={{0,2},{2,4},{4,6},{6,8},{8,10},{10,12},{12,14},{14,16},{16,18},{18... | collective-permute-start | bytes 24584 | tf_op jit(solution)/shard_map/ppermute | solution.py:320
  20.5 0.7 copy-done.2
  22.2 0.7 copy-done.5
  22.9 0.7 copy-done.6
  24.7 7.4 %collective-permute-start.8 = (bf16[32,640]{1,0:T(8,128)(2,1)S(1)}, bf16[32,640]{1,0:T(8,128)(2,1)S(1)}, u32[]{:S(2)}, u32[]{:S(2)}) collective-permute-start(bf16[32,640]{1,0:T(8,128)(2,1)S(1)} %get-tuple-element.24), channel_id=1, source_target_pairs={{16,0},{20,4},{24,8},{28,12},{32,16},{36,20},{40,24},{44,28},{48,3... | collective-permute-start | bytes 122888 | tf_op jit(solution)/shard_map/ppermute | solution.py:288
  32.1 1.3 collective-permute-start
  33.5 2.2 %collective-permute-start.10 = (bf16[339,128]{1,0:T(8,128)(2,1)S(1)}, bf16[339,128]{1,0:T(8,128)(2,1)S(1)}, u32[]{:S(2)}, u32[]{:S(2)}) collective-permute-start(bf16[339,128]{1,0:T(8,128)(2,1)S(1)} %get-tuple-element.11), channel_id=1, source_target_pairs={{0,1},{1,0},{2,3},{3,2},{4,5},{5,4},{6,7},{7,6},{8,9},{9,8},{10,11... | collective-permute-start | bytes 260360 | tf_op jit(solution)/shard_map/ppermute | solution.py:240
  37.8 2.3 %collective-permute-done.10 = bf16[339,128]{1,0:T(8,128)(2,1)S(1)} collective-permute-done((bf16[339,128]{1,0:T(8,128)(2,1)S(1)}, bf16[339,128]{1,0:T(8,128)(2,1)S(1)}, u32[]{:S(2)}, u32[]{:S(2)}) %collective-permute-start.10) | collective-permute-done | bytes 86816 | tf_op jit(solution)/shard_map/ppermute | solution.py:240
  42.8 0.8 slice-done.1
  43.7 36.3 %shard_map.111 = (bf16[384,512]{1,0:T(8,128)(2,1)S(1)}, f32[2,64,8,128]{3,2,1,0:T(8,128)S(1)}) custom-call(s32[3]{0:T(128)S(1)} %pad_add_fusion.scalars, bf16[384,640]{1,0:T(8,128)(2,1)S(1)} %maximum_select_fusion.win, bf16[64,512]{1,0:T(8,128)(2,1)S(1)} %reshape_reshape.7.wt, f32[64,384]{1,0:T(8,128)S(1)} %pad_convert_fusion.bias, ...), custom_call_target="tpu_custom_call" | custom-call | tf_op jit(solution)/shard_map/pallas_call | solution.py:205
  80.0 2.1 %collective-permute-start.18 = (f32[64,8,128]{2,1,0:T(8,128)S(1)}, f32[64,8,128]{2,1,0:T(8,128)S(1)}, u32[]{:S(2)}, u32[]{:S(2)}) collective-permute-start(f32[64,8,128]{2,1,0:T(8,128)S(1)} %select_bitcast_fusion), channel_id=1, source_target_pairs={{0,1},{1,0},{2,3},{3,2},{4,5},{5,4},{6,7},{7,6},{8,9},{9,8},{10,11... | collective-permute-start | bytes 786440 | tf_op jit(solution)/shard_map/ppermute | solution.py:245
  82.2 7.7 %collective-permute-done.18 = f32[64,8,128]{2,1,0:T(8,128)S(1)} collective-permute-done((f32[64,8,128]{2,1,0:T(8,128)S(1)}, f32[64,8,128]{2,1,0:T(8,128)S(1)}, u32[]{:S(2)}, u32[]{:S(2)}) %collective-permute-start.18) | collective-permute-done | bytes 262176 | tf_op jit(solution)/shard_map/ppermute | solution.py:245
  90.7 1.0 collective-permute-done.12
  91.8 0.7 add.62
  92.5 8.6 %all-to-all-start = ((f32[64,8,128]{2,1,0:T(8,128)}), f32[64,8,128]{2,1,0:T(8,128)S(1)}, u32[]{:S(2)}, u32[]{:S(2)}) async-start(f32[64,8,128]{2,1,0:T(8,128)} %add.62), calls=%async_computation | async-start | bytes 524288 | tf_op jit(solution)/shard_map/all_to_all | solution.py:357
  101.2 0.7 collective-permute-start.13
  102.0 13.0 %all-to-all-done = f32[64,8,128]{2,1,0:T(8,128)S(1)} async-done(((f32[64,8,128]{2,1,0:T(8,128)}), f32[64,8,128]{2,1,0:T(8,128)S(1)}, u32[]{:S(2)}, u32[]{:S(2)}) %all-to-all-start) | async-done | bytes 262176 | tf_op jit(solution)/shard_map/all_to_all | solution.py:357
  115.0 0.7 broadcast_in_dim.8
  115.7 4.9 %all-to-all-start.1 = ((f32[64,8,128]{2,1,0:T(8,128)}), f32[64,8,128]{2,1,0:T(8,128)S(1)}, u32[]{:S(2)}, u32[]{:S(2)}) async-start(f32[64,8,128]{2,1,0:T(8,128)} %broadcast_in_dim.8), calls=%async_computation.1 | async-start | bytes 524288 | tf_op jit(solution)/shard_map/all_to_all | solution.py:359
  120.7 3.4 %collective-permute-start.14 = (bf16[32,256]{1,0:T(8,128)(2,1)S(1)}, bf16[32,256]{1,0:T(8,128)(2,1)S(1)}, u32[]{:S(2)}, u32[]{:S(2)}) collective-permute-start(bf16[32,256]{1,0:T(8,128)(2,1)S(1)} %get-tuple-element.12), channel_id=1, source_target_pairs={{0,4},{4,8},{8,12},{12,16},{16,20},{20,24},{24,28},{28,32},{32,36}... | collective-permute-start | bytes 49160 | tf_op jit(solution)/shard_map/ppermute | solution.py:347
  124.1 4.3 %collective-permute-start.15 = (bf16[32,256]{1,0:T(8,128)(2,1)S(1)}, bf16[32,256]{1,0:T(8,128)(2,1)S(1)}, u32[]{:S(2)}, u32[]{:S(2)}) collective-permute-start(bf16[32,256]{1,0:T(8,128)(2,1)S(1)} %get-tuple-element.15), channel_id=1, source_target_pairs={{0,8},{4,12},{8,16},{12,20},{16,24},{20,28},{24,32},{28,36},{32,40... | collective-permute-start | bytes 49160 | tf_op jit(solution)/shard_map/ppermute | solution.py:347
  128.4 4.6 %collective-permute-start.16 = (bf16[32,256]{1,0:T(8,128)(2,1)S(1)}, bf16[32,256]{1,0:T(8,128)(2,1)S(1)}, u32[]{:S(2)}, u32[]{:S(2)}) collective-permute-start(bf16[32,256]{1,0:T(8,128)(2,1)S(1)} %get-tuple-element.14), channel_id=1, source_target_pairs={{0,12},{4,16},{8,20},{12,24},{16,28},{20,32},{24,36},{28,40},{32,4... | collective-permute-start | bytes 49160 | tf_op jit(solution)/shard_map/ppermute | solution.py:347
  133.0 5.2 %collective-permute-start.17 = (bf16[32,256]{1,0:T(8,128)(2,1)S(1)}, bf16[32,256]{1,0:T(8,128)(2,1)S(1)}, u32[]{:S(2)}, u32[]{:S(2)}) collective-permute-start(bf16[32,256]{1,0:T(8,128)(2,1)S(1)} %get-tuple-element.13), channel_id=1, source_target_pairs={{0,16},{4,20},{8,24},{12,28},{16,32},{20,36},{24,40},{28,44},{32,4... | collective-permute-start | bytes 49160 | tf_op jit(solution)/shard_map/ppermute | solution.py:347
  138.2 2.0 %collective-permute-done.16 = bf16[32,256]{1,0:T(8,128)(2,1)S(1)} collective-permute-done((bf16[32,256]{1,0:T(8,128)(2,1)S(1)}, bf16[32,256]{1,0:T(8,128)(2,1)S(1)}, u32[]{:S(2)}, u32[]{:S(2)}) %collective-permute-start.16) | collective-permute-done | bytes 16416 | tf_op jit(solution)/shard_map/ppermute | solution.py:347
  140.2 5.4 %collective-permute-done.17 = bf16[32,256]{1,0:T(8,128)(2,1)S(1)} collective-permute-done((bf16[32,256]{1,0:T(8,128)(2,1)S(1)}, bf16[32,256]{1,0:T(8,128)(2,1)S(1)}, u32[]{:S(2)}, u32[]{:S(2)}) %collective-permute-start.17) | collective-permute-done | bytes 16416 | tf_op jit(solution)/shard_map/ppermute | solution.py:347
  147.0 0.7 copy.38
  147.8 0.7 slice_select_fusion.2
  (111 shorter events, 9.7 us)
Async XLA Ops:
  1.4 16.8 %copy-start.1 = (f32[32,256]{1,0:T(8,128)S(1)}, f32[32,256]{1,0:T(8,128)}, u32[]{:S(2)}) copy-start(f32[32,256]{1,0:T(8,128)} %param.10) | copy-start | bytes 98308
  2.1 29.9 %collective-permute-start.2 = (bf16[32,640]{1,0:T(8,128)(2,1)S(1)}, bf16[32,640]{1,0:T(8,128)(2,1)S(1)}, u32[]{:S(2)}, u32[]{:S(2)}) collective-permute-start(bf16[32,640]{1,0:T(8,128)(2,1)S(1)} %get-tuple-element.24), channel_id=1, source_target_pairs={{4,0},{8,4},{12,8},{16,12},{20,16},{24,20},{28,24},{32,28},{36,32}... | collective-permute-start | bytes 122888 | tf_op jit(solution)/shard_map/ppermute | solution.py:288
  12.3 21.1 %collective-permute-start.1 = (bf16[32,640]{1,0:T(8,128)(2,1)S(1)}, bf16[32,640]{1,0:T(8,128)(2,1)S(1)}, u32[]{:S(2)}, u32[]{:S(2)}) collective-permute-start(bf16[32,640]{1,0:T(8,128)(2,1)S(1)} %get-tuple-element.24), channel_id=1, source_target_pairs={{0,2},{2,0},{1,3},{3,1},{4,6},{6,4},{5,7},{7,5},{8,10},{10,8},{9,1... | collective-permute-start | bytes 122888 | tf_op jit(solution)/shard_map/ppermute | solution.py:245
  12.4 21.1 %collective-permute-start.4 = (bf16[32,640]{1,0:T(8,128)(2,1)S(1)}, bf16[32,640]{1,0:T(8,128)(2,1)S(1)}, u32[]{:S(2)}, u32[]{:S(2)}) collective-permute-start(bf16[32,640]{1,0:T(8,128)(2,1)S(1)} %get-tuple-element.24), channel_id=1, source_target_pairs={{8,0},{12,4},{16,8},{20,12},{24,16},{28,20},{32,24},{36,28},{40,32... | collective-permute-start | bytes 122888 | tf_op jit(solution)/shard_map/ppermute | solution.py:288
  15.7 20.0 %collective-permute-start.6 = (bf16[32,640]{1,0:T(8,128)(2,1)S(1)}, bf16[32,640]{1,0:T(8,128)(2,1)S(1)}, u32[]{:S(2)}, u32[]{:S(2)}) collective-permute-start(bf16[32,640]{1,0:T(8,128)(2,1)S(1)} %get-tuple-element.24), channel_id=1, source_target_pairs={{12,0},{16,4},{20,8},{24,12},{28,16},{32,20},{36,24},{40,28},{44,3... | collective-permute-start | bytes 122888 | tf_op jit(solution)/shard_map/ppermute | solution.py:288
  18.1 6.5 %collective-permute-start.11 = (f32[8,256]{1,0:T(8,128)S(1)}, f32[8,256]{1,0:T(8,128)S(1)}, u32[]{:S(2)}, u32[]{:S(2)}) collective-permute-start(f32[8,256]{1,0:T(8,128)S(1)} %slice_select_fusion.3), channel_id=1, source_target_pairs={{0,2},{2,4},{4,6},{6,8},{8,10},{10,12},{12,14},{14,16},{16,18},{18... | collective-permute-start | bytes 24584 | tf_op jit(solution)/shard_map/ppermute | solution.py:320
  20.4 0.8 copy-start.2
  20.5 0.9 copy-start.3
  21.4 0.8 copy-start.4
  22.2 0.7 copy-start.5
  22.9 0.7 copy-start.6
  23.8 0.7 copy-start.7
  24.7 11.1 %collective-permute-start.8 = (bf16[32,640]{1,0:T(8,128)(2,1)S(1)}, bf16[32,640]{1,0:T(8,128)(2,1)S(1)}, u32[]{:S(2)}, u32[]{:S(2)}) collective-permute-start(bf16[32,640]{1,0:T(8,128)(2,1)S(1)} %get-tuple-element.24), channel_id=1, source_target_pairs={{16,0},{20,4},{24,8},{28,12},{32,16},{36,20},{40,24},{44,28},{48,3... | collective-permute-start | bytes 122888 | tf_op jit(solution)/shard_map/ppermute | solution.py:288
  32.1 5.5 %collective-permute-start = (bf16[16,640]{1,0:T(8,128)(2,1)S(1)}, bf16[16,640]{1,0:T(8,128)(2,1)S(1)}, u32[]{:S(2)}, u32[]{:S(2)}) collective-permute-start(bf16[16,640]{1,0:T(8,128)(2,1)S(1)} %fusion.5), channel_id=1, source_target_pairs={{2,4},{6,8},{10,12},{14,16},{18,20},{22,24},{26,28},{30,32},{34,36... | collective-permute-start | bytes 61448 | tf_op jit(solution)/shard_map/ppermute | solution.py:294
  33.4 2.9 %collective-permute-start.3 = (bf16[32,640]{1,0:T(8,128)(2,1)S(1)}, bf16[32,640]{1,0:T(8,128)(2,1)S(1)}, u32[]{:S(2)}, u32[]{:S(2)}) collective-permute-start(bf16[32,640]{1,0:T(8,128)(2,1)S(1)} %collective-permute-done.2), channel_id=1, source_target_pairs={{0,2},{2,0},{1,3},{3,1},{4,6},{6,4},{5,7},{7,5},{8,10},{10,8},{9,1... | collective-permute-start | bytes 122888 | tf_op jit(solution)/shard_map/ppermute | solution.py:245
  33.5 6.6 %collective-permute-start.10 = (bf16[339,128]{1,0:T(8,128)(2,1)S(1)}, bf16[339,128]{1,0:T(8,128)(2,1)S(1)}, u32[]{:S(2)}, u32[]{:S(2)}) collective-permute-start(bf16[339,128]{1,0:T(8,128)(2,1)S(1)} %get-tuple-element.11), channel_id=1, source_target_pairs={{0,1},{1,0},{2,3},{3,2},{4,5},{5,4},{6,7},{7,6},{8,9},{9,8},{10,11... | collective-permute-start | bytes 260360 | tf_op jit(solution)/shard_map/ppermute | solution.py:240
  35.7 1.2 collective-permute-start.5
  35.7 1.4 collective-permute-start.7
  36.3 1.2 collective-permute-start.9
  40.1 0.7 copy-start
  42.0 0.8 slice-start
  42.8 0.8 slice-start.1
  80.0 9.9 %collective-permute-start.18 = (f32[64,8,128]{2,1,0:T(8,128)S(1)}, f32[64,8,128]{2,1,0:T(8,128)S(1)}, u32[]{:S(2)}, u32[]{:S(2)}) collective-permute-start(f32[64,8,128]{2,1,0:T(8,128)S(1)} %select_bitcast_fusion), channel_id=1, source_target_pairs={{0,1},{1,0},{2,3},{3,2},{4,5},{5,4},{6,7},{7,6},{8,9},{9,8},{10,11... | collective-permute-start | bytes 786440 | tf_op jit(solution)/shard_map/ppermute | solution.py:245
  90.0 1.8 %collective-permute-start.19 = (f32[64,8,128]{2,1,0:T(8,128)S(1)}, f32[64,8,128]{2,1,0:T(8,128)S(1)}, u32[]{:S(2)}, u32[]{:S(2)}) collective-permute-start(f32[64,8,128]{2,1,0:T(8,128)S(1)} %bitcast_add_fusion), channel_id=1, source_target_pairs={{0,2},{2,0},{1,3},{3,1},{4,6},{6,4},{5,7},{7,5},{8,10},{10,8},{9,1... | collective-permute-start | bytes 786440 | tf_op jit(solution)/shard_map/ppermute | solution.py:245
  90.2 1.6 %collective-permute-start.12 = (bf16[4,32,512]{2,1,0:T(8,128)(2,1)S(1)}, bf16[4,32,512]{2,1,0:T(8,128)(2,1)S(1)}, u32[]{:S(2)}, u32[]{:S(2)}) collective-permute-start(bf16[4,32,512]{2,1,0:T(8,128)(2,1)S(1)} %slice.126), channel_id=1, source_target_pairs={{0,2},{2,0},{1,3},{3,1},{4,6},{6,4},{5,7},{7,5},{8,10},{10,8},{9,1... | collective-permute-start | bytes 393224 | tf_op jit(solution)/shard_map/ppermute | solution.py:245
  92.5 22.4 %all-to-all-start = ((f32[64,8,128]{2,1,0:T(8,128)}), f32[64,8,128]{2,1,0:T(8,128)S(1)}, u32[]{:S(2)}, u32[]{:S(2)}) async-start(f32[64,8,128]{2,1,0:T(8,128)} %add.62), calls=%async_computation | async-start | bytes 524288 | tf_op jit(solution)/shard_map/all_to_all | solution.py:357
  101.2 19.4 %collective-permute-start.13 = (bf16[5,32,256]{2,1,0:T(8,128)(2,1)S(1)}, bf16[5,32,256]{2,1,0:T(8,128)(2,1)S(1)}, u32[]{:S(2)}, u32[]{:S(2)}) collective-permute-start(bf16[5,32,256]{2,1,0:T(8,128)(2,1)S(1)} %select_convert_fusion), channel_id=1, source_target_pairs={{0,1},{1,0},{2,3},{3,2},{4,5},{5,4},{6,7},{7,6},{8,9},{9,8},{10,11... | collective-permute-start | bytes 245768 | tf_op jit(solution)/shard_map/ppermute | solution.py:245
  115.7 30.5 %all-to-all-start.1 = ((f32[64,8,128]{2,1,0:T(8,128)}), f32[64,8,128]{2,1,0:T(8,128)S(1)}, u32[]{:S(2)}, u32[]{:S(2)}) async-start(f32[64,8,128]{2,1,0:T(8,128)} %broadcast_in_dim.8), calls=%async_computation.1 | async-start | bytes 524288 | tf_op jit(solution)/shard_map/all_to_all | solution.py:359
  120.7 17.5 %collective-permute-start.14 = (bf16[32,256]{1,0:T(8,128)(2,1)S(1)}, bf16[32,256]{1,0:T(8,128)(2,1)S(1)}, u32[]{:S(2)}, u32[]{:S(2)}) collective-permute-start(bf16[32,256]{1,0:T(8,128)(2,1)S(1)} %get-tuple-element.12), channel_id=1, source_target_pairs={{0,4},{4,8},{8,12},{12,16},{16,20},{20,24},{24,28},{28,32},{32,36}... | collective-permute-start | bytes 49160 | tf_op jit(solution)/shard_map/ppermute | solution.py:347
  124.1 14.1 %collective-permute-start.15 = (bf16[32,256]{1,0:T(8,128)(2,1)S(1)}, bf16[32,256]{1,0:T(8,128)(2,1)S(1)}, u32[]{:S(2)}, u32[]{:S(2)}) collective-permute-start(bf16[32,256]{1,0:T(8,128)(2,1)S(1)} %get-tuple-element.15), channel_id=1, source_target_pairs={{0,8},{4,12},{8,16},{12,20},{16,24},{20,28},{24,32},{28,36},{32,40... | collective-permute-start | bytes 49160 | tf_op jit(solution)/shard_map/ppermute | solution.py:347
  128.4 11.8 %collective-permute-start.16 = (bf16[32,256]{1,0:T(8,128)(2,1)S(1)}, bf16[32,256]{1,0:T(8,128)(2,1)S(1)}, u32[]{:S(2)}, u32[]{:S(2)}) collective-permute-start(bf16[32,256]{1,0:T(8,128)(2,1)S(1)} %get-tuple-element.14), channel_id=1, source_target_pairs={{0,12},{4,16},{8,20},{12,24},{16,28},{20,32},{24,36},{28,40},{32,4... | collective-permute-start | bytes 49160 | tf_op jit(solution)/shard_map/ppermute | solution.py:347
  133.0 12.6 %collective-permute-start.17 = (bf16[32,256]{1,0:T(8,128)(2,1)S(1)}, bf16[32,256]{1,0:T(8,128)(2,1)S(1)}, u32[]{:S(2)}, u32[]{:S(2)}) collective-permute-start(bf16[32,256]{1,0:T(8,128)(2,1)S(1)} %get-tuple-element.13), channel_id=1, source_target_pairs={{0,16},{4,20},{8,24},{12,28},{16,32},{20,36},{24,40},{28,44},{32,4... | collective-permute-start | bytes 49160 | tf_op jit(solution)/shard_map/ppermute | solution.py:347

commit v2 on v1

v2 whole, which is shorter than its diff:
```python
import functools

import jax
import jax.numpy as jnp
from jax import lax
from jax.experimental import pallas as pl
from jax.experimental.pallas import tpu as pltpu
from jax.sharding import Mesh, PartitionSpec as P

F32 = jnp.float32
BF16 = jnp.bfloat16
EMB = 512
CH = 64
HALF = CH // 2
BAND = 256
BINS = 4096
BLOCK = 32
OWN = 16
HALO = 16
ROWS = OWN + 2 * HALO
WIDE = 384
LEAD = 32
PACK = 96
MARKED = EMB + 128
PIECE = 384
AHEAD = 5
GENOME = ("yl", "x", "z", "core")
CHIPS = ("yl", "x", "z")
ALL = GENOME + ("chan",)
NT = (((1,), (1,)), ((), ()))
TN = (((0,), (0,)), ((), ()))


def dot(a, b, dims=(((1,), (0,)), ((), ()))):
    return lax.dot_general(a, b, dims, preferred_element_type=F32)


def sigmoid(v):
    return 0.5 * jnp.tanh(0.5 * v) + 0.5


def pack_kernel(emb, mask, proj, bias, pair, head, marked, packed):
    marked[:, :EMB] = emb[...]
    line = jnp.broadcast_to(mask[...].astype(F32), (BLOCK, BLOCK))
    row = lax.broadcasted_iota(jnp.int32, (BLOCK, BLOCK), 0)
    own = jnp.where(row == lax.broadcasted_iota(jnp.int32, (BLOCK, BLOCK), 1), line, 0.0)
    column = jnp.sum(own, axis=1, keepdims=True)
    marked[:, EMB:] = jnp.broadcast_to(column, (BLOCK, 128)).astype(BF16)
    packed[:HALF, :] = proj[...]
    packed[32:48, :] = jnp.concatenate([bias[:16], bias[16:]], 1)
    taps = [pair[tap].astype(F32) for tap in range(9)]
    packed[48:80, :] = jnp.concatenate(taps[:8], 1).astype(BF16)
    last = jnp.concatenate([taps[8][:16], taps[8][16:]], 1)
    heads = jnp.concatenate([head[...].astype(F32), jnp.zeros((7, HALF), F32)], 0)
    rest = jnp.zeros((16, EMB - 128 - HALF), F32)
    packed[80:96, :] = jnp.concatenate([last, heads, rest], 1).astype(BF16)


def kernel(scalars, *refs):
    same, sibling = refs[:AHEAD], refs[AHEAD : 2 * AHEAD]
    (
        rim, own_pack, other_pack, target, rim_target,
        keep_out, give_out, w_out,
        window, wt, bias, kf, kb, hk, hkt,
        et, ef, mrow, cmask, pre, hz, d0, h1, d1, s1, s1b, sz, aown, q, rgb, tgw, pacc, g1, pg, hg, gs,
    ) = refs[2 * AHEAD :]
    r0 = scalars[0]
    r1 = scalars[1]
    w0 = scalars[2]
    core = scalars[3]
    chan = scalars[4]
    col = lax.broadcasted_iota(jnp.int32, (1, WIDE), 1)

    def band(r):
        high = jnp.where(w0 + r >= 0, jnp.minimum(r + BAND, BINS - w0), 0)
        return jnp.where((col >= r) & (col < high), 1.0, 0.0).astype(F32)

    def back_roll(v, by):
        return pltpu.roll(v, WIDE - by, 1)

    window[...] = jnp.zeros_like(window)
    for n in range(AHEAD):
        at = LEAD + 64 * n + HALO - OWN * chan
        window[pl.ds(pl.multiple_of(at, 16), BLOCK), :] = same[n][...]
        at = at + BLOCK * (1 - 2 * core)
        window[pl.ds(pl.multiple_of(at, 16), BLOCK), :] = sibling[n][...]

    @pl.when((core == 0) & (chan == 0))
    def _():
        window[LEAD : LEAD + OWN, :] = rim[...]

    @pl.when((core == 1) & (chan == 1))
    def _():
        window[LEAD + 288 : LEAD + 304, :] = rim[...]

    win = window.at[LEAD : LEAD + WIDE]

    flip = jnp.full((PACK, EMB), chan, jnp.int32) == 0
    mine, other = own_pack[...].astype(F32), other_pack[...].astype(F32)
    halves = [jnp.where(flip, mine, other), jnp.where(flip, other, mine)]
    wt[...] = jnp.concatenate([h[:HALF] for h in halves], 0)
    rows = []
    for h in halves:
        rows += [h[32:48, :BAND], h[32:48, BAND:]]
    bias[...] = jnp.concatenate(
        [jnp.concatenate(rows, 0), jnp.zeros((CH, WIDE - BAND), F32)], 1
    )
    taps = []
    for tap in range(9):
        parts = []
        for h in halves:
            if tap < 8:
                parts.append(h[48:80, tap * CH : tap * CH + CH])
            else:
                parts += [h[80:96, :CH], h[80:96, CH : 2 * CH]]
        taps.append(jnp.concatenate(parts, 0))
    grid = lambda pick: jnp.concatenate(
        [jnp.concatenate([taps[pick(n, m)] for m in range(3)], 1) for n in range(3)], 0
    )
    kf[...] = grid(lambda b, a: 3 * a + b).astype(BF16)
    kb[...] = grid(lambda a, b: 3 * a + b).T.astype(BF16)
    heads = jnp.concatenate([h[80:96, 128 : 128 + HALF] for h in halves], 1)
    rest = jnp.zeros((5, CH), F32)
    rows = []
    for b in range(3):
        rows += [heads[3 * a + b : 3 * a + b + 1] for a in range(3)] + [rest]
    hk[...] = jnp.concatenate(rows, 0).astype(BF16)
    rows = []
    for a in range(3):
        rows += [heads[3 * a : 3 * a + 3], rest] * 2
    hkt[...] = jnp.concatenate(rows, 0).T.astype(BF16)

    wide = win[:, :EMB].astype(F32)
    et[...] = wide.T.astype(BF16)
    ef[...] = wide[:ROWS]
    marks = win[:, EMB:].astype(F32)
    mrow[...] = marks[:ROWS]
    cmask[...] = marks.T[:8]

    tgt = jnp.where(
        jnp.full((BLOCK, BAND), chan, jnp.int32) == 0,
        jnp.concatenate([rim_target[...], target[:24]], 0),
        jnp.concatenate([target[8:], rim_target[...]], 0),
    )
    padded = jnp.concatenate([tgt, jnp.zeros((BLOCK, WIDE - BAND), F32)], 1)
    tgw[...] = pltpu.roll(padded, 8, 1, stride=1, stride_axis=0)

    def forward(b, _):
        e8 = ef[pl.ds(pl.multiple_of(b * 8, 8), 8), :]
        w = wt[...]
        a = jnp.concatenate([(w * e8[k : k + 1]).astype(BF16) for k in range(8)], 0)

        @pl.when((b >= 2) & (b < 4))
        def _():
            aown[pl.ds(pl.multiple_of((b - 2) * 512, 512), 512), :] = a

        pre[...] = dot(a, et[...])

        def row(k, _):
            r = b * 8 + k
            v = pre[pl.ds(pl.multiple_of(k * CH, CH), CH), :] + pltpu.roll(bias[...], r, 1)
            s = sigmoid(v)
            m = band(r)
            hz[r] = (v * s * m).astype(BF16)

            @pl.when((r >= HALO) & (r < HALO + OWN))
            def _():
                d0[r - HALO] = s * (1.0 + v * (1.0 - s)) * m

            return 0

        lax.fori_loop(0, 8, row, 0)
        return 0

    lax.fori_loop(0, ROWS // 8, forward, 0)

    def second(n, _):
        for k in range(4):
            r = 4 + n * 4 + k
            near = jnp.concatenate([hz[r - r0], hz[r], hz[r + r0]], 0)
            p = dot(kf[...], near)
            v = pltpu.roll(p[:CH], r0, 1) + p[CH : 2 * CH] + back_roll(p[2 * CH :], r0)
            s = sigmoid(v)
            m = band(r)
            one = (v * s * m).astype(BF16)
            h1[r] = one
            d1[r] = s * (1.0 + v * (1.0 - s)) * m
            p9 = dot(hk[...], one)
            q[r] = pltpu.roll(p9[:8], r1, 1) + p9[8:16] + back_roll(p9[16:24], r1)
        return 0

    lax.fori_loop(0, 10, second, 0)

    which = lax.broadcasted_iota(jnp.int32, (8, WIDE), 0)

    def residual(n, _):
        for k in range(4):
            r = 8 + n * 4 + k
            pred = q[r - r1][0:1] + q[r][1:2] + q[r + r1][2:3]
            mark = mrow[pl.ds(r, 1), :]
            lm = jnp.concatenate([mark] * (WIDE // 128), 1) * cmask[0:1] * band(r)
            rg = lm * (pred - tgw[pl.ds(r - 8, 1), :]) * (1.0 / BAND)
            rg = jnp.broadcast_to(rg, (8, WIDE))
            taps = jnp.where(
                which == 0,
                back_roll(rg, r1),
                jnp.where(which == 1, rg, jnp.where(which == 2, pltpu.roll(rg, r1, 1), 0.0)),
            )
            high = taps.astype(BF16).astype(F32)
            rgb[r] = jnp.concatenate([high, taps - high], 0).astype(BF16)
        return 0

    lax.fori_loop(0, 8, residual, 0)

    def slope(n, _):
        for k in range(4):
            r = 12 + n * 4 + k
            near = jnp.concatenate([rgb[r + r1], rgb[r], rgb[r - r1]], 0)
            s = (dot(hkt[...], near) * d1[r]).astype(BF16)
            s1[r] = s

            @pl.when((r >= HALO) & (r < HALO + OWN))
            def _():
                sf = s.astype(F32)
                s1b[r - HALO] = jnp.concatenate(
                    [back_roll(sf, r0).astype(BF16), s, pltpu.roll(sf, r0, 1).astype(BF16)], 0
                )

        return 0

    lax.fori_loop(0, 6, slope, 0)

    pg[...] = jnp.zeros_like(pg)
    hg[...] = jnp.zeros_like(hg)

    def grads(n, _):
        psum, hsum = 0.0, 0.0
        for k in range(4):
            i = n * 4 + k
            r = HALO + i
            near = jnp.concatenate([hz[r - r0], hz[r], hz[r + r0]], 0)
            psum = psum + dot(s1b[i], near, NT)
            near = jnp.concatenate([h1[r - r1], h1[r], h1[r + r1]], 0)
            hsum = hsum + dot(rgb[r], near, NT)
            near = jnp.concatenate([s1[r + r0], s1[r], s1[r - r0]], 0)
            p = dot(kb[...], near)
            zg = back_roll(p[:CH], r0) + p[CH : 2 * CH] + pltpu.roll(p[2 * CH :], r0, 1)
            sz[pl.ds(pl.multiple_of(i * CH, CH), CH), :] = (zg * d0[i]).astype(BF16)
        pg[...] += psum
        hg[...] += hsum
        return 0

    lax.fori_loop(0, 4, grads, 0)

    pacc[...] = jnp.zeros_like(pacc)

    def back(n, _):
        t = dot(sz[pl.ds(pl.multiple_of(n * 256, 256), 256), :], win[:, :EMB])
        w = wt[...]
        acc = pacc[...]
        for k in range(4):
            tr = t[k * CH : (k + 1) * CH]
            g1[pl.ds(n * 4 + k, 1), :] = jnp.sum(w * tr, axis=0, keepdims=True)
            acc = acc + tr * ef[pl.ds(HALO + n * 4 + k, 1), :]
        pacc[...] = acc
        return 0

    lax.fori_loop(0, 4, back, 0)
    g = dot(sz[...], aown[...], TN)
    gs[...] = g
    gs[HALO : HALO + OWN, :] = g[HALO : HALO + OWN] + g1[...]
    for n in range(2 * AHEAD - 1):
        block = gs[pl.ds(pl.multiple_of(BLOCK * n + HALO - OWN * chan, 16), BLOCK), :]
        if n % 2:
            give_out[n // 2] = block.astype(BF16)
        else:
            keep_out[n // 2] = block

    heads = hg[0:8] + hg[8:16]
    blank = jnp.zeros((8, 256 - 3 * CH), F32)
    for half in range(2):
        tiles = []
        for a in range(4):
            for b in range(4):
                tiles.append(pacc[half * 32 + a * 8 : half * 32 + a * 8 + 8, b * 128 : b * 128 + 128])
        for b in range(3):
            for a in range(4):
                at = b * CH + half * 32 + a * 8
                row = jnp.concatenate([pg[at : at + 8, :], blank], 1)
                tiles += [row[:, :128], row[:, 128:]]
        row = jnp.concatenate([heads, blank], 1)
        tiles += [row[:, :128], row[:, 128:]]
        tiles += [jnp.zeros((8, 128), F32)] * (48 - len(tiles))
        for t, tile in enumerate(tiles):
            at, lane = half * 64 + t % 24 // 3 * 8, t % 3 * 128
            w_out[t // 24, at : at + 8, lane : lane + 128] = tile


VMEM = pl.BlockSpec(memory_space=pltpu.VMEM)
SMEM = pl.BlockSpec(memory_space=pltpu.SMEM)


def run_pack(*args):
    return pl.pallas_call(
        pack_kernel,
        out_shape=(
            jax.ShapeDtypeStruct((BLOCK, MARKED), BF16),
            jax.ShapeDtypeStruct((PACK, EMB), BF16),
        ),
        in_specs=[VMEM] * len(args),
        out_specs=(VMEM, VMEM),
    )(*args)


def run_kernel(*args):
    return pl.pallas_call(
        kernel,
        out_shape=(
            jax.ShapeDtypeStruct((AHEAD, BLOCK, EMB), F32),
            jax.ShapeDtypeStruct((AHEAD - 1, BLOCK, EMB), BF16),
            jax.ShapeDtypeStruct((2, 128, PIECE), F32),
        ),
        in_specs=[SMEM] + [VMEM] * (len(args) - 1),
        out_specs=(VMEM, VMEM, VMEM),
        scratch_shapes=[
            pltpu.VMEM((LEAD + WIDE, MARKED), BF16),
            pltpu.VMEM((CH, EMB), F32),
            pltpu.VMEM((CH, WIDE), F32),
            pltpu.VMEM((3 * CH, 3 * CH), BF16),
            pltpu.VMEM((3 * CH, 3 * CH), BF16),
            pltpu.VMEM((24, CH), BF16),
            pltpu.VMEM((CH, 48), BF16),
            pltpu.VMEM((EMB, WIDE), BF16),
            pltpu.VMEM((ROWS, EMB), F32),
            pltpu.VMEM((ROWS, 128), F32),
            pltpu.VMEM((8, WIDE), F32),
            pltpu.VMEM((8 * CH, WIDE), F32),
            pltpu.VMEM((ROWS, CH, WIDE), BF16),
            pltpu.VMEM((OWN, CH, WIDE), F32),
            pltpu.VMEM((ROWS, CH, WIDE), BF16),
            pltpu.VMEM((ROWS, CH, WIDE), F32),
            pltpu.VMEM((ROWS, CH, WIDE), BF16),
            pltpu.VMEM((OWN, 3 * CH, WIDE), BF16),
            pltpu.VMEM((OWN * CH, WIDE), BF16),
            pltpu.VMEM((OWN * CH, EMB), BF16),
            pltpu.VMEM((ROWS, 8, WIDE), F32),
            pltpu.VMEM((ROWS, 16, WIDE), BF16),
            pltpu.VMEM((BLOCK, WIDE), F32),
            pltpu.VMEM((CH, EMB), F32),
            pltpu.VMEM((OWN, EMB), F32),
            pltpu.VMEM((3 * CH, 3 * CH), F32),
            pltpu.VMEM((16, 3 * CH), F32),
            pltpu.VMEM((WIDE, EMB), F32),
        ],
        compiler_params=pltpu.CompilerParams(vmem_limit_bytes=48 * 1024 * 1024),
    )(*args)


def final_kernel(scalars, own, other, proj_out, pair_out, head_out):
    core = scalars[3]
    chan = scalars[4]
    flip = jnp.full((64, PIECE), core, jnp.int32) == 0
    mine, theirs = own[...], other[...]
    scale = 1.0 / BINS
    both = [jnp.where(flip, mine, theirs) * scale, jnp.where(flip, theirs, mine) * scale]

    def tile(t):
        at, lane = t % 24 // 3 * 8, t % 3 * 128
        return both[t // 24][at : at + 8, lane : lane + 128]

    proj = [jnp.concatenate([tile(4 * a + b) for b in range(4)], 1) for a in range(4)]
    proj_out[...] = jnp.concatenate(proj, 0)
    for b in range(3):
        for a in range(4):
            t = 16 + (b * 4 + a) * 2
            row = jnp.concatenate([tile(t), tile(t + 1)], 1)
            for k in range(3):
                pair_out[3 * k + b, 8 * a : 8 * a + 8, :] = row[:, CH * k : CH * k + CH]
    row = jnp.concatenate([tile(40), tile(41)], 1)
    for k in range(3):
        line = row[:3, CH * k : CH * k + CH]
        first = jnp.full((3, HALF), chan, jnp.int32) == 0
        head_out[3 * k : 3 * k + 3, :] = jnp.where(first, line[:, :HALF], line[:, HALF:])


def run_final(*args):
    return pl.pallas_call(
        final_kernel,
        out_shape=(
            jax.ShapeDtypeStruct((HALF, EMB), F32),
            jax.ShapeDtypeStruct((9, HALF, CH), F32),
            jax.ShapeDtypeStruct((9, HALF), F32),
        ),
        in_specs=[SMEM] + [VMEM] * (len(args) - 1),
        out_specs=(VMEM, VMEM, VMEM),
    )(*args)


def swap(value, axis):
    return lax.ppermute(value, axis, [(0, 1), (1, 0)])


def cycle(value, axes, length, by):
    return lax.ppermute(value, axes, [(i, (i + by) % length) for i in range(length)])


def exchange(value, axes):
    return lax.all_to_all(value, axes, 0, 0, tiled=True)


def local(sizes, embeddings, bin_mask, target, proj_weight, dist_bias, pair_kernel, head_kernel, dilations):
    chips = sizes["yl"] * sizes["x"] * sizes["z"]
    chan = lax.axis_index("chan")
    core = lax.axis_index("core")
    first = (lax.axis_index(GENOME) * 2 + chan) * OWN
    scalars = jnp.stack([dilations[0], dilations[1], first - HALO, core, chan]).astype(jnp.int32)

    marked, packed = run_pack(
        embeddings, bin_mask[None, :], proj_weight.T, dist_bias, pair_kernel, head_kernel
    )
    other_pack = swap(packed, "chan")
    same = [marked] + [cycle(marked, CHIPS, chips, -n) for n in range(1, AHEAD)]
    flat = lambda chip, c, h: (chip % chips * 2 + c) * 2 + h
    routes = []
    for i in range(chips):
        routes.append((flat(i, 1, 0), flat(i + 1, 0, 0)))
        routes.append((flat(i, 0, 1), flat(i - AHEAD, 1, 1)))
        routes.append((flat(i, 0, 0), flat(i, 1, 0)))
        routes.append((flat(i, 1, 1), flat(i, 0, 1)))
    rim = lax.ppermute(jnp.where(core == 0, marked[:OWN], marked[OWN:]), ALL, routes)
    routes = []
    for i in range(2 * chips):
        routes.append((2 * i, (2 * i + 2) % (4 * chips)))
        routes.append((2 * i + 1, (2 * i - 1) % (4 * chips)))
    rim_target = lax.ppermute(jnp.where(chan == 0, target[24:], target[:8]), ALL, routes)
    sibling = [swap(value, "core") for value in same]
    keep, give, w = run_kernel(
        scalars, *same, *sibling, rim, packed, other_pack, target, rim_target
    )

    w_mine = jnp.where(core == 0, w[0], w[1])
    w = w_mine + swap(jnp.where(core == 0, w[1], w[0]), "core")
    w = jnp.sum(exchange(w, ("chan",) + CHIPS), axis=0, keepdims=True)
    w = exchange(jnp.broadcast_to(w, (chips, PIECE)), CHIPS)

    given = swap(give, "core").astype(F32)
    total = 0.0
    for n in range(AHEAD):
        before = given[n - 1] if n > 0 else 0.0
        behind = given[n] if n < AHEAD - 1 else 0.0
        block = keep[n] + jnp.where(core == 0, before, behind)
        if n > 0:
            block = cycle(block.astype(BF16), CHIPS, chips, n).astype(F32)
        total = total + block
    mine = jnp.where(chan == 0, total[:, :256], total[:, 256:])
    other = jnp.where(chan == 0, total[:, 256:], total[:, :256])
    mine = mine + swap(other.astype(BF16), "chan").astype(F32)
    proj, pair, head = run_final(scalars, w, swap(w, "core"))
    return mine, proj.T, pair, head


def solution(mesh):
    split = mesh.devices.reshape(2, 4, 8, 2, 2)
    sizes = dict(yl=2, x=4, z=8, core=2, chan=2)
    fine = Mesh(split, ("yl", "x", "z", "core", "chan"))
    return jax.shard_map(
        functools.partial(local, sizes),
        mesh=fine,
        in_specs=(
            P(GENOME, None),
            P(GENOME),
            P(GENOME, None),
            P(None, "chan"),
            P("chan", None),
            P(None, "chan", None),
            P(None, "chan"),
            P(),
        ),
        out_specs=(P(GENOME, "chan"), P(None, "chan"), P(None, "chan", None), P(None, "chan")),
        check_vma=False,
    )
```

time: 149 us -> 119 us (0.80)
  the two profiles are of different devices: /device:TPU:24 before, /device:TPU:1 now
where the time goes in v2:
time: 119 us; the launch traced here: 118 us
  starting transfers between devices  57.1 us (48%)
  Pallas kernels  40 us (34%)
  waiting for transfers between devices  16.3 us (14%)
  local copies, waits for them, and re-layouts  2.24 us (2%)
  other arithmetic  1.84 us (2%)
    pallas_call x1, Pallas kernels, run_kernel(): pl.pallas_call(kernel, out_shape=(jax.ShapeDtypeStruct((AHEAD, BLOCK, EMB...  36.6 us
    ppermute x8, starting transfers between devices, cycle(): lax.ppermute(value, axes, [(i, (i + by) % length) for i in range(length)])  22.4 us
    all_to_all x2, starting transfers between devices, exchange(): return lax.all_to_all(value, axes, 0, 0, tiled=True)  17.5 us
    ppermute x10, starting transfers between devices, swap(): return lax.ppermute(value, axis, [(0, 1), (1, 0)])  14 us
    ppermute x8, waiting for transfers between devices, cycle(): lax.ppermute(value, axes, [(i, (i + by) % length) for i in range(length)])  7.04 us
    all_to_all x2, waiting for transfers between devices, exchange(): return lax.all_to_all(value, axes, 0, 0, tiled=True)  6.8 us
    ppermute x1, starting transfers between devices, local(): lax.ppermute(jnp.where(core == 0, marked[:OWN], marked[OWN:]), ALL, routes)  3.03 us
    ppermute x10, waiting for transfers between devices, swap(): return lax.ppermute(value, axis, [(0, 1), (1, 0)])  2.44 us
  transfers between devices with their start and end apart: 22, of which 10 were waited for; matrix products, arithmetic and copies ran while one was open for 1% of the time, Pallas kernels for 0%

profile of v2, /device:TPU:1, one launch (start us, length us, event | category | flops | bytes accessed | tf_op | source)
XLA Modules:
  0.0 118.2 jit_solution(473083440833960971)
XLA Ops:
  0.7 1.7 %shard_map.111 = (bf16[32,640]{1,0:T(8,128)(2,1)}, bf16[96,512]{1,0:T(8,128)(2,1)}) custom-call(bf16[32,512]{1,0:T(8,128)(2,1)} %emb.1, s32[1,32]{1,0:T(1,128)} %bitcast.36, bf16[32,512]{1,0:T(8,128)(2,1)} %bitcast.35, bf16[32,256]{1,0:T(8,128)(2,1)} %bias.1, bf16[9,32,64]{2,1,0:T(8,128)(2,1)} %pair.1, bf16[9,32]{1,0:T(8,128)(2,1)} %head.1), custom_call_target="tpu_custom_call" | custom-call | tf_op jit(solution)/shard_map/pallas_call | solution.py:304
  2.4 0.8 slice_select_fusion
  3.2 3.0 %collective-permute-start.9 = (bf16[16,640]{1,0:T(8,128)(2,1)S(1)}, bf16[16,640]{1,0:T(8,128)(2,1)S(1)}, u32[]{:S(2)}, u32[]{:S(2)}) collective-permute-start(bf16[16,640]{1,0:T(8,128)(2,1)S(1)} %slice_select_fusion), channel_id=1, source_target_pairs={{2,4},{1,239},{0,2},{3,1},{6,8},{5,243},{4,6},{7,5},{10,12},{9,247... | collective-permute-start | bytes 61448 | tf_op jit(solution)/shard_map/ppermute | solution.py:430
  6.3 0.4 collective-permute-start.4
  6.7 9.2 %collective-permute-start.3 = (bf16[32,640]{1,0:T(8,128)(2,1)S(1)}, bf16[32,640]{1,0:T(8,128)(2,1)S(1)}, u32[]{:S(2)}, u32[]{:S(2)}) collective-permute-start(bf16[32,640]{1,0:T(8,128)(2,1)S(1)} %copy-done), channel_id=1, source_target_pairs={{0,240},{4,244},{8,248},{12,252},{16,0},{20,4},{24,8},{28,12},{32,... | collective-permute-start | bytes 122888 | tf_op jit(solution)/shard_map/ppermute | solution.py:404
  16.0 3.4 %collective-permute-start.1 = (bf16[32,640]{1,0:T(8,128)(2,1)S(1)}, bf16[32,640]{1,0:T(8,128)(2,1)S(1)}, u32[]{:S(2)}, u32[]{:S(2)}) collective-permute-start(bf16[32,640]{1,0:T(8,128)(2,1)S(1)} %copy-done), channel_id=1, source_target_pairs={{0,248},{4,252},{8,0},{12,4},{16,8},{20,12},{24,16},{28,20},{32,24... | collective-permute-start | bytes 122888 | tf_op jit(solution)/shard_map/ppermute | solution.py:404
  19.4 1.7 %collective-permute-start = (bf16[32,640]{1,0:T(8,128)(2,1)S(1)}, bf16[32,640]{1,0:T(8,128)(2,1)S(1)}, u32[]{:S(2)}, u32[]{:S(2)}) collective-permute-start(bf16[32,640]{1,0:T(8,128)(2,1)S(1)} %copy-done), channel_id=1, source_target_pairs={{0,252},{4,0},{8,4},{12,8},{16,12},{20,16},{24,20},{28,24},{32,28}... | collective-permute-start | bytes 122888 | tf_op jit(solution)/shard_map/ppermute | solution.py:404
  21.0 2.6 %collective-permute-start.10 = (bf16[96,512]{1,0:T(8,128)(2,1)}, bf16[96,512]{1,0:T(8,128)(2,1)S(1)}, u32[]{:S(2)}, u32[]{:S(2)}) collective-permute-start(bf16[96,512]{1,0:T(8,128)(2,1)} %get-tuple-element.13.refs_11_), channel_id=1, source_target_pairs={{0,1},{1,0},{2,3},{3,2},{4,5},{5,4},{6,7},{7,6},{8,9},{9,8},{10,11... | collective-permute-start | bytes 294920 | tf_op jit(solution)/shard_map/ppermute | solution.py:400
  23.6 1.4 %collective-permute-start.8 = (bf16[32,640]{1,0:T(8,128)(2,1)S(1)}, bf16[32,640]{1,0:T(8,128)(2,1)S(1)}, u32[]{:S(2)}, u32[]{:S(2)}) collective-permute-start(bf16[32,640]{1,0:T(8,128)(2,1)S(1)} %collective-permute-done.3.refs_4_), channel_id=1, source_target_pairs={{0,2},{2,0},{1,3},{3,1},{4,6},{6,4},{5,7},{7,5},{8,10},{10,8},{9,1... | collective-permute-start | bytes 122888 | tf_op jit(solution)/shard_map/ppermute | solution.py:400
  25.1 0.4 collective-permute-start.6
  25.9 0.4 collective-permute-done.7.refs_8_
  26.4 0.4 collective-permute-done.5.refs_6_
  26.8 36.6 %shard_map.112 = (f32[5,32,512]{2,1,0:T(8,128)S(1)}, bf16[4,32,512]{2,1,0:T(8,128)(2,1)S(1)}, f32[2,128,384]{2,1,0:T(8,128)S(1)}) custom-call(s32[5]{0:T(128)S(1)} %pad_add_fusion.scalars, bf16[32,640]{1,0:T(8,128)(2,1)S(1)} %copy-done, bf16[32,640]{1,0:T(8,128)(2,1)S(1)} %collective-permute-done.refs_1_, ...), custom_call_target="tpu_custom_call" | custom-call | tf_op jit(solution)/shard_map/pallas_call | solution.py:316
  63.4 1.9 %collective-permute-start.18 = (f32[128,384]{1,0:T(8,128)S(1)}, f32[128,384]{1,0:T(8,128)S(1)}, u32[]{:S(2)}, u32[]{:S(2)}) collective-permute-start(f32[128,384]{1,0:T(8,128)S(1)} %select_bitcast_fusion), channel_id=1, source_target_pairs={{0,2},{2,0},{1,3},{3,1},{4,6},{6,4},{5,7},{7,5},{8,10},{10,8},{9,1... | collective-permute-start | bytes 589832 | tf_op jit(solution)/shard_map/ppermute | solution.py:400
  65.6 1.1 collective-permute-done.12
  66.7 0.9 copy.12
  67.6 10.6 %all-to-all-start = ((f32[128,1,384]{2,1,0:T(1,128)}), f32[128,1,384]{2,1,0:T(1,128)S(1)}, u32[]{:S(2)}, u32[]{:S(2)}) async-start(f32[128,1,384]{2,1,0:T(1,128)} %copy.12), calls=%async_computation | async-start | bytes 393216 | tf_op jit(solution)/shard_map/all_to_all | solution.py:408
  78.3 0.6 collective-permute-start.13
  78.9 4.2 %collective-permute-start.16 = (bf16[32,512]{1,0:T(8,128)(2,1)S(1)}, bf16[32,512]{1,0:T(8,128)(2,1)S(1)}, u32[]{:S(2)}, u32[]{:S(2)}) collective-permute-start(bf16[32,512]{1,0:T(8,128)(2,1)S(1)} %get-tuple-element.21), channel_id=1, source_target_pairs={{0,16},{4,20},{8,24},{12,28},{16,32},{20,36},{24,40},{28,44},{32,4... | collective-permute-start | bytes 98312 | tf_op jit(solution)/shard_map/ppermute | solution.py:404
  83.1 1.2 %collective-permute-start.15 = (bf16[32,512]{1,0:T(8,128)(2,1)S(1)}, bf16[32,512]{1,0:T(8,128)(2,1)S(1)}, u32[]{:S(2)}, u32[]{:S(2)}) collective-permute-start(bf16[32,512]{1,0:T(8,128)(2,1)S(1)} %get-tuple-element.22), channel_id=1, source_target_pairs={{0,12},{4,16},{8,20},{12,24},{16,28},{20,32},{24,36},{28,40},{32,4... | collective-permute-start | bytes 98312 | tf_op jit(solution)/shard_map/ppermute | solution.py:404
  84.3 2.1 %collective-permute-start.14 = (bf16[32,512]{1,0:T(8,128)(2,1)S(1)}, bf16[32,512]{1,0:T(8,128)(2,1)S(1)}, u32[]{:S(2)}, u32[]{:S(2)}) collective-permute-start(bf16[32,512]{1,0:T(8,128)(2,1)S(1)} %get-tuple-element.23), channel_id=1, source_target_pairs={{0,8},{4,12},{8,16},{12,20},{16,24},{20,28},{24,32},{28,36},{32,40... | collective-permute-start | bytes 98312 | tf_op jit(solution)/shard_map/ppermute | solution.py:404
  86.4 0.5 collective-permute-done.13
  86.9 5.1 %collective-permute-done.16 = bf16[32,512]{1,0:T(8,128)(2,1)S(1)} collective-permute-done((bf16[32,512]{1,0:T(8,128)(2,1)S(1)}, bf16[32,512]{1,0:T(8,128)(2,1)S(1)}, u32[]{:S(2)}, u32[]{:S(2)}) %collective-permute-start.16) | collective-permute-done | bytes 32800 | tf_op jit(solution)/shard_map/ppermute | solution.py:404
  92.0 1.4 %collective-permute-done.15 = bf16[32,512]{1,0:T(8,128)(2,1)S(1)} collective-permute-done((bf16[32,512]{1,0:T(8,128)(2,1)S(1)}, bf16[32,512]{1,0:T(8,128)(2,1)S(1)}, u32[]{:S(2)}, u32[]{:S(2)}) %collective-permute-start.15) | collective-permute-done | bytes 32800 | tf_op jit(solution)/shard_map/ppermute | solution.py:404
  93.6 0.7 broadcast_in_dim.17
  94.3 6.9 %all-to-all-start.1 = ((f32[64,1,384]{2,1,0:T(1,128)}), f32[64,1,384]{2,1,0:T(1,128)S(1)}, u32[]{:S(2)}, u32[]{:S(2)}) async-start(f32[64,1,384]{2,1,0:T(1,128)} %broadcast_in_dim.17), calls=%async_computation.1 | async-start | bytes 196608 | tf_op jit(solution)/shard_map/all_to_all | solution.py:408
  101.3 2.9 %collective-permute-start.17 = (bf16[32,256]{1,0:T(8,128)(2,1)S(1)}, bf16[32,256]{1,0:T(8,128)(2,1)S(1)}, u32[]{:S(2)}, u32[]{:S(2)}) collective-permute-start(bf16[32,256]{1,0:T(8,128)(2,1)S(1)} %select_convert_fusion), channel_id=1, source_target_pairs={{0,1},{1,0},{2,3},{3,2},{4,5},{5,4},{6,7},{7,6},{8,9},{9,8},{10,11... | collective-permute-start | bytes 49160 | tf_op jit(solution)/shard_map/ppermute | solution.py:400
  104.2 6.8 %all-to-all-done.1 = f32[64,1,384]{2,1,0:T(1,128)S(1)} async-done(((f32[64,1,384]{2,1,0:T(1,128)}), f32[64,1,384]{2,1,0:T(1,128)S(1)}, u32[]{:S(2)}, u32[]{:S(2)}) %all-to-all-start.1) | async-done | bytes 98336 | tf_op jit(solution)/shard_map/all_to_all | solution.py:408
  111.0 3.9 %collective-permute-start.19 = (f32[64,384]{1,0:T(8,128)S(1)}, f32[64,384]{1,0:T(8,128)S(1)}, u32[]{:S(2)}, u32[]{:S(2)}) collective-permute-start(f32[64,384]{1,0:T(8,128)S(1)} %bitcast.33), channel_id=1, source_target_pairs={{0,2},{2,0},{1,3},{3,1},{4,6},{6,4},{5,7},{7,5},{8,10},{10,8},{9,1... | collective-permute-start | bytes 294920 | tf_op jit(solution)/shard_map/ppermute | solution.py:400
  114.9 0.6 convert_add_fusion
  115.9 0.6 copy-done.5
  116.5 1.7 %shard_map.113 = (f32[32,512]{1,0:T(8,128)}, f32[9,32,64]{2,1,0:T(8,128)}, f32[9,32]{1,0:T(8,128)}) custom-call(s32[5]{0:T(128)} %copy-done.3, f32[64,384]{1,0:T(8,128)} %bitcast.34, f32[64,384]{1,0:T(8,128)} %copy-done.5), custom_call_target="tpu_custom_call" | custom-call | tf_op jit(solution)/shard_map/pallas_call | solution.py:387
  (43 shorter events, 1.7 us)
Async XLA Ops:
  0.6 5.6 %copy-start.2 = (f32[32,256]{1,0:T(8,128)S(1)}, f32[32,256]{1,0:T(8,128)}, u32[]{:S(2)}) copy-start(f32[32,256]{1,0:T(8,128)} %refs_13_.1) | copy-start | bytes 98308
  0.7 25.0 %copy-start.6 = (s32[2]{0:T(128)S(1)}, s32[2]{0:T(128)}, u32[]{:S(2)}) copy-start(s32[2]{0:T(128)} %param.15) | copy-start | bytes 28
  2.4 4.0 %copy-start = (bf16[32,640]{1,0:T(8,128)(2,1)S(1)}, bf16[32,640]{1,0:T(8,128)(2,1)}, u32[]{:S(2)}) copy-start(bf16[32,640]{1,0:T(8,128)(2,1)} %get-tuple-element.12.refs_0_) | copy-start | bytes 122884
  2.4 24.4 %copy-start.1 = (bf16[96,512]{1,0:T(8,128)(2,1)S(1)}, bf16[96,512]{1,0:T(8,128)(2,1)}, u32[]{:S(2)}) copy-start(bf16[96,512]{1,0:T(8,128)(2,1)} %get-tuple-element.13.refs_11_) | copy-start | bytes 294916
  3.2 16.2 %collective-permute-start.9 = (bf16[16,640]{1,0:T(8,128)(2,1)S(1)}, bf16[16,640]{1,0:T(8,128)(2,1)S(1)}, u32[]{:S(2)}, u32[]{:S(2)}) collective-permute-start(bf16[16,640]{1,0:T(8,128)(2,1)S(1)} %slice_select_fusion), channel_id=1, source_target_pairs={{2,4},{1,239},{0,2},{3,1},{6,8},{5,243},{4,6},{7,5},{10,12},{9,247... | collective-permute-start | bytes 61448 | tf_op jit(solution)/shard_map/ppermute | solution.py:430
  6.2 9.8 %collective-permute-start.11 = (f32[8,256]{1,0:T(8,128)S(1)}, f32[8,256]{1,0:T(8,128)S(1)}, u32[]{:S(2)}, u32[]{:S(2)}) collective-permute-start(f32[8,256]{1,0:T(8,128)S(1)} %slice_select_fusion.1), channel_id=1, source_target_pairs={{0,2},{1,255},{2,4},{3,1},{4,6},{5,3},{6,8},{7,5},{8,10},{9,7},{10... | collective-permute-start | bytes 24584 | tf_op jit(solution)/shard_map/ppermute | solution.py:435
  6.3 14.7 %collective-permute-start.4 = (bf16[32,640]{1,0:T(8,128)(2,1)S(1)}, bf16[32,640]{1,0:T(8,128)(2,1)S(1)}, u32[]{:S(2)}, u32[]{:S(2)}) collective-permute-start(bf16[32,640]{1,0:T(8,128)(2,1)S(1)} %copy-done), channel_id=1, source_target_pairs={{0,2},{2,0},{1,3},{3,1},{4,6},{6,4},{5,7},{7,5},{8,10},{10,8},{9,1... | collective-permute-start | bytes 122888 | tf_op jit(solution)/shard_map/ppermute | solution.py:400
  6.7 16.9 %collective-permute-start.3 = (bf16[32,640]{1,0:T(8,128)(2,1)S(1)}, bf16[32,640]{1,0:T(8,128)(2,1)S(1)}, u32[]{:S(2)}, u32[]{:S(2)}) collective-permute-start(bf16[32,640]{1,0:T(8,128)(2,1)S(1)} %copy-done), channel_id=1, source_target_pairs={{0,240},{4,244},{8,248},{12,252},{16,0},{20,4},{24,8},{28,12},{32,... | collective-permute-start | bytes 122888 | tf_op jit(solution)/shard_map/ppermute | solution.py:404
  16.0 9.0 %collective-permute-start.2 = (bf16[32,640]{1,0:T(8,128)(2,1)S(1)}, bf16[32,640]{1,0:T(8,128)(2,1)S(1)}, u32[]{:S(2)}, u32[]{:S(2)}) collective-permute-start(bf16[32,640]{1,0:T(8,128)(2,1)S(1)} %copy-done), channel_id=1, source_target_pairs={{0,244},{4,248},{8,252},{12,0},{16,4},{20,8},{24,12},{28,16},{32,2... | collective-permute-start | bytes 122888 | tf_op jit(solution)/shard_map/ppermute | solution.py:404
  16.0 9.1 %collective-permute-start.1 = (bf16[32,640]{1,0:T(8,128)(2,1)S(1)}, bf16[32,640]{1,0:T(8,128)(2,1)S(1)}, u32[]{:S(2)}, u32[]{:S(2)}) collective-permute-start(bf16[32,640]{1,0:T(8,128)(2,1)S(1)} %copy-done), channel_id=1, source_target_pairs={{0,248},{4,252},{8,0},{12,4},{16,8},{20,12},{24,16},{28,20},{32,24... | collective-permute-start | bytes 122888 | tf_op jit(solution)/shard_map/ppermute | solution.py:404
  19.4 6.2 %collective-permute-start = (bf16[32,640]{1,0:T(8,128)(2,1)S(1)}, bf16[32,640]{1,0:T(8,128)(2,1)S(1)}, u32[]{:S(2)}, u32[]{:S(2)}) collective-permute-start(bf16[32,640]{1,0:T(8,128)(2,1)S(1)} %copy-done), channel_id=1, source_target_pairs={{0,252},{4,0},{8,4},{12,8},{16,12},{20,16},{24,20},{28,24},{32,28}... | collective-permute-start | bytes 122888 | tf_op jit(solution)/shard_map/ppermute | solution.py:404
  21.0 5.7 %collective-permute-start.10 = (bf16[96,512]{1,0:T(8,128)(2,1)}, bf16[96,512]{1,0:T(8,128)(2,1)S(1)}, u32[]{:S(2)}, u32[]{:S(2)}) collective-permute-start(bf16[96,512]{1,0:T(8,128)(2,1)} %get-tuple-element.13.refs_11_), channel_id=1, source_target_pairs={{0,1},{1,0},{2,3},{3,2},{4,5},{5,4},{6,7},{7,6},{8,9},{9,8},{10,11... | collective-permute-start | bytes 294920 | tf_op jit(solution)/shard_map/ppermute | solution.py:400
  23.6 2.3 %collective-permute-start.8 = (bf16[32,640]{1,0:T(8,128)(2,1)S(1)}, bf16[32,640]{1,0:T(8,128)(2,1)S(1)}, u32[]{:S(2)}, u32[]{:S(2)}) collective-permute-start(bf16[32,640]{1,0:T(8,128)(2,1)S(1)} %collective-permute-done.3.refs_4_), channel_id=1, source_target_pairs={{0,2},{2,0},{1,3},{3,1},{4,6},{6,4},{5,7},{7,5},{8,10},{10,8},{9,1... | collective-permute-start | bytes 122888 | tf_op jit(solution)/shard_map/ppermute | solution.py:400
  25.0 1.2 %collective-permute-start.7 = (bf16[32,640]{1,0:T(8,128)(2,1)S(1)}, bf16[32,640]{1,0:T(8,128)(2,1)S(1)}, u32[]{:S(2)}, u32[]{:S(2)}) collective-permute-start(bf16[32,640]{1,0:T(8,128)(2,1)S(1)} %collective-permute-done.2.refs_3_), channel_id=1, source_target_pairs={{0,2},{2,0},{1,3},{3,1},{4,6},{6,4},{5,7},{7,5},{8,10},{10,8},{9,1... | collective-permute-start | bytes 122888 | tf_op jit(solution)/shard_map/ppermute | solution.py:400
  25.1 1.3 %collective-permute-start.6 = (bf16[32,640]{1,0:T(8,128)(2,1)S(1)}, bf16[32,640]{1,0:T(8,128)(2,1)S(1)}, u32[]{:S(2)}, u32[]{:S(2)}) collective-permute-start(bf16[32,640]{1,0:T(8,128)(2,1)S(1)} %collective-permute-done.1.refs_2_), channel_id=1, source_target_pairs={{0,2},{2,0},{1,3},{3,1},{4,6},{6,4},{5,7},{7,5},{8,10},{10,8},{9,1... | collective-permute-start | bytes 122888 | tf_op jit(solution)/shard_map/ppermute | solution.py:400
  25.5 1.2 %collective-permute-start.5 = (bf16[32,640]{1,0:T(8,128)(2,1)S(1)}, bf16[32,640]{1,0:T(8,128)(2,1)S(1)}, u32[]{:S(2)}, u32[]{:S(2)}) collective-permute-start(bf16[32,640]{1,0:T(8,128)(2,1)S(1)} %collective-permute-done.refs_1_), channel_id=1, source_target_pairs={{0,2},{2,0},{1,3},{3,1},{4,6},{6,4},{5,7},{7,5},{8,10},{10,8},{9,1... | collective-permute-start | bytes 122888 | tf_op jit(solution)/shard_map/ppermute | solution.py:400
  25.7 37.6 %copy-start.3 = (s32[5]{0:T(128)}, s32[5]{0:T(128)S(1)}, u32[]{:S(2)}) copy-start(s32[5]{0:T(128)S(1)} %pad_add_fusion.scalars) | copy-start | bytes 64
  63.4 3.3 %collective-permute-start.18 = (f32[128,384]{1,0:T(8,128)S(1)}, f32[128,384]{1,0:T(8,128)S(1)}, u32[]{:S(2)}, u32[]{:S(2)}) collective-permute-start(f32[128,384]{1,0:T(8,128)S(1)} %select_bitcast_fusion), channel_id=1, source_target_pairs={{0,2},{2,0},{1,3},{3,1},{4,6},{6,4},{5,7},{7,5},{8,10},{10,8},{9,1... | collective-permute-start | bytes 589832 | tf_op jit(solution)/shard_map/ppermute | solution.py:400
  65.3 1.3 %collective-permute-start.12 = (bf16[4,32,512]{2,1,0:T(8,128)(2,1)S(1)}, bf16[4,32,512]{2,1,0:T(8,128)(2,1)S(1)}, u32[]{:S(2)}, u32[]{:S(2)}) collective-permute-start(bf16[4,32,512]{2,1,0:T(8,128)(2,1)S(1)} %get-tuple-element.15), channel_id=1, source_target_pairs={{0,2},{2,0},{1,3},{3,1},{4,6},{6,4},{5,7},{7,5},{8,10},{10,8},{9,1... | collective-permute-start | bytes 393224 | tf_op jit(solution)/shard_map/ppermute | solution.py:400
  67.6 25.9 %all-to-all-start = ((f32[128,1,384]{2,1,0:T(1,128)}), f32[128,1,384]{2,1,0:T(1,128)S(1)}, u32[]{:S(2)}, u32[]{:S(2)}) async-start(f32[128,1,384]{2,1,0:T(1,128)} %copy.12), calls=%async_computation | async-start | bytes 393216 | tf_op jit(solution)/shard_map/all_to_all | solution.py:408
  78.3 8.6 %collective-permute-start.13 = (bf16[32,512]{1,0:T(8,128)(2,1)S(1)}, bf16[32,512]{1,0:T(8,128)(2,1)S(1)}, u32[]{:S(2)}, u32[]{:S(2)}) collective-permute-start(bf16[32,512]{1,0:T(8,128)(2,1)S(1)} %get-tuple-element.20), channel_id=1, source_target_pairs={{0,4},{4,8},{8,12},{12,16},{16,20},{20,24},{24,28},{28,32},{32,36}... | collective-permute-start | bytes 98312 | tf_op jit(solution)/shard_map/ppermute | solution.py:404
  78.9 13.1 %collective-permute-start.16 = (bf16[32,512]{1,0:T(8,128)(2,1)S(1)}, bf16[32,512]{1,0:T(8,128)(2,1)S(1)}, u32[]{:S(2)}, u32[]{:S(2)}) collective-permute-start(bf16[32,512]{1,0:T(8,128)(2,1)S(1)} %get-tuple-element.21), channel_id=1, source_target_pairs={{0,16},{4,20},{8,24},{12,28},{16,32},{20,36},{24,40},{28,44},{32,4... | collective-permute-start | bytes 98312 | tf_op jit(solution)/shard_map/ppermute | solution.py:404
  83.1 10.3 %collective-permute-start.15 = (bf16[32,512]{1,0:T(8,128)(2,1)S(1)}, bf16[32,512]{1,0:T(8,128)(2,1)S(1)}, u32[]{:S(2)}, u32[]{:S(2)}) collective-permute-start(bf16[32,512]{1,0:T(8,128)(2,1)S(1)} %get-tuple-element.22), channel_id=1, source_target_pairs={{0,12},{4,16},{8,20},{12,24},{16,28},{20,32},{24,36},{28,40},{32,4... | collective-permute-start | bytes 98312 | tf_op jit(solution)/shard_map/ppermute | solution.py:404
  84.3 9.1 %collective-permute-start.14 = (bf16[32,512]{1,0:T(8,128)(2,1)S(1)}, bf16[32,512]{1,0:T(8,128)(2,1)S(1)}, u32[]{:S(2)}, u32[]{:S(2)}) collective-permute-start(bf16[32,512]{1,0:T(8,128)(2,1)S(1)} %get-tuple-element.23), channel_id=1, source_target_pairs={{0,8},{4,12},{8,16},{12,20},{16,24},{20,28},{24,32},{28,36},{32,40... | collective-permute-start | bytes 98312 | tf_op jit(solution)/shard_map/ppermute | solution.py:404
  94.3 16.6 %all-to-all-start.1 = ((f32[64,1,384]{2,1,0:T(1,128)}), f32[64,1,384]{2,1,0:T(1,128)S(1)}, u32[]{:S(2)}, u32[]{:S(2)}) async-start(f32[64,1,384]{2,1,0:T(1,128)} %broadcast_in_dim.17), calls=%async_computation.1 | async-start | bytes 196608 | tf_op jit(solution)/shard_map/all_to_all | solution.py:408
  101.3 13.7 %collective-permute-start.17 = (bf16[32,256]{1,0:T(8,128)(2,1)S(1)}, bf16[32,256]{1,0:T(8,128)(2,1)S(1)}, u32[]{:S(2)}, u32[]{:S(2)}) collective-permute-start(bf16[32,256]{1,0:T(8,128)(2,1)S(1)} %select_convert_fusion), channel_id=1, source_target_pairs={{0,1},{1,0},{2,3},{3,2},{4,5},{5,4},{6,7},{7,6},{8,9},{9,8},{10,11... | collective-permute-start | bytes 49160 | tf_op jit(solution)/shard_map/ppermute | solution.py:400
  111.0 4.9 %copy-start.4 = (f32[64,1,384]{2,0,1:T(8,128)}, f32[64,1,384]{2,0,1:T(8,128)S(1)}, u32[]{:S(2)}) copy-start(f32[64,1,384]{2,0,1:T(8,128)S(1)} %copy.15) | copy-start | bytes 294916
  111.0 4.9 %collective-permute-start.19 = (f32[64,384]{1,0:T(8,128)S(1)}, f32[64,384]{1,0:T(8,128)S(1)}, u32[]{:S(2)}, u32[]{:S(2)}) collective-permute-start(f32[64,384]{1,0:T(8,128)S(1)} %bitcast.33), channel_id=1, source_target_pairs={{0,2},{2,0},{1,3},{3,1},{4,6},{6,4},{5,7},{7,5},{8,10},{10,8},{9,1... | collective-permute-start | bytes 294920 | tf_op jit(solution)/shard_map/ppermute | solution.py:400
  115.9 0.6 copy-start.5

commit v3 on v2

--- a/solution.py
+++ b/solution.py
@@ -35,8 +35,26 @@
     return lax.dot_general(a, b, dims, preferred_element_type=F32)
 
 
-def sigmoid(v):
-    return 0.5 * jnp.tanh(0.5 * v) + 0.5
+def shift_up(v, by):
+    low = lax.broadcasted_iota(jnp.int32, (v.shape[0], 128), 1) < by
+    tiles = [pltpu.roll(v[:, t : t + 128], by, 1) for t in range(0, v.shape[1], 128)]
+    return jnp.concatenate([jnp.where(low, tiles[n - 1], tiles[n]) for n in range(len(tiles))], 1)
+
+
+def shift_down(v, by):
+    low = lax.broadcasted_iota(jnp.int32, (v.shape[0], 128), 1) < 128 - by
+    tiles = [pltpu.roll(v[:, t : t + 128], 128 - by, 1) for t in range(0, v.shape[1], 128)]
+    tiles.append(tiles[0])
+    return jnp.concatenate(
+        [jnp.where(low, tiles[n], tiles[n + 1]) for n in range(len(tiles) - 1)], 1
+    )
+
+
+def silu_and_slope(u, mask):
+    t = jnp.tanh(u)
+    w = (1.0 + t) * mask
+    value = u * w
+    return value, w + (value - value * t)
 
 
 def pack_kernel(emb, mask, proj, bias, pair, head, marked, packed):
@@ -75,9 +93,6 @@
         high = jnp.where(w0 + r >= 0, jnp.minimum(r + BAND, BINS - w0), 0)
         return jnp.where((col >= r) & (col < high), 1.0, 0.0).astype(F32)
 
-    def back_roll(v, by):
-        return pltpu.roll(v, WIDE - by, 1)
-
     window[...] = jnp.zeros_like(window)
     for n in range(AHEAD):
         at = LEAD + 64 * n + HALO - OWN * chan
@@ -103,7 +118,7 @@
     for h in halves:
         rows += [h[32:48, :BAND], h[32:48, BAND:]]
     bias[...] = jnp.concatenate(
-        [jnp.concatenate(rows, 0), jnp.zeros((CH, WIDE - BAND), F32)], 1
+        [0.5 * jnp.concatenate(rows, 0), jnp.zeros((CH, WIDE - BAND), F32)], 1
     )
     taps = []
     for tap in range(9):
@@ -117,8 +132,8 @@
     grid = lambda pick: jnp.concatenate(
         [jnp.concatenate([taps[pick(n, m)] for m in range(3)], 1) for n in range(3)], 0
     )
-    kf[...] = grid(lambda b, a: 3 * a + b).astype(BF16)
-    kb[...] = grid(lambda a, b: 3 * a + b).T.astype(BF16)
+    kf[...] = (0.5 * grid(lambda b, a: 3 * a + b)).astype(BF16)
+    kb[...] = (0.5 * grid(lambda a, b: 3 * a + b)).T.astype(BF16)
     heads = jnp.concatenate([h[80:96, 128 : 128 + HALF] for h in halves], 1)
     rest = jnp.zeros((5, CH), F32)
     rows = []
@@ -128,7 +143,7 @@
     rows = []
     for a in range(3):
         rows += [heads[3 * a : 3 * a + 3], rest] * 2
-    hkt[...] = jnp.concatenate(rows, 0).T.astype(BF16)
+    hkt[...] = (0.5 * jnp.concatenate(rows, 0)).T.astype(BF16)
 
     wide = win[:, :EMB].astype(F32)
     et[...] = wide.T.astype(BF16)
@@ -147,7 +162,7 @@
 
     def forward(b, _):
         e8 = ef[pl.ds(pl.multiple_of(b * 8, 8), 8), :]
-        w = wt[...]
+        w = 0.5 * wt[...]
         a = jnp.concatenate([(w * e8[k : k + 1]).astype(BF16) for k in range(8)], 0)
 
         @pl.when((b >= 2) & (b < 4))
@@ -156,37 +171,41 @@
 
         pre[...] = dot(a, et[...])
 
-        def row(k, _):
+        for k in range(8):
             r = b * 8 + k
-            v = pre[pl.ds(pl.multiple_of(k * CH, CH), CH), :] + pltpu.roll(bias[...], r, 1)
-            s = sigmoid(v)
-            m = band(r)
-            hz[r] = (v * s * m).astype(BF16)
-
-            @pl.when((r >= HALO) & (r < HALO + OWN))
-            def _():
-                d0[r - HALO] = s * (1.0 + v * (1.0 - s)) * m
-
-            return 0
-
-        lax.fori_loop(0, 8, row, 0)
+            u = pre[k * CH : k * CH + CH, :] + shift_up(bias[...], r)
+            value, gain = silu_and_slope(u, band(r))
+            hz[r] = value.astype(BF16)
+            d0[r] = gain
         return 0
 
     lax.fori_loop(0, ROWS // 8, forward, 0)
 
+    def near(field, r, step):
+        return jnp.concatenate([field[r - step], field[r], field[r + step]], 0)
+
+    def four(rows):
+        return jnp.concatenate(rows, 1)
+
+    def part(v, k):
+        return v[:, k * WIDE : k * WIDE + WIDE]
+
     def second(n, _):
-        for k in range(4):
-            r = 4 + n * 4 + k
-            near = jnp.concatenate([hz[r - r0], hz[r], hz[r + r0]], 0)
-            p = dot(kf[...], near)
-            v = pltpu.roll(p[:CH], r0, 1) + p[CH : 2 * CH] + back_roll(p[2 * CH :], r0)
-            s = sigmoid(v)
-            m = band(r)
-            one = (v * s * m).astype(BF16)
-            h1[r] = one
-            d1[r] = s * (1.0 + v * (1.0 - s)) * m
-            p9 = dot(hk[...], one)
-            q[r] = pltpu.roll(p9[:8], r1, 1) + p9[8:16] + back_roll(p9[16:24], r1)
+        first = 4 + n * 4
+        p = dot(kf[...], four([near(hz, first + k, r0) for k in range(4)]))
+        ones = []
+        for k in range(4):
+            r = first + k
+            pk = part(p, k)
+            u = shift_up(pk[:CH], r0) + pk[CH : 2 * CH] + shift_down(pk[2 * CH :], r0)
+            value, gain = silu_and_slope(u, band(r))
+            ones.append(value.astype(BF16))
+            h1[r] = ones[k]
+            d1[r] = gain
+        p = dot(hk[...], four(ones))
+        for k in range(4):
+            pk = part(p, k)
+            q[first + k] = shift_up(pk[:8], r1) + pk[8:16] + shift_down(pk[16:24], r1)
         return 0
 
     lax.fori_loop(0, 10, second, 0)
@@ -203,8 +222,8 @@
             rg = jnp.broadcast_to(rg, (8, WIDE))
             taps = jnp.where(
                 which == 0,
-                back_roll(rg, r1),
-                jnp.where(which == 1, rg, jnp.where(which == 2, pltpu.roll(rg, r1, 1), 0.0)),
+                shift_down(rg, r1),
+                jnp.where(which == 1, rg, jnp.where(which == 2, shift_up(rg, r1), 0.0)),
             )
             high = taps.astype(BF16).astype(F32)
             rgb[r] = jnp.concatenate([high, taps - high], 0).astype(BF16)
@@ -213,19 +232,17 @@
     lax.fori_loop(0, 8, residual, 0)
 
     def slope(n, _):
-        for k in range(4):
-            r = 12 + n * 4 + k
-            near = jnp.concatenate([rgb[r + r1], rgb[r], rgb[r - r1]], 0)
-            s = (dot(hkt[...], near) * d1[r]).astype(BF16)
+        first = 12 + n * 4
+        h = dot(hkt[...], four([near(rgb, first + k, -r1) for k in range(4)]))
+        for k in range(4):
+            r = first + k
+            sf = part(h, k) * d1[r]
+            s = sf.astype(BF16)
             s1[r] = s
-
-            @pl.when((r >= HALO) & (r < HALO + OWN))
-            def _():
-                sf = s.astype(F32)
-                s1b[r - HALO] = jnp.concatenate(
-                    [back_roll(sf, r0).astype(BF16), s, pltpu.roll(sf, r0, 1).astype(BF16)], 0
-                )
-
+            sf = s.astype(F32)
+            s1b[r] = jnp.concatenate(
+                [shift_down(sf, r0).astype(BF16), s, shift_up(sf, r0).astype(BF16)], 0
+            )
         return 0
 
     lax.fori_loop(0, 6, slope, 0)
@@ -234,20 +251,16 @@
     hg[...] = jnp.zeros_like(hg)
 
     def grads(n, _):
-        psum, hsum = 0.0, 0.0
-        for k in range(4):
-            i = n * 4 + k
-            r = HALO + i
-            near = jnp.concatenate([hz[r - r0], hz[r], hz[r + r0]], 0)
-            psum = psum + dot(s1b[i], near, NT)
-            near = jnp.concatenate([h1[r - r1], h1[r], h1[r + r1]], 0)
-            hsum = hsum + dot(rgb[r], near, NT)
-            near = jnp.concatenate([s1[r + r0], s1[r], s1[r - r0]], 0)
-            p = dot(kb[...], near)
-            zg = back_roll(p[:CH], r0) + p[CH : 2 * CH] + pltpu.roll(p[2 * CH :], r0, 1)
-            sz[pl.ds(pl.multiple_of(i * CH, CH), CH), :] = (zg * d0[i]).astype(BF16)
-        pg[...] += psum
-        hg[...] += hsum
+        first = HALO + n * 4
+        rows = [first + k for k in range(4)]
+        pg[...] += dot(four([s1b[r] for r in rows]), four([near(hz, r, r0) for r in rows]), NT)
+        hg[...] += dot(four([rgb[r] for r in rows]), four([near(h1, r, r1) for r in rows]), NT)
+        p = dot(kb[...], four([near(s1, r, -r0) for r in rows]))
+        for k in range(4):
+            pk = part(p, k)
+            zg = shift_down(pk[:CH], r0) + pk[CH : 2 * CH] + shift_up(pk[2 * CH :], r0)
+            at = pl.multiple_of((n * 4 + k) * CH, CH)
+            sz[pl.ds(at, CH), :] = (zg * d0[first + k]).astype(BF16)
         return 0
 
     lax.fori_loop(0, 4, grads, 0)
@@ -267,6 +280,7 @@
 
     lax.fori_loop(0, 4, back, 0)
     g = dot(sz[...], aown[...], TN)
+    g = 2.0 * g
     gs[...] = g
     gs[HALO : HALO + OWN, :] = g[HALO : HALO + OWN] + g1[...]
     for n in range(2 * AHEAD - 1):
@@ -336,11 +350,11 @@
             pltpu.VMEM((8, WIDE), F32),
             pltpu.VMEM((8 * CH, WIDE), F32),
             pltpu.VMEM((ROWS, CH, WIDE), BF16),
-            pltpu.VMEM((OWN, CH, WIDE), F32),
+            pltpu.VMEM((ROWS, CH, WIDE), F32),
             pltpu.VMEM((ROWS, CH, WIDE), BF16),
             pltpu.VMEM((ROWS, CH, WIDE), F32),
             pltpu.VMEM((ROWS, CH, WIDE), BF16),
-            pltpu.VMEM((OWN, 3 * CH, WIDE), BF16),
+            pltpu.VMEM((ROWS, 3 * CH, WIDE), BF16),
             pltpu.VMEM((OWN * CH, WIDE), BF16),
             pltpu.VMEM((OWN * CH, EMB), BF16),
             pltpu.VMEM((ROWS, 8, WIDE), F32),

time: 119 us -> 102 us (0.86)
  Pallas kernels: 40 us -> 23.1 us
    pallas_call x1, Pallas kernels: 36.6 us -> 19.7 us  [run_kernel(): pl.pallas_call(kernel, out_shape=(jax.ShapeDtypeStruct((AHEAD, BLOCK, EMB...]
where the time goes in v3:
time: 102 us; the launch traced here: 101 us
  starting transfers between devices  57.1 us (56%)
  Pallas kernels  23.1 us (23%)
  waiting for transfers between devices  16.3 us (16%)
  local copies, waits for them, and re-layouts  2.24 us (2%)
  other arithmetic  1.84 us (2%)
    ppermute x8, starting transfers between devices, cycle(): lax.ppermute(value, axes, [(i, (i + by) % length) for i in range(length)])  22.4 us
    pallas_call x1, Pallas kernels, run_kernel(): pl.pallas_call(kernel, out_shape=(jax.ShapeDtypeStruct((AHEAD, BLOCK, EMB...  19.7 us
    all_to_all x2, starting transfers between devices, exchange(): return lax.all_to_all(value, axes, 0, 0, tiled=True)  17.5 us
    ppermute x10, starting transfers between devices, swap(): return lax.ppermute(value, axis, [(0, 1), (1, 0)])  14 us
    ppermute x8, waiting for transfers between devices, cycle(): lax.ppermute(value, axes, [(i, (i + by) % length) for i in range(length)])  7.04 us
    all_to_all x2, waiting for transfers between devices, exchange(): return lax.all_to_all(value, axes, 0, 0, tiled=True)  6.8 us
    ppermute x1, starting transfers between devices, local(): lax.ppermute(jnp.where(core == 0, marked[:OWN], marked[OWN:]), ALL, routes)  3.03 us
    ppermute x10, waiting for transfers between devices, swap(): return lax.ppermute(value, axis, [(0, 1), (1, 0)])  2.44 us
  transfers between devices with their start and end apart: 22, of which 10 were waited for; matrix products, arithmetic and copies ran while one was open for 1% of the time, Pallas kernels for 0%

profile of v3, /device:TPU:1, one launch (start us, length us, event | category | flops | bytes accessed | tf_op | source)
XLA Modules:
  0.0 101.4 jit_solution(16589556353093490084)
XLA Ops:
  0.7 1.7 %shard_map.111 = (bf16[32,640]{1,0:T(8,128)(2,1)}, bf16[96,512]{1,0:T(8,128)(2,1)}) custom-call(bf16[32,512]{1,0:T(8,128)(2,1)} %emb.1, s32[1,32]{1,0:T(1,128)} %bitcast.36, bf16[32,512]{1,0:T(8,128)(2,1)} %bitcast.35, bf16[32,256]{1,0:T(8,128)(2,1)} %bias.1, bf16[9,32,64]{2,1,0:T(8,128)(2,1)} %pair.1, bf16[9,32]{1,0:T(8,128)(2,1)} %head.1), custom_call_target="tpu_custom_call" | custom-call | tf_op jit(solution)/shard_map/pallas_call | solution.py:318
  2.4 0.8 slice_select_fusion
  3.2 3.0 %collective-permute-start.9 = (bf16[16,640]{1,0:T(8,128)(2,1)S(1)}, bf16[16,640]{1,0:T(8,128)(2,1)S(1)}, u32[]{:S(2)}, u32[]{:S(2)}) collective-permute-start(bf16[16,640]{1,0:T(8,128)(2,1)S(1)} %slice_select_fusion), channel_id=1, source_target_pairs={{2,4},{1,239},{0,2},{3,1},{6,8},{5,243},{4,6},{7,5},{10,12},{9,247... | collective-permute-start | bytes 61448 | tf_op jit(solution)/shard_map/ppermute | solution.py:444
  6.3 0.4 collective-permute-start.4
  6.7 9.2 %collective-permute-start.3 = (bf16[32,640]{1,0:T(8,128)(2,1)S(1)}, bf16[32,640]{1,0:T(8,128)(2,1)S(1)}, u32[]{:S(2)}, u32[]{:S(2)}) collective-permute-start(bf16[32,640]{1,0:T(8,128)(2,1)S(1)} %copy-done), channel_id=1, source_target_pairs={{0,240},{4,244},{8,248},{12,252},{16,0},{20,4},{24,8},{28,12},{32,... | collective-permute-start | bytes 122888 | tf_op jit(solution)/shard_map/ppermute | solution.py:418
  16.0 3.4 %collective-permute-start.1 = (bf16[32,640]{1,0:T(8,128)(2,1)S(1)}, bf16[32,640]{1,0:T(8,128)(2,1)S(1)}, u32[]{:S(2)}, u32[]{:S(2)}) collective-permute-start(bf16[32,640]{1,0:T(8,128)(2,1)S(1)} %copy-done), channel_id=1, source_target_pairs={{0,248},{4,252},{8,0},{12,4},{16,8},{20,12},{24,16},{28,20},{32,24... | collective-permute-start | bytes 122888 | tf_op jit(solution)/shard_map/ppermute | solution.py:418
  19.4 1.7 %collective-permute-start = (bf16[32,640]{1,0:T(8,128)(2,1)S(1)}, bf16[32,640]{1,0:T(8,128)(2,1)S(1)}, u32[]{:S(2)}, u32[]{:S(2)}) collective-permute-start(bf16[32,640]{1,0:T(8,128)(2,1)S(1)} %copy-done), channel_id=1, source_target_pairs={{0,252},{4,0},{8,4},{12,8},{16,12},{20,16},{24,20},{28,24},{32,28}... | collective-permute-start | bytes 122888 | tf_op jit(solution)/shard_map/ppermute | solution.py:418
  21.0 2.6 %collective-permute-start.10 = (bf16[96,512]{1,0:T(8,128)(2,1)}, bf16[96,512]{1,0:T(8,128)(2,1)S(1)}, u32[]{:S(2)}, u32[]{:S(2)}) collective-permute-start(bf16[96,512]{1,0:T(8,128)(2,1)} %get-tuple-element.13.refs_11_), channel_id=1, source_target_pairs={{0,1},{1,0},{2,3},{3,2},{4,5},{5,4},{6,7},{7,6},{8,9},{9,8},{10,11... | collective-permute-start | bytes 294920 | tf_op jit(solution)/shard_map/ppermute | solution.py:414
  23.6 1.4 %collective-permute-start.8 = (bf16[32,640]{1,0:T(8,128)(2,1)S(1)}, bf16[32,640]{1,0:T(8,128)(2,1)S(1)}, u32[]{:S(2)}, u32[]{:S(2)}) collective-permute-start(bf16[32,640]{1,0:T(8,128)(2,1)S(1)} %collective-permute-done.3.refs_4_), channel_id=1, source_target_pairs={{0,2},{2,0},{1,3},{3,1},{4,6},{6,4},{5,7},{7,5},{8,10},{10,8},{9,1... | collective-permute-start | bytes 122888 | tf_op jit(solution)/shard_map/ppermute | solution.py:414
  25.1 0.4 collective-permute-start.6
  25.9 0.4 collective-permute-done.7.refs_8_
  26.4 0.4 collective-permute-done.5.refs_6_
  26.8 19.7 %shard_map.112 = (f32[5,32,512]{2,1,0:T(8,128)S(1)}, bf16[4,32,512]{2,1,0:T(8,128)(2,1)S(1)}, f32[2,128,384]{2,1,0:T(8,128)S(1)}) custom-call(s32[5]{0:T(128)S(1)} %pad_add_fusion.scalars, bf16[32,640]{1,0:T(8,128)(2,1)S(1)} %copy-done, bf16[32,640]{1,0:T(8,128)(2,1)S(1)} %collective-permute-done.refs_1_, ...), custom_call_target="tpu_custom_call" | custom-call | tf_op jit(solution)/shard_map/pallas_call | solution.py:330
  46.5 1.9 %collective-permute-start.18 = (f32[128,384]{1,0:T(8,128)S(1)}, f32[128,384]{1,0:T(8,128)S(1)}, u32[]{:S(2)}, u32[]{:S(2)}) collective-permute-start(f32[128,384]{1,0:T(8,128)S(1)} %select_bitcast_fusion), channel_id=1, source_target_pairs={{0,2},{2,0},{1,3},{3,1},{4,6},{6,4},{5,7},{7,5},{8,10},{10,8},{9,1... | collective-permute-start | bytes 589832 | tf_op jit(solution)/shard_map/ppermute | solution.py:414
  48.7 1.1 %collective-permute-done.12 = bf16[4,32,512]{2,1,0:T(8,128)(2,1)S(1)} collective-permute-done((bf16[4,32,512]{2,1,0:T(8,128)(2,1)S(1)}, bf16[4,32,512]{2,1,0:T(8,128)(2,1)S(1)}, u32[]{:S(2)}, u32[]{:S(2)}) %collective-permute-start.12) | collective-permute-done | bytes 131104 | tf_op jit(solution)/shard_map/ppermute | solution.py:414
  49.9 0.9 copy.12
  50.7 10.6 %all-to-all-start = ((f32[128,1,384]{2,1,0:T(1,128)}), f32[128,1,384]{2,1,0:T(1,128)S(1)}, u32[]{:S(2)}, u32[]{:S(2)}) async-start(f32[128,1,384]{2,1,0:T(1,128)} %copy.12), calls=%async_computation | async-start | bytes 393216 | tf_op jit(solution)/shard_map/all_to_all | solution.py:422
  61.4 0.6 collective-permute-start.13
  62.1 4.2 %collective-permute-start.16 = (bf16[32,512]{1,0:T(8,128)(2,1)S(1)}, bf16[32,512]{1,0:T(8,128)(2,1)S(1)}, u32[]{:S(2)}, u32[]{:S(2)}) collective-permute-start(bf16[32,512]{1,0:T(8,128)(2,1)S(1)} %get-tuple-element.21), channel_id=1, source_target_pairs={{0,16},{4,20},{8,24},{12,28},{16,32},{20,36},{24,40},{28,44},{32,4... | collective-permute-start | bytes 98312 | tf_op jit(solution)/shard_map/ppermute | solution.py:418
  66.3 1.2 %collective-permute-start.15 = (bf16[32,512]{1,0:T(8,128)(2,1)S(1)}, bf16[32,512]{1,0:T(8,128)(2,1)S(1)}, u32[]{:S(2)}, u32[]{:S(2)}) collective-permute-start(bf16[32,512]{1,0:T(8,128)(2,1)S(1)} %get-tuple-element.22), channel_id=1, source_target_pairs={{0,12},{4,16},{8,20},{12,24},{16,28},{20,32},{24,36},{28,40},{32,4... | collective-permute-start | bytes 98312 | tf_op jit(solution)/shard_map/ppermute | solution.py:418
  67.5 2.1 %collective-permute-start.14 = (bf16[32,512]{1,0:T(8,128)(2,1)S(1)}, bf16[32,512]{1,0:T(8,128)(2,1)S(1)}, u32[]{:S(2)}, u32[]{:S(2)}) collective-permute-start(bf16[32,512]{1,0:T(8,128)(2,1)S(1)} %get-tuple-element.23), channel_id=1, source_target_pairs={{0,8},{4,12},{8,16},{12,20},{16,24},{20,28},{24,32},{28,36},{32,40... | collective-permute-start | bytes 98312 | tf_op jit(solution)/shard_map/ppermute | solution.py:418
  69.5 0.5 collective-permute-done.13
  70.1 5.1 %collective-permute-done.16 = bf16[32,512]{1,0:T(8,128)(2,1)S(1)} collective-permute-done((bf16[32,512]{1,0:T(8,128)(2,1)S(1)}, bf16[32,512]{1,0:T(8,128)(2,1)S(1)}, u32[]{:S(2)}, u32[]{:S(2)}) %collective-permute-start.16) | collective-permute-done | bytes 32800 | tf_op jit(solution)/shard_map/ppermute | solution.py:418
  75.2 1.4 %collective-permute-done.15 = bf16[32,512]{1,0:T(8,128)(2,1)S(1)} collective-permute-done((bf16[32,512]{1,0:T(8,128)(2,1)S(1)}, bf16[32,512]{1,0:T(8,128)(2,1)S(1)}, u32[]{:S(2)}, u32[]{:S(2)}) %collective-permute-start.15) | collective-permute-done | bytes 32800 | tf_op jit(solution)/shard_map/ppermute | solution.py:418
  76.8 0.7 broadcast_in_dim.17
  77.5 6.9 %all-to-all-start.1 = ((f32[64,1,384]{2,1,0:T(1,128)}), f32[64,1,384]{2,1,0:T(1,128)S(1)}, u32[]{:S(2)}, u32[]{:S(2)}) async-start(f32[64,1,384]{2,1,0:T(1,128)} %broadcast_in_dim.17), calls=%async_computation.1 | async-start | bytes 196608 | tf_op jit(solution)/shard_map/all_to_all | solution.py:422
  84.4 2.9 %collective-permute-start.17 = (bf16[32,256]{1,0:T(8,128)(2,1)S(1)}, bf16[32,256]{1,0:T(8,128)(2,1)S(1)}, u32[]{:S(2)}, u32[]{:S(2)}) collective-permute-start(bf16[32,256]{1,0:T(8,128)(2,1)S(1)} %select_convert_fusion), channel_id=1, source_target_pairs={{0,1},{1,0},{2,3},{3,2},{4,5},{5,4},{6,7},{7,6},{8,9},{9,8},{10,11... | collective-permute-start | bytes 49160 | tf_op jit(solution)/shard_map/ppermute | solution.py:414
  87.3 6.8 %all-to-all-done.1 = f32[64,1,384]{2,1,0:T(1,128)S(1)} async-done(((f32[64,1,384]{2,1,0:T(1,128)}), f32[64,1,384]{2,1,0:T(1,128)S(1)}, u32[]{:S(2)}, u32[]{:S(2)}) %all-to-all-start.1) | async-done | bytes 98336 | tf_op jit(solution)/shard_map/all_to_all | solution.py:422
  94.2 3.9 %collective-permute-start.19 = (f32[64,384]{1,0:T(8,128)S(1)}, f32[64,384]{1,0:T(8,128)S(1)}, u32[]{:S(2)}, u32[]{:S(2)}) collective-permute-start(f32[64,384]{1,0:T(8,128)S(1)} %bitcast.33), channel_id=1, source_target_pairs={{0,2},{2,0},{1,3},{3,1},{4,6},{6,4},{5,7},{7,5},{8,10},{10,8},{9,1... | collective-permute-start | bytes 294920 | tf_op jit(solution)/shard_map/ppermute | solution.py:414
  98.1 0.6 convert_add_fusion
  99.0 0.6 copy-done.5
  99.7 1.7 %shard_map.113 = (f32[32,512]{1,0:T(8,128)}, f32[9,32,64]{2,1,0:T(8,128)}, f32[9,32]{1,0:T(8,128)}) custom-call(s32[5]{0:T(128)} %copy-done.3, f32[64,384]{1,0:T(8,128)} %bitcast.34, f32[64,384]{1,0:T(8,128)} %copy-done.5), custom_call_target="tpu_custom_call" | custom-call | tf_op jit(solution)/shard_map/pallas_call | solution.py:401
  (43 shorter events, 1.7 us)
Async XLA Ops:
  0.6 5.6 %copy-start.2 = (f32[32,256]{1,0:T(8,128)S(1)}, f32[32,256]{1,0:T(8,128)}, u32[]{:S(2)}) copy-start(f32[32,256]{1,0:T(8,128)} %refs_13_.1) | copy-start | bytes 98308
  0.7 25.0 %copy-start.6 = (s32[2]{0:T(128)S(1)}, s32[2]{0:T(128)}, u32[]{:S(2)}) copy-start(s32[2]{0:T(128)} %param.15) | copy-start | bytes 28
  2.4 4.0 %copy-start = (bf16[32,640]{1,0:T(8,128)(2,1)S(1)}, bf16[32,640]{1,0:T(8,128)(2,1)}, u32[]{:S(2)}) copy-start(bf16[32,640]{1,0:T(8,128)(2,1)} %get-tuple-element.12.refs_0_) | copy-start | bytes 122884
  2.4 24.4 %copy-start.1 = (bf16[96,512]{1,0:T(8,128)(2,1)S(1)}, bf16[96,512]{1,0:T(8,128)(2,1)}, u32[]{:S(2)}) copy-start(bf16[96,512]{1,0:T(8,128)(2,1)} %get-tuple-element.13.refs_11_) | copy-start | bytes 294916
  3.2 16.2 %collective-permute-start.9 = (bf16[16,640]{1,0:T(8,128)(2,1)S(1)}, bf16[16,640]{1,0:T(8,128)(2,1)S(1)}, u32[]{:S(2)}, u32[]{:S(2)}) collective-permute-start(bf16[16,640]{1,0:T(8,128)(2,1)S(1)} %slice_select_fusion), channel_id=1, source_target_pairs={{2,4},{1,239},{0,2},{3,1},{6,8},{5,243},{4,6},{7,5},{10,12},{9,247... | collective-permute-start | bytes 61448 | tf_op jit(solution)/shard_map/ppermute | solution.py:444
  6.2 9.8 %collective-permute-start.11 = (f32[8,256]{1,0:T(8,128)S(1)}, f32[8,256]{1,0:T(8,128)S(1)}, u32[]{:S(2)}, u32[]{:S(2)}) collective-permute-start(f32[8,256]{1,0:T(8,128)S(1)} %slice_select_fusion.1), channel_id=1, source_target_pairs={{0,2},{1,255},{2,4},{3,1},{4,6},{5,3},{6,8},{7,5},{8,10},{9,7},{10... | collective-permute-start | bytes 24584 | tf_op jit(solution)/shard_map/ppermute | solution.py:449
  6.3 14.7 %collective-permute-start.4 = (bf16[32,640]{1,0:T(8,128)(2,1)S(1)}, bf16[32,640]{1,0:T(8,128)(2,1)S(1)}, u32[]{:S(2)}, u32[]{:S(2)}) collective-permute-start(bf16[32,640]{1,0:T(8,128)(2,1)S(1)} %copy-done), channel_id=1, source_target_pairs={{0,2},{2,0},{1,3},{3,1},{4,6},{6,4},{5,7},{7,5},{8,10},{10,8},{9,1... | collective-permute-start | bytes 122888 | tf_op jit(solution)/shard_map/ppermute | solution.py:414
  6.7 16.9 %collective-permute-start.3 = (bf16[32,640]{1,0:T(8,128)(2,1)S(1)}, bf16[32,640]{1,0:T(8,128)(2,1)S(1)}, u32[]{:S(2)}, u32[]{:S(2)}) collective-permute-start(bf16[32,640]{1,0:T(8,128)(2,1)S(1)} %copy-done), channel_id=1, source_target_pairs={{0,240},{4,244},{8,248},{12,252},{16,0},{20,4},{24,8},{28,12},{32,... | collective-permute-start | bytes 122888 | tf_op jit(solution)/shard_map/ppermute | solution.py:418
  16.0 9.0 %collective-permute-start.2 = (bf16[32,640]{1,0:T(8,128)(2,1)S(1)}, bf16[32,640]{1,0:T(8,128)(2,1)S(1)}, u32[]{:S(2)}, u32[]{:S(2)}) collective-permute-start(bf16[32,640]{1,0:T(8,128)(2,1)S(1)} %copy-done), channel_id=1, source_target_pairs={{0,244},{4,248},{8,252},{12,0},{16,4},{20,8},{24,12},{28,16},{32,2... | collective-permute-start | bytes 122888 | tf_op jit(solution)/shard_map/ppermute | solution.py:418
  16.0 9.1 %collective-permute-start.1 = (bf16[32,640]{1,0:T(8,128)(2,1)S(1)}, bf16[32,640]{1,0:T(8,128)(2,1)S(1)}, u32[]{:S(2)}, u32[]{:S(2)}) collective-permute-start(bf16[32,640]{1,0:T(8,128)(2,1)S(1)} %copy-done), channel_id=1, source_target_pairs={{0,248},{4,252},{8,0},{12,4},{16,8},{20,12},{24,16},{28,20},{32,24... | collective-permute-start | bytes 122888 | tf_op jit(solution)/shard_map/ppermute | solution.py:418
  19.4 6.2 %collective-permute-start = (bf16[32,640]{1,0:T(8,128)(2,1)S(1)}, bf16[32,640]{1,0:T(8,128)(2,1)S(1)}, u32[]{:S(2)}, u32[]{:S(2)}) collective-permute-start(bf16[32,640]{1,0:T(8,128)(2,1)S(1)} %copy-done), channel_id=1, source_target_pairs={{0,252},{4,0},{8,4},{12,8},{16,12},{20,16},{24,20},{28,24},{32,28}... | collective-permute-start | bytes 122888 | tf_op jit(solution)/shard_map/ppermute | solution.py:418
  21.0 5.7 %collective-permute-start.10 = (bf16[96,512]{1,0:T(8,128)(2,1)}, bf16[96,512]{1,0:T(8,128)(2,1)S(1)}, u32[]{:S(2)}, u32[]{:S(2)}) collective-permute-start(bf16[96,512]{1,0:T(8,128)(2,1)} %get-tuple-element.13.refs_11_), channel_id=1, source_target_pairs={{0,1},{1,0},{2,3},{3,2},{4,5},{5,4},{6,7},{7,6},{8,9},{9,8},{10,11... | collective-permute-start | bytes 294920 | tf_op jit(solution)/shard_map/ppermute | solution.py:414
  23.6 2.3 %collective-permute-start.8 = (bf16[32,640]{1,0:T(8,128)(2,1)S(1)}, bf16[32,640]{1,0:T(8,128)(2,1)S(1)}, u32[]{:S(2)}, u32[]{:S(2)}) collective-permute-start(bf16[32,640]{1,0:T(8,128)(2,1)S(1)} %collective-permute-done.3.refs_4_), channel_id=1, source_target_pairs={{0,2},{2,0},{1,3},{3,1},{4,6},{6,4},{5,7},{7,5},{8,10},{10,8},{9,1... | collective-permute-start | bytes 122888 | tf_op jit(solution)/shard_map/ppermute | solution.py:414
  25.0 1.2 %collective-permute-start.7 = (bf16[32,640]{1,0:T(8,128)(2,1)S(1)}, bf16[32,640]{1,0:T(8,128)(2,1)S(1)}, u32[]{:S(2)}, u32[]{:S(2)}) collective-permute-start(bf16[32,640]{1,0:T(8,128)(2,1)S(1)} %collective-permute-done.2.refs_3_), channel_id=1, source_target_pairs={{0,2},{2,0},{1,3},{3,1},{4,6},{6,4},{5,7},{7,5},{8,10},{10,8},{9,1... | collective-permute-start | bytes 122888 | tf_op jit(solution)/shard_map/ppermute | solution.py:414
  25.1 1.3 %collective-permute-start.6 = (bf16[32,640]{1,0:T(8,128)(2,1)S(1)}, bf16[32,640]{1,0:T(8,128)(2,1)S(1)}, u32[]{:S(2)}, u32[]{:S(2)}) collective-permute-start(bf16[32,640]{1,0:T(8,128)(2,1)S(1)} %collective-permute-done.1.refs_2_), channel_id=1, source_target_pairs={{0,2},{2,0},{1,3},{3,1},{4,6},{6,4},{5,7},{7,5},{8,10},{10,8},{9,1... | collective-permute-start | bytes 122888 | tf_op jit(solution)/shard_map/ppermute | solution.py:414
  25.5 1.2 %collective-permute-start.5 = (bf16[32,640]{1,0:T(8,128)(2,1)S(1)}, bf16[32,640]{1,0:T(8,128)(2,1)S(1)}, u32[]{:S(2)}, u32[]{:S(2)}) collective-permute-start(bf16[32,640]{1,0:T(8,128)(2,1)S(1)} %collective-permute-done.refs_1_), channel_id=1, source_target_pairs={{0,2},{2,0},{1,3},{3,1},{4,6},{6,4},{5,7},{7,5},{8,10},{10,8},{9,1... | collective-permute-start | bytes 122888 | tf_op jit(solution)/shard_map/ppermute | solution.py:414
  25.7 20.8 %copy-start.3 = (s32[5]{0:T(128)}, s32[5]{0:T(128)S(1)}, u32[]{:S(2)}) copy-start(s32[5]{0:T(128)S(1)} %pad_add_fusion.scalars) | copy-start | bytes 64
  46.5 3.3 %collective-permute-start.18 = (f32[128,384]{1,0:T(8,128)S(1)}, f32[128,384]{1,0:T(8,128)S(1)}, u32[]{:S(2)}, u32[]{:S(2)}) collective-permute-start(f32[128,384]{1,0:T(8,128)S(1)} %select_bitcast_fusion), channel_id=1, source_target_pairs={{0,2},{2,0},{1,3},{3,1},{4,6},{6,4},{5,7},{7,5},{8,10},{10,8},{9,1... | collective-permute-start | bytes 589832 | tf_op jit(solution)/shard_map/ppermute | solution.py:414
  48.4 1.3 %collective-permute-start.12 = (bf16[4,32,512]{2,1,0:T(8,128)(2,1)S(1)}, bf16[4,32,512]{2,1,0:T(8,128)(2,1)S(1)}, u32[]{:S(2)}, u32[]{:S(2)}) collective-permute-start(bf16[4,32,512]{2,1,0:T(8,128)(2,1)S(1)} %get-tuple-element.15), channel_id=1, source_target_pairs={{0,2},{2,0},{1,3},{3,1},{4,6},{6,4},{5,7},{7,5},{8,10},{10,8},{9,1... | collective-permute-start | bytes 393224 | tf_op jit(solution)/shard_map/ppermute | solution.py:414
  50.7 25.9 %all-to-all-start = ((f32[128,1,384]{2,1,0:T(1,128)}), f32[128,1,384]{2,1,0:T(1,128)S(1)}, u32[]{:S(2)}, u32[]{:S(2)}) async-start(f32[128,1,384]{2,1,0:T(1,128)} %copy.12), calls=%async_computation | async-start | bytes 393216 | tf_op jit(solution)/shard_map/all_to_all | solution.py:422
  61.4 8.6 %collective-permute-start.13 = (bf16[32,512]{1,0:T(8,128)(2,1)S(1)}, bf16[32,512]{1,0:T(8,128)(2,1)S(1)}, u32[]{:S(2)}, u32[]{:S(2)}) collective-permute-start(bf16[32,512]{1,0:T(8,128)(2,1)S(1)} %get-tuple-element.20), channel_id=1, source_target_pairs={{0,4},{4,8},{8,12},{12,16},{16,20},{20,24},{24,28},{28,32},{32,36}... | collective-permute-start | bytes 98312 | tf_op jit(solution)/shard_map/ppermute | solution.py:418
  62.1 13.1 %collective-permute-start.16 = (bf16[32,512]{1,0:T(8,128)(2,1)S(1)}, bf16[32,512]{1,0:T(8,128)(2,1)S(1)}, u32[]{:S(2)}, u32[]{:S(2)}) collective-permute-start(bf16[32,512]{1,0:T(8,128)(2,1)S(1)} %get-tuple-element.21), channel_id=1, source_target_pairs={{0,16},{4,20},{8,24},{12,28},{16,32},{20,36},{24,40},{28,44},{32,4... | collective-permute-start | bytes 98312 | tf_op jit(solution)/shard_map/ppermute | solution.py:418
  66.3 10.3 %collective-permute-start.15 = (bf16[32,512]{1,0:T(8,128)(2,1)S(1)}, bf16[32,512]{1,0:T(8,128)(2,1)S(1)}, u32[]{:S(2)}, u32[]{:S(2)}) collective-permute-start(bf16[32,512]{1,0:T(8,128)(2,1)S(1)} %get-tuple-element.22), channel_id=1, source_target_pairs={{0,12},{4,16},{8,20},{12,24},{16,28},{20,32},{24,36},{28,40},{32,4... | collective-permute-start | bytes 98312 | tf_op jit(solution)/shard_map/ppermute | solution.py:418
  67.5 9.1 %collective-permute-start.14 = (bf16[32,512]{1,0:T(8,128)(2,1)S(1)}, bf16[32,512]{1,0:T(8,128)(2,1)S(1)}, u32[]{:S(2)}, u32[]{:S(2)}) collective-permute-start(bf16[32,512]{1,0:T(8,128)(2,1)S(1)} %get-tuple-element.23), channel_id=1, source_target_pairs={{0,8},{4,12},{8,16},{12,20},{16,24},{20,28},{24,32},{28,36},{32,40... | collective-permute-start | bytes 98312 | tf_op jit(solution)/shard_map/ppermute | solution.py:418
  77.5 16.6 %all-to-all-start.1 = ((f32[64,1,384]{2,1,0:T(1,128)}), f32[64,1,384]{2,1,0:T(1,128)S(1)}, u32[]{:S(2)}, u32[]{:S(2)}) async-start(f32[64,1,384]{2,1,0:T(1,128)} %broadcast_in_dim.17), calls=%async_computation.1 | async-start | bytes 196608 | tf_op jit(solution)/shard_map/all_to_all | solution.py:422
  84.4 13.7 %collective-permute-start.17 = (bf16[32,256]{1,0:T(8,128)(2,1)S(1)}, bf16[32,256]{1,0:T(8,128)(2,1)S(1)}, u32[]{:S(2)}, u32[]{:S(2)}) collective-permute-start(bf16[32,256]{1,0:T(8,128)(2,1)S(1)} %select_convert_fusion), channel_id=1, source_target_pairs={{0,1},{1,0},{2,3},{3,2},{4,5},{5,4},{6,7},{7,6},{8,9},{9,8},{10,11... | collective-permute-start | bytes 49160 | tf_op jit(solution)/shard_map/ppermute | solution.py:414
  94.1 4.9 %copy-start.4 = (f32[64,1,384]{2,0,1:T(8,128)}, f32[64,1,384]{2,0,1:T(8,128)S(1)}, u32[]{:S(2)}) copy-start(f32[64,1,384]{2,0,1:T(8,128)S(1)} %copy.15) | copy-start | bytes 294916
  94.2 4.9 %collective-permute-start.19 = (f32[64,384]{1,0:T(8,128)S(1)}, f32[64,384]{1,0:T(8,128)S(1)}, u32[]{:S(2)}, u32[]{:S(2)}) collective-permute-start(f32[64,384]{1,0:T(8,128)S(1)} %bitcast.33), channel_id=1, source_target_pairs={{0,2},{2,0},{1,3},{3,1},{4,6},{6,4},{5,7},{7,5},{8,10},{10,8},{9,1... | collective-permute-start | bytes 294920 | tf_op jit(solution)/shard_map/ppermute | solution.py:414
  99.0 0.6 copy-start.5

commit v4 on v3

--- a/solution.py
+++ b/solution.py
@@ -22,7 +22,8 @@
 LEAD = 32
 PACK = 96
 MARKED = EMB + 128
-PIECE = 384
+SLOTS = 64
+TILES = 21
 AHEAD = 5
 GENOME = ("yl", "x", "z", "core")
 CHIPS = ("yl", "x", "z")
@@ -57,36 +58,53 @@
     return value, w + (value - value * t)
 
 
-def pack_kernel(emb, mask, proj, bias, pair, head, marked, packed):
-    marked[:, :EMB] = emb[...]
+def mark_kernel(place, emb, mask, target, marked, first, rim):
+    core = place[1]
+    chan = place[2]
     line = jnp.broadcast_to(mask[...].astype(F32), (BLOCK, BLOCK))
     row = lax.broadcasted_iota(jnp.int32, (BLOCK, BLOCK), 0)
     own = jnp.where(row == lax.broadcasted_iota(jnp.int32, (BLOCK, BLOCK), 1), line, 0.0)
     column = jnp.sum(own, axis=1, keepdims=True)
-    marked[:, EMB:] = jnp.broadcast_to(column, (BLOCK, 128)).astype(BF16)
+    column = jnp.broadcast_to(column, (BLOCK, 128)).astype(BF16)
+    for out in (marked, first):
+        out[:, :EMB] = emb[...]
+        out[:, EMB:MARKED] = column
+    rows = target[pl.ds(pl.multiple_of(24 - 24 * chan, 8), 8), :]
+    high = rows.astype(BF16).astype(F32)
+    low = rows - high
+    high = jnp.concatenate([high[:, :128], high[:, 128:]], 0).astype(BF16)
+    low = jnp.concatenate([low[:, :128], low[:, 128:]], 0).astype(BF16)
+    first[:OWN, MARKED:] = high
+    first[OWN:, MARKED:] = low
+    rim[:, :MARKED] = marked[pl.ds(pl.multiple_of(core * OWN, OWN), OWN), :]
+    rim[:, MARKED : MARKED + 128] = high
+    rim[:, MARKED + 128 :] = low
+
+
+def pack_kernel(proj, bias, pair, head, packed):
     packed[:HALF, :] = proj[...]
     packed[32:48, :] = jnp.concatenate([bias[:16], bias[16:]], 1)
     taps = [pair[tap].astype(F32) for tap in range(9)]
     packed[48:80, :] = jnp.concatenate(taps[:8], 1).astype(BF16)
     last = jnp.concatenate([taps[8][:16], taps[8][16:]], 1)
     heads = jnp.concatenate([head[...].astype(F32), jnp.zeros((7, HALF), F32)], 0)
-    rest = jnp.zeros((16, EMB - 128 - HALF), F32)
-    packed[80:96, :] = jnp.concatenate([last, heads, rest], 1).astype(BF16)
-
-
-def kernel(scalars, *refs):
+    blank = jnp.zeros((16, EMB - 128 - HALF), F32)
+    packed[80:96, :] = jnp.concatenate([last, heads, blank], 1).astype(BF16)
+
+
+def kernel(rates, place, *refs):
     same, sibling = refs[:AHEAD], refs[AHEAD : 2 * AHEAD]
     (
-        rim, own_pack, other_pack, target, rim_target,
+        rim, own_pack, other_pack, target,
         keep_out, give_out, w_out,
         window, wt, bias, kf, kb, hk, hkt,
-        et, ef, mrow, cmask, pre, hz, d0, h1, d1, s1, s1b, sz, aown, q, rgb, tgw, pacc, g1, pg, hg, gs,
+        ef, mrow, cmask, hz, d0, h1, d1, s1, s1b, sz, aown, q, rgb, tgw, pacc, g1, pg, hg, gs,
     ) = refs[2 * AHEAD :]
-    r0 = scalars[0]
-    r1 = scalars[1]
-    w0 = scalars[2]
-    core = scalars[3]
-    chan = scalars[4]
+    r0 = rates[0]
+    r1 = rates[1]
+    w0 = place[0]
+    core = place[1]
+    chan = place[2]
     col = lax.broadcasted_iota(jnp.int32, (1, WIDE), 1)
 
     def band(r):
@@ -96,17 +114,17 @@
     window[...] = jnp.zeros_like(window)
     for n in range(AHEAD):
         at = LEAD + 64 * n + HALO - OWN * chan
-        window[pl.ds(pl.multiple_of(at, 16), BLOCK), :] = same[n][...]
+        window[pl.ds(pl.multiple_of(at, 16), BLOCK), :] = same[n][:, :MARKED]
         at = at + BLOCK * (1 - 2 * core)
-        window[pl.ds(pl.multiple_of(at, 16), BLOCK), :] = sibling[n][...]
+        window[pl.ds(pl.multiple_of(at, 16), BLOCK), :] = sibling[n][:, :MARKED]
 
     @pl.when((core == 0) & (chan == 0))
     def _():
-        window[LEAD : LEAD + OWN, :] = rim[...]
+        window[LEAD : LEAD + OWN, :] = rim[:, :MARKED]
 
     @pl.when((core == 1) & (chan == 1))
     def _():
-        window[LEAD + 288 : LEAD + 304, :] = rim[...]
+        window[LEAD + 288 : LEAD + 304, :] = rim[:, :MARKED]
 
     win = window.at[LEAD : LEAD + WIDE]
 
@@ -146,55 +164,60 @@
     hkt[...] = (0.5 * jnp.concatenate(rows, 0)).T.astype(BF16)
 
     wide = win[:, :EMB].astype(F32)
-    et[...] = wide.T.astype(BF16)
     ef[...] = wide[:ROWS]
     marks = win[:, EMB:].astype(F32)
     mrow[...] = marks[:ROWS]
     cmask[...] = marks.T[:8]
 
+    def joined(parts):
+        whole = parts[0].astype(F32) + parts[1].astype(F32)
+        return jnp.concatenate([whole[:8], whole[8:]], 1)
+
+    def sent(ref):
+        return joined([ref[:OWN, MARKED:], ref[OWN:, MARKED:]])
+
+    def at_core(zero, one):
+        return jnp.where(jnp.full((8, BAND), core, jnp.int32) == 0, zero, one)
+
+    before = joined([rim[:, MARKED : MARKED + 128], rim[:, MARKED + 128 :]])
+    before = at_core(before, sent(sibling[0]))
+    behind = at_core(sent(sibling[0]), sent(sibling[1]))
     tgt = jnp.where(
         jnp.full((BLOCK, BAND), chan, jnp.int32) == 0,
-        jnp.concatenate([rim_target[...], target[:24]], 0),
-        jnp.concatenate([target[8:], rim_target[...]], 0),
+        jnp.concatenate([before, target[:24]], 0),
+        jnp.concatenate([target[8:], behind], 0),
     )
     padded = jnp.concatenate([tgt, jnp.zeros((BLOCK, WIDE - BAND), F32)], 1)
     tgw[...] = pltpu.roll(padded, 8, 1, stride=1, stride_axis=0)
 
-    def forward(b, _):
-        e8 = ef[pl.ds(pl.multiple_of(b * 8, 8), 8), :]
+    for b in range(ROWS // 8):
+        e8 = ef[b * 8 : b * 8 + 8, :]
         w = 0.5 * wt[...]
         a = jnp.concatenate([(w * e8[k : k + 1]).astype(BF16) for k in range(8)], 0)
-
-        @pl.when((b >= 2) & (b < 4))
-        def _():
-            aown[pl.ds(pl.multiple_of((b - 2) * 512, 512), 512), :] = a
-
-        pre[...] = dot(a, et[...])
-
+        if 2 <= b < 4:
+            aown[(b - 2) * 512 : (b - 1) * 512, :] = a
+        p = dot(a, win[:, :EMB], NT)
         for k in range(8):
             r = b * 8 + k
-            u = pre[k * CH : k * CH + CH, :] + shift_up(bias[...], r)
+            u = p[k * CH : k * CH + CH, :] + shift_up(bias[...], r)
             value, gain = silu_and_slope(u, band(r))
             hz[r] = value.astype(BF16)
             d0[r] = gain
-        return 0
-
-    lax.fori_loop(0, ROWS // 8, forward, 0)
 
     def near(field, r, step):
         return jnp.concatenate([field[r - step], field[r], field[r + step]], 0)
 
-    def four(rows):
+    def side(rows):
         return jnp.concatenate(rows, 1)
 
     def part(v, k):
         return v[:, k * WIDE : k * WIDE + WIDE]
 
     def second(n, _):
-        first = 4 + n * 4
-        p = dot(kf[...], four([near(hz, first + k, r0) for k in range(4)]))
+        first = 4 + n * 20
+        p = dot(kf[...], side([near(hz, first + k, r0) for k in range(20)]))
         ones = []
-        for k in range(4):
+        for k in range(20):
             r = first + k
             pk = part(p, k)
             u = shift_up(pk[:CH], r0) + pk[CH : 2 * CH] + shift_down(pk[2 * CH :], r0)
@@ -202,19 +225,19 @@
             ones.append(value.astype(BF16))
             h1[r] = ones[k]
             d1[r] = gain
-        p = dot(hk[...], four(ones))
-        for k in range(4):
+        p = dot(hk[...], side(ones))
+        for k in range(20):
             pk = part(p, k)
             q[first + k] = shift_up(pk[:8], r1) + pk[8:16] + shift_down(pk[16:24], r1)
         return 0
 
-    lax.fori_loop(0, 10, second, 0)
+    lax.fori_loop(0, 2, second, 0)
 
     which = lax.broadcasted_iota(jnp.int32, (8, WIDE), 0)
 
     def residual(n, _):
-        for k in range(4):
-            r = 8 + n * 4 + k
+        for k in range(16):
+            r = 8 + n * 16 + k
             pred = q[r - r1][0:1] + q[r][1:2] + q[r + r1][2:3]
             mark = mrow[pl.ds(r, 1), :]
             lm = jnp.concatenate([mark] * (WIDE // 128), 1) * cmask[0:1] * band(r)
@@ -229,12 +252,12 @@
             rgb[r] = jnp.concatenate([high, taps - high], 0).astype(BF16)
         return 0
 
-    lax.fori_loop(0, 8, residual, 0)
+    lax.fori_loop(0, 2, residual, 0)
 
     def slope(n, _):
-        first = 12 + n * 4
-        h = dot(hkt[...], four([near(rgb, first + k, -r1) for k in range(4)]))
-        for k in range(4):
+        first = 12 + n * 24
+        h = dot(hkt[...], side([near(rgb, first + k, -r1) for k in range(24)]))
+        for k in range(24):
             r = first + k
             sf = part(h, k) * d1[r]
             s = sf.astype(BF16)
@@ -245,40 +268,27 @@
             )
         return 0
 
-    lax.fori_loop(0, 6, slope, 0)
-
-    pg[...] = jnp.zeros_like(pg)
-    hg[...] = jnp.zeros_like(hg)
-
-    def grads(n, _):
-        first = HALO + n * 4
-        rows = [first + k for k in range(4)]
-        pg[...] += dot(four([s1b[r] for r in rows]), four([near(hz, r, r0) for r in rows]), NT)
-        hg[...] += dot(four([rgb[r] for r in rows]), four([near(h1, r, r1) for r in rows]), NT)
-        p = dot(kb[...], four([near(s1, r, -r0) for r in rows]))
+    lax.fori_loop(0, 1, slope, 0)
+
+    rows = range(HALO, HALO + OWN)
+    pg[...] = dot(side([s1b[r] for r in rows]), side([near(hz, r, r0) for r in rows]), NT)
+    hg[...] = dot(side([rgb[r] for r in rows]), side([near(h1, r, r1) for r in rows]), NT)
+    p = dot(kb[...], side([near(s1, r, -r0) for r in rows]))
+    for k, r in enumerate(rows):
+        pk = part(p, k)
+        zg = shift_down(pk[:CH], r0) + pk[CH : 2 * CH] + shift_up(pk[2 * CH :], r0)
+        sz[k * CH : k * CH + CH, :] = (zg * d0[r]).astype(BF16)
+
+    pacc[...] = jnp.zeros_like(pacc)
+
+    w = wt[...]
+    for n in range(4):
+        t = dot(sz[n * 256 : n * 256 + 256, :], win[:, :EMB])
         for k in range(4):
-            pk = part(p, k)
-            zg = shift_down(pk[:CH], r0) + pk[CH : 2 * CH] + shift_up(pk[2 * CH :], r0)
-            at = pl.multiple_of((n * 4 + k) * CH, CH)
-            sz[pl.ds(at, CH), :] = (zg * d0[first + k]).astype(BF16)
-        return 0
-
-    lax.fori_loop(0, 4, grads, 0)
-
-    pacc[...] = jnp.zeros_like(pacc)
-
-    def back(n, _):
-        t = dot(sz[pl.ds(pl.multiple_of(n * 256, 256), 256), :], win[:, :EMB])
-        w = wt[...]
-        acc = pacc[...]
-        for k in range(4):
+            i = n * 4 + k
             tr = t[k * CH : (k + 1) * CH]
-            g1[pl.ds(n * 4 + k, 1), :] = jnp.sum(w * tr, axis=0, keepdims=True)
-            acc = acc + tr * ef[pl.ds(HALO + n * 4 + k, 1), :]
-        pacc[...] = acc
-        return 0
-
-    lax.fori_loop(0, 4, back, 0)
+            g1[i : i + 1, :] = jnp.sum(w * tr, axis=0, keepdims=True)
+            pacc[...] += tr * ef[HALO + i : HALO + i + 1, :]
     g = dot(sz[...], aown[...], TN)
     g = 2.0 * g
     gs[...] = g
@@ -304,25 +314,40 @@
                 tiles += [row[:, :128], row[:, 128:]]
         row = jnp.concatenate([heads, blank], 1)
         tiles += [row[:, :128], row[:, 128:]]
-        tiles += [jnp.zeros((8, 128), F32)] * (48 - len(tiles))
         for t, tile in enumerate(tiles):
-            at, lane = half * 64 + t % 24 // 3 * 8, t % 3 * 128
-            w_out[t // 24, at : at + 8, lane : lane + 128] = tile
+            at = half * SLOTS + t % TILES * 2
+            w_out[t // TILES, at] = tile[:4]
+            w_out[t // TILES, at + 1] = tile[4:]
+        for t in range(2):
+            at = half * SLOTS + 2 * TILES
+            w_out[t, at : at + SLOTS - 2 * TILES] = jnp.zeros((SLOTS - 2 * TILES, 4, 128), F32)
 
 
 VMEM = pl.BlockSpec(memory_space=pltpu.VMEM)
 SMEM = pl.BlockSpec(memory_space=pltpu.SMEM)
+
+
+def run_mark(place, *args):
+    return pl.pallas_call(
+        mark_kernel,
+        out_shape=(
+            jax.ShapeDtypeStruct((BLOCK, MARKED), BF16),
+            jax.ShapeDtypeStruct((BLOCK, MARKED + 128), BF16),
+            jax.ShapeDtypeStruct((OWN, MARKED + 256), BF16),
+        ),
+        in_specs=[SMEM] + [VMEM] * len(args),
+        out_specs=(VMEM,) * 3,
+        compiler_params=pltpu.CompilerParams(vmem_limit_bytes=8 * 1024 * 1024),
+    )(place, *args)
 
 
 def run_pack(*args):
     return pl.pallas_call(
         pack_kernel,
-        out_shape=(
-            jax.ShapeDtypeStruct((BLOCK, MARKED), BF16),
-            jax.ShapeDtypeStruct((PACK, EMB), BF16),
-        ),
+        out_shape=jax.ShapeDtypeStruct((PACK, EMB), BF16),
         in_specs=[VMEM] * len(args),
-        out_specs=(VMEM, VMEM),
+        out_specs=VMEM,
+        compiler_params=pltpu.CompilerParams(vmem_limit_bytes=8 * 1024 * 1024),
     )(*args)
 
 
@@ -332,9 +357,9 @@
         out_shape=(
             jax.ShapeDtypeStruct((AHEAD, BLOCK, EMB), F32),
             jax.ShapeDtypeStruct((AHEAD - 1, BLOCK, EMB), BF16),
-            jax.ShapeDtypeStruct((2, 128, PIECE), F32),
+            jax.ShapeDtypeStruct((2, 2 * SLOTS, 4, 128), F32),
         ),
-        in_specs=[SMEM] + [VMEM] * (len(args) - 1),
+        in_specs=[SMEM] * 2 + [VMEM] * (len(args) - 2),
         out_specs=(VMEM, VMEM, VMEM),
         scratch_shapes=[
             pltpu.VMEM((LEAD + WIDE, MARKED), BF16),
@@ -344,11 +369,9 @@
             pltpu.VMEM((3 * CH, 3 * CH), BF16),
             pltpu.VMEM((24, CH), BF16),
             pltpu.VMEM((CH, 48), BF16),
-            pltpu.VMEM((EMB, WIDE), BF16),
             pltpu.VMEM((ROWS, EMB), F32),
             pltpu.VMEM((ROWS, 128), F32),
             pltpu.VMEM((8, WIDE), F32),
-            pltpu.VMEM((8 * CH, WIDE), F32),
             pltpu.VMEM((ROWS, CH, WIDE), BF16),
             pltpu.VMEM((ROWS, CH, WIDE), F32),
             pltpu.VMEM((ROWS, CH, WIDE), BF16),
@@ -370,17 +393,24 @@
     )(*args)
 
 
-def final_kernel(scalars, own, other, proj_out, pair_out, head_out):
-    core = scalars[3]
-    chan = scalars[4]
-    flip = jnp.full((64, PIECE), core, jnp.int32) == 0
-    mine, theirs = own[...], other[...]
+def final_kernel(place, own, other, *refs):
+    *moved, proj_out, pair_out, head_out, emb_out = refs
+    total = moved[0][...]
+    for block in moved[1:]:
+        total = total + block[...].astype(F32)
+    emb_out[...] = total
+    core = place[1]
+    chan = place[2]
+    flip = jnp.full((8, 128), core, jnp.int32) == 0
     scale = 1.0 / BINS
-    both = [jnp.where(flip, mine, theirs) * scale, jnp.where(flip, theirs, mine) * scale]
 
     def tile(t):
-        at, lane = t % 24 // 3 * 8, t % 3 * 128
-        return both[t // 24][at : at + 8, lane : lane + 128]
+        at = t % TILES * 2
+        mine = jnp.concatenate([own[at], own[at + 1]], 0)
+        theirs = jnp.concatenate([other[at], other[at + 1]], 0)
+        if t < TILES:
+            return jnp.where(flip, mine, theirs) * scale
+        return jnp.where(flip, theirs, mine) * scale
 
     proj = [jnp.concatenate([tile(4 * a + b) for b in range(4)], 1) for a in range(4)]
     proj_out[...] = jnp.concatenate(proj, 0)
@@ -404,9 +434,11 @@
             jax.ShapeDtypeStruct((HALF, EMB), F32),
             jax.ShapeDtypeStruct((9, HALF, CH), F32),
             jax.ShapeDtypeStruct((9, HALF), F32),
+            jax.ShapeDtypeStruct((BLOCK, EMB // 2), F32),
         ),
         in_specs=[SMEM] + [VMEM] * (len(args) - 1),
-        out_specs=(VMEM, VMEM, VMEM),
+        out_specs=(VMEM,) * 4,
+        compiler_params=pltpu.CompilerParams(vmem_limit_bytes=8 * 1024 * 1024),
     )(*args)
 
 
@@ -426,14 +458,14 @@
     chips = sizes["yl"] * sizes["x"] * sizes["z"]
     chan = lax.axis_index("chan")
     core = lax.axis_index("core")
-    first = (lax.axis_index(GENOME) * 2 + chan) * OWN
-    scalars = jnp.stack([dilations[0], dilations[1], first - HALO, core, chan]).astype(jnp.int32)
-
-    marked, packed = run_pack(
-        embeddings, bin_mask[None, :], proj_weight.T, dist_bias, pair_kernel, head_kernel
-    )
+    at = (lax.axis_index(GENOME) * 2 + chan) * OWN - HALO
+    place = jnp.stack([at, core, chan]).astype(jnp.int32)
+
+    marked, first, rim = run_mark(place, embeddings, bin_mask[None, :], target)
+    packed = run_pack(proj_weight.T, dist_bias, pair_kernel, head_kernel)
     other_pack = swap(packed, "chan")
-    same = [marked] + [cycle(marked, CHIPS, chips, -n) for n in range(1, AHEAD)]
+    same = [first, cycle(first, CHIPS, chips, -1), cycle(marked, CHIPS, chips, -2)]
+    same += [cycle(same[n], CHIPS, chips, -2) for n in (1, 2)]
     flat = lambda chip, c, h: (chip % chips * 2 + c) * 2 + h
     routes = []
     for i in range(chips):
@@ -441,36 +473,31 @@
         routes.append((flat(i, 0, 1), flat(i - AHEAD, 1, 1)))
         routes.append((flat(i, 0, 0), flat(i, 1, 0)))
         routes.append((flat(i, 1, 1), flat(i, 0, 1)))
-    rim = lax.ppermute(jnp.where(core == 0, marked[:OWN], marked[OWN:]), ALL, routes)
-    routes = []
-    for i in range(2 * chips):
-        routes.append((2 * i, (2 * i + 2) % (4 * chips)))
-        routes.append((2 * i + 1, (2 * i - 1) % (4 * chips)))
-    rim_target = lax.ppermute(jnp.where(chan == 0, target[24:], target[:8]), ALL, routes)
+    rim = lax.ppermute(rim, ALL, routes)
     sibling = [swap(value, "core") for value in same]
     keep, give, w = run_kernel(
-        scalars, *same, *sibling, rim, packed, other_pack, target, rim_target
+        dilations, place, *same, *sibling, rim, packed, other_pack, target
     )
 
-    w_mine = jnp.where(core == 0, w[0], w[1])
-    w = w_mine + swap(jnp.where(core == 0, w[1], w[0]), "core")
-    w = jnp.sum(exchange(w, ("chan",) + CHIPS), axis=0, keepdims=True)
-    w = exchange(jnp.broadcast_to(w, (chips, PIECE)), CHIPS)
-
     given = swap(give, "core").astype(F32)
-    total = 0.0
-    for n in range(AHEAD):
-        before = given[n - 1] if n > 0 else 0.0
-        behind = given[n] if n < AHEAD - 1 else 0.0
-        block = keep[n] + jnp.where(core == 0, before, behind)
-        if n > 0:
-            block = cycle(block.astype(BF16), CHIPS, chips, n).astype(F32)
-        total = total + block
-    mine = jnp.where(chan == 0, total[:, :256], total[:, 256:])
-    other = jnp.where(chan == 0, total[:, 256:], total[:, :256])
-    mine = mine + swap(other.astype(BF16), "chan").astype(F32)
-    proj, pair, head = run_final(scalars, w, swap(w, "core"))
-    return mine, proj.T, pair, head
+    none = jnp.zeros((1, BLOCK, EMB), F32)
+    before = jnp.concatenate([none, given], 0)
+    behind = jnp.concatenate([given, none], 0)
+    blocks = keep + jnp.where(core == 0, before, behind)
+    low, high = blocks[..., : EMB // 2], blocks[..., EMB // 2 :]
+    other = swap(jnp.where(chan == 0, high, low).astype(BF16), "chan")
+    blocks = jnp.where(chan == 0, low, high) + other.astype(F32)
+    moved = [blocks[0]]
+    moved += [cycle(blocks[n].astype(BF16), CHIPS, chips, n) for n in range(1, AHEAD)]
+
+    w = jnp.where(core == 0, w[0], w[1]) + swap(jnp.where(core == 0, w[1], w[0]), "core")
+    per = SLOTS // chips
+    w = exchange(w.reshape(2 * chips, per * 4, 128), ("chan",) + CHIPS)
+    w = jnp.sum(w, axis=0, keepdims=True)
+    w, *moved[3:] = lax.optimization_barrier((w, *moved[3:]))
+    w = exchange(jnp.broadcast_to(w, (chips, per * 4, 128)), CHIPS).reshape(SLOTS, 4, 128)
+    proj, pair, head, emb = run_final(place, w, swap(w, "core"), *moved)
+    return emb, proj.T, pair, head
 
 
 def solution(mesh):

time: 102 us -> 91.2 us (0.89)
  Pallas kernels: 23.1 us -> 13 us
  starting transfers between devices: 57.1 us -> 52.5 us
  waiting for transfers between devices: 16.3 us -> 19.9 us
  local copies, waits for them, and re-layouts: 2.24 us -> 3.52 us
    all_to_all x2, waiting for transfers between devices: 6.8 us -> 15.8 us  [exchange(): return lax.all_to_all(value, axes, 0, 0, tiled=True)]
    pallas_call x1, Pallas kernels: 19.7 us -> 11 us  [run_kernel(): pl.pallas_call(kernel, out_shape=(jax.ShapeDtypeStruct((AHEAD, BLOCK, EMB...]
    ppermute x8, waiting for transfers between devices: 7.04 us -> 0.02 us  [cycle(): lax.ppermute(value, axes, [(i, (i + by) % length) for i in range(length)])]
    all_to_all x2, starting transfers between devices: 17.5 us -> 11.9 us  [exchange(): return lax.all_to_all(value, axes, 0, 0, tiled=True)]
    unnamed x15 -> x16, local copies, waits for them, and re-layouts: 0.66 us -> 2.83 us
    ppermute x10, starting transfers between devices: 14 us -> 15.6 us  [swap(): return lax.ppermute(value, axis, [(0, 1), (1, 0)])]
    ppermute x2 -> x1, starting transfers between devices: 3.14 us -> 2.23 us  [local(): rim = lax.ppermute(rim, ALL, routes)]
  transfers between devices with their start and end apart: 22 -> 21, of which waited for: 10 -> 8; matrix products, arithmetic and copies ran while one was open for 1% -> 1% of each run, Pallas kernels for 0% -> 0%
where the time goes in v4:
time: 91.2 us; the launch traced here: 90.8 us
  starting transfers between devices  52.5 us (58%)
  waiting for transfers between devices  19.9 us (22%)
  Pallas kernels  13 us (14%)
  local copies, waits for them, and re-layouts  3.52 us (4%)
  other arithmetic  1.19 us (1%)
    ppermute x8, starting transfers between devices, cycle(): lax.ppermute(value, axes, [(i, (i + by) % length) for i in range(length)])  22.8 us
    all_to_all x2, waiting for transfers between devices, exchange(): return lax.all_to_all(value, axes, 0, 0, tiled=True)  15.8 us
    ppermute x10, starting transfers between devices, swap(): return lax.ppermute(value, axis, [(0, 1), (1, 0)])  15.6 us
    all_to_all x2, starting transfers between devices, exchange(): return lax.all_to_all(value, axes, 0, 0, tiled=True)  11.9 us
    pallas_call x1, Pallas kernels, run_kernel(): pl.pallas_call(kernel, out_shape=(jax.ShapeDtypeStruct((AHEAD, BLOCK, EMB...  11 us
    ppermute x10, waiting for transfers between devices, swap(): return lax.ppermute(value, axis, [(0, 1), (1, 0)])  3.08 us
    unnamed x16, local copies, waits for them, and re-layouts  2.83 us
    ppermute x1, starting transfers between devices, local(): rim = lax.ppermute(rim, ALL, routes)  2.23 us
  transfers between devices with their start and end apart: 21, of which 8 were waited for; matrix products, arithmetic and copies ran while one was open for 1% of the time, Pallas kernels for 0%

profile of v4, /device:TPU:1, one launch (start us, length us, event | category | flops | bytes accessed | tf_op | source)
XLA Modules:
  0.0 90.8 jit_solution(7502327319397607091)
XLA Ops:
  0.7 0.6 copy-done
  1.4 0.8 copy-done.3
  2.2 0.7 copy-done.6
  2.8 0.6 shard_map.111
  3.4 9.7 %collective-permute-start = (bf16[32,768]{1,0:T(8,128)(2,1)S(1)}, bf16[32,768]{1,0:T(8,128)(2,1)S(1)}, u32[]{:S(2)}, u32[]{:S(2)}) collective-permute-start(bf16[32,768]{1,0:T(8,128)(2,1)S(1)} %get-tuple-element.17.refs_0_), channel_id=1, source_target_pairs={{0,252},{4,0},{8,4},{12,8},{16,12},{20,16},{24,20},{28,24},{32,28}... | collective-permute-start | bytes 147464 | tf_op jit(solution)/shard_map/ppermute | solution.py:450
  13.1 1.2 %collective-permute-start.1 = (bf16[32,640]{1,0:T(8,128)(2,1)S(1)}, bf16[32,640]{1,0:T(8,128)(2,1)S(1)}, u32[]{:S(2)}, u32[]{:S(2)}) collective-permute-start(bf16[32,640]{1,0:T(8,128)(2,1)S(1)} %get-tuple-element.18), channel_id=1, source_target_pairs={{0,248},{4,252},{8,0},{12,4},{16,8},{20,12},{24,16},{28,20},{32,24... | collective-permute-start | bytes 122888 | tf_op jit(solution)/shard_map/ppermute | solution.py:450
  14.3 0.8 copy-done.2
  15.2 2.7 %collective-permute-start.10 = (bf16[96,512]{1,0:T(8,128)(2,1)S(1)}, bf16[96,512]{1,0:T(8,128)(2,1)S(1)}, u32[]{:S(2)}, u32[]{:S(2)}) collective-permute-start(bf16[96,512]{1,0:T(8,128)(2,1)S(1)} %shard_map.112.refs_11_), channel_id=1, source_target_pairs={{0,1},{1,0},{2,3},{3,2},{4,5},{5,4},{6,7},{7,6},{8,9},{9,8},{10,11... | collective-permute-start | bytes 294920 | tf_op jit(solution)/shard_map/ppermute | solution.py:446
  17.9 1.5 %collective-permute-start.4 = (bf16[32,768]{1,0:T(8,128)(2,1)S(1)}, bf16[32,768]{1,0:T(8,128)(2,1)S(1)}, u32[]{:S(2)}, u32[]{:S(2)}) collective-permute-start(bf16[32,768]{1,0:T(8,128)(2,1)S(1)} %get-tuple-element.17.refs_0_), channel_id=1, source_target_pairs={{0,2},{2,0},{1,3},{3,1},{4,6},{6,4},{5,7},{7,5},{8,10},{10,8},{9,1... | collective-permute-start | bytes 147464 | tf_op jit(solution)/shard_map/ppermute | solution.py:446
  19.4 3.8 %collective-permute-start.3 = (bf16[32,640]{1,0:T(8,128)(2,1)S(1)}, bf16[32,640]{1,0:T(8,128)(2,1)S(1)}, u32[]{:S(2)}, u32[]{:S(2)}) collective-permute-start(bf16[32,640]{1,0:T(8,128)(2,1)S(1)} %collective-permute-done.1.refs_2_), channel_id=1, source_target_pairs={{0,248},{4,252},{8,0},{12,4},{16,8},{20,12},{24,16},{28,20},{32,24... | collective-permute-start | bytes 122888 | tf_op jit(solution)/shard_map/ppermute | solution.py:450
  23.1 2.2 %collective-permute-start.9 = (bf16[16,896]{1,0:T(8,128)(2,1)S(1)}, bf16[16,896]{1,0:T(8,128)(2,1)S(1)}, u32[]{:S(2)}, u32[]{:S(2)}) collective-permute-start(bf16[16,896]{1,0:T(8,128)(2,1)S(1)} %get-tuple-element.19), channel_id=1, source_target_pairs={{2,4},{1,239},{0,2},{3,1},{6,8},{5,243},{4,6},{7,5},{10,12},{9,247... | collective-permute-start | bytes 86024 | tf_op jit(solution)/shard_map/ppermute | solution.py:476
  25.4 1.0 %collective-permute-done.9.refs_10_ = bf16[16,896]{1,0:T(8,128)(2,1)S(1)} collective-permute-done((bf16[16,896]{1,0:T(8,128)(2,1)S(1)}, bf16[16,896]{1,0:T(8,128)(2,1)S(1)}, u32[]{:S(2)}, u32[]{:S(2)}) %collective-permute-start.9) | collective-permute-done | bytes 28704 | tf_op jit(solution)/shard_map/ppermute | solution.py:476
  26.4 5.9 %collective-permute-start.5 = (bf16[32,768]{1,0:T(8,128)(2,1)S(1)}, bf16[32,768]{1,0:T(8,128)(2,1)S(1)}, u32[]{:S(2)}, u32[]{:S(2)}) collective-permute-start(bf16[32,768]{1,0:T(8,128)(2,1)S(1)} %collective-permute-done.refs_1_), channel_id=1, source_target_pairs={{0,2},{2,0},{1,3},{3,1},{4,6},{6,4},{5,7},{7,5},{8,10},{10,8},{9,1... | collective-permute-start | bytes 147464 | tf_op jit(solution)/shard_map/ppermute | solution.py:446
  32.3 0.5 collective-permute-start.6
  32.9 0.8 collective-permute-done.6.refs_7_
  33.7 0.3 collective-permute-done.8.refs_9_
  34.0 11.0 %shard_map.113 = (f32[5,32,512]{2,1,0:T(8,128)S(1)}, bf16[4,32,512]{2,1,0:T(8,128)(2,1)S(1)}, f32[2,128,4,128]{3,2,1,0:T(4,128)S(1)}) custom-call(s32[2]{0:T(128)S(1)} %copy-done.7, s32[3]{0:T(128)S(1)} %pad_add_fusion.place, bf16[32,768]{1,0:T(8,128)(2,1)S(1)} %get-tuple-element.17.refs_0_, bf16[32,768]{1,0:T(8,128)(2,1)S(1)} %collective-permute-done.refs_1_, ...), custom_call_target="tpu_custom_call" | custom-call | tf_op jit(solution)/shard_map/pallas_call | solution.py:355
  45.3 0.4 collective-permute-start.11
  45.8 0.7 collective-permute-done.12
  46.7 0.3 collective-permute-done.11
  46.9 0.8 bitcast_add_fusion
  47.7 7.3 %all-to-all-start = ((f32[128,4,128]{2,1,0:T(4,128)}), f32[128,4,128]{2,1,0:T(4,128)S(1)}, u32[]{:S(2)}, u32[]{:S(2)}) async-start(f32[128,4,128]{2,1,0:T(4,128)} %bitcast_add_fusion), calls=%async_computation | async-start | bytes 524288 | tf_op jit(solution)/shard_map/all_to_all | solution.py:454
  55.1 4.8 %collective-permute-start.15 = (bf16[32,256]{1,0:T(8,128)(2,1)S(1)}, bf16[32,256]{1,0:T(8,128)(2,1)S(1)}, u32[]{:S(2)}, u32[]{:S(2)}) collective-permute-start(bf16[32,256]{1,0:T(8,128)(2,1)S(1)} %get-tuple-element.34), channel_id=1, source_target_pairs={{0,16},{4,20},{8,24},{12,28},{16,32},{20,36},{24,40},{28,44},{32,4... | collective-permute-start | bytes 49160 | tf_op jit(solution)/shard_map/ppermute | solution.py:450
  60.1 8.9 %all-to-all-done = f32[128,4,128]{2,1,0:T(4,128)S(1)} async-done(((f32[128,4,128]{2,1,0:T(4,128)}), f32[128,4,128]{2,1,0:T(4,128)S(1)}, u32[]{:S(2)}, u32[]{:S(2)}) %all-to-all-start) | async-done | bytes 262176 | tf_op jit(solution)/shard_map/all_to_all | solution.py:454
  69.2 0.7 broadcast_in_dim.17
  69.8 4.6 %all-to-all-start.1 = ((f32[64,4,128]{2,1,0:T(4,128)}), f32[64,4,128]{2,1,0:T(4,128)S(1)}, u32[]{:S(2)}, u32[]{:S(2)}) async-start(f32[64,4,128]{2,1,0:T(4,128)} %broadcast_in_dim.17), calls=%async_computation.1 | async-start | bytes 262144 | tf_op jit(solution)/shard_map/all_to_all | solution.py:454
  74.5 1.9 %collective-permute-start.18 = (bf16[32,256]{1,0:T(8,128)(2,1)S(1)}, bf16[32,256]{1,0:T(8,128)(2,1)S(1)}, u32[]{:S(2)}, u32[]{:S(2)}) collective-permute-start(bf16[32,256]{1,0:T(8,128)(2,1)S(1)} %get-tuple-element.32), channel_id=1, source_target_pairs={{0,8},{4,12},{8,16},{12,20},{16,24},{20,28},{24,32},{28,36},{32,40... | collective-permute-start | bytes 49160 | tf_op jit(solution)/shard_map/ppermute | solution.py:450
  76.4 1.2 %collective-permute-start.17 = (bf16[32,256]{1,0:T(8,128)(2,1)S(1)}, bf16[32,256]{1,0:T(8,128)(2,1)S(1)}, u32[]{:S(2)}, u32[]{:S(2)}) collective-permute-start(bf16[32,256]{1,0:T(8,128)(2,1)S(1)} %get-tuple-element.33), channel_id=1, source_target_pairs={{0,4},{4,8},{8,12},{12,16},{16,20},{20,24},{24,28},{28,32},{32,36}... | collective-permute-start | bytes 49160 | tf_op jit(solution)/shard_map/ppermute | solution.py:450
  77.5 6.9 %all-to-all-done.1.own = f32[64,4,128]{2,1,0:T(4,128)S(1)} async-done(((f32[64,4,128]{2,1,0:T(4,128)}), f32[64,4,128]{2,1,0:T(4,128)S(1)}, u32[]{:S(2)}, u32[]{:S(2)}) %all-to-all-start.1) | async-done | bytes 131104 | tf_op jit(solution)/shard_map/all_to_all | solution.py:454
  84.5 4.1 %collective-permute-start.16 = (f32[64,4,128]{2,1,0:T(4,128)S(1)}, f32[64,4,128]{2,1,0:T(4,128)S(1)}, u32[]{:S(2)}, u32[]{:S(2)}) collective-permute-start(f32[64,4,128]{2,1,0:T(4,128)S(1)} %all-to-all-done.1.own), channel_id=1, source_target_pairs={{0,2},{2,0},{1,3},{3,1},{4,6},{6,4},{5,7},{7,5},{8,10},{10,8},{9,1... | collective-permute-start | bytes 393224 | tf_op jit(solution)/shard_map/ppermute | solution.py:446
  88.5 1.0 %collective-permute-done.16.other = f32[64,4,128]{2,1,0:T(4,128)S(1)} collective-permute-done((f32[64,4,128]{2,1,0:T(4,128)S(1)}, f32[64,4,128]{2,1,0:T(4,128)S(1)}, u32[]{:S(2)}, u32[]{:S(2)}) %collective-permute-start.16) | collective-permute-done | bytes 131104 | tf_op jit(solution)/shard_map/ppermute | solution.py:446
  89.5 1.3 %shard_map.114 = (f32[32,512]{1,0:T(8,128)}, f32[9,32,64]{2,1,0:T(8,128)}, f32[9,32]{1,0:T(8,128)}, f32[32,256]{1,0:T(8,128)}) custom-call(s32[3]{0:T(128)S(1)} %pad_add_fusion.place, f32[64,4,128]{2,1,0:T(4,128)S(1)} %all-to-all-done.1.own, f32[64,4,128]{2,1,0:T(4,128)S(1)} %collective-permute-done.16.other, f32[32,256]{1,0:T(8,128)S(1)} %slice_bitcast_fusion.refs_0_, ...), custom_call_target="tpu_custom_call" | custom-call | tf_op jit(solution)/shard_map/pallas_call | solution.py:431
  (41 shorter events, 1.3 us)
Async XLA Ops:
  0.6 0.8 copy-start
  0.6 13.7 %copy-start.1 = (bf16[9,32,64]{2,1,0:T(8,128)(2,1)S(1)}, bf16[9,32,64]{2,1,0:T(8,128)(2,1)}, u32[]{:S(2)}) copy-start(bf16[9,32,64]{2,1,0:T(8,128)(2,1)} %pair.1) | copy-start | bytes 110596
  1.4 0.8 copy-start.3
  2.1 0.7 copy-start.6
  2.8 11.5 %copy-start.4 = (bf16[32,256]{1,0:T(8,128)(2,1)S(1)}, bf16[32,256]{1,0:T(8,128)(2,1)}, u32[]{:S(2)}) copy-start(bf16[32,256]{1,0:T(8,128)(2,1)} %bias.1) | copy-start | bytes 49156
  3.4 10.9 %copy-start.5 = (bf16[9,32]{1,0:T(8,128)(2,1)S(1)}, bf16[9,32]{1,0:T(8,128)(2,1)}, u32[]{:S(2)}) copy-start(bf16[9,32]{1,0:T(8,128)(2,1)} %head.1) | copy-start | bytes 1732
  3.4 14.4 %collective-permute-start = (bf16[32,768]{1,0:T(8,128)(2,1)S(1)}, bf16[32,768]{1,0:T(8,128)(2,1)S(1)}, u32[]{:S(2)}, u32[]{:S(2)}) collective-permute-start(bf16[32,768]{1,0:T(8,128)(2,1)S(1)} %get-tuple-element.17.refs_0_), channel_id=1, source_target_pairs={{0,252},{4,0},{8,4},{12,8},{16,12},{20,16},{24,20},{28,24},{32,28}... | collective-permute-start | bytes 147464 | tf_op jit(solution)/shard_map/ppermute | solution.py:450
  13.1 6.3 %collective-permute-start.1 = (bf16[32,640]{1,0:T(8,128)(2,1)S(1)}, bf16[32,640]{1,0:T(8,128)(2,1)S(1)}, u32[]{:S(2)}, u32[]{:S(2)}) collective-permute-start(bf16[32,640]{1,0:T(8,128)(2,1)S(1)} %get-tuple-element.18), channel_id=1, source_target_pairs={{0,248},{4,252},{8,0},{12,4},{16,8},{20,12},{24,16},{28,20},{32,24... | collective-permute-start | bytes 122888 | tf_op jit(solution)/shard_map/ppermute | solution.py:450
  14.3 0.8 copy-start.2
  15.2 18.5 %collective-permute-start.10 = (bf16[96,512]{1,0:T(8,128)(2,1)S(1)}, bf16[96,512]{1,0:T(8,128)(2,1)S(1)}, u32[]{:S(2)}, u32[]{:S(2)}) collective-permute-start(bf16[96,512]{1,0:T(8,128)(2,1)S(1)} %shard_map.112.refs_11_), channel_id=1, source_target_pairs={{0,1},{1,0},{2,3},{3,2},{4,5},{5,4},{6,7},{7,6},{8,9},{9,8},{10,11... | collective-permute-start | bytes 294920 | tf_op jit(solution)/shard_map/ppermute | solution.py:446
  17.9 14.4 %collective-permute-start.2 = (bf16[32,768]{1,0:T(8,128)(2,1)S(1)}, bf16[32,768]{1,0:T(8,128)(2,1)S(1)}, u32[]{:S(2)}, u32[]{:S(2)}) collective-permute-start(bf16[32,768]{1,0:T(8,128)(2,1)S(1)} %collective-permute-done.refs_1_), channel_id=1, source_target_pairs={{0,248},{4,252},{8,0},{12,4},{16,8},{20,12},{24,16},{28,20},{32,24... | collective-permute-start | bytes 147464 | tf_op jit(solution)/shard_map/ppermute | solution.py:450
  17.9 14.4 %collective-permute-start.4 = (bf16[32,768]{1,0:T(8,128)(2,1)S(1)}, bf16[32,768]{1,0:T(8,128)(2,1)S(1)}, u32[]{:S(2)}, u32[]{:S(2)}) collective-permute-start(bf16[32,768]{1,0:T(8,128)(2,1)S(1)} %get-tuple-element.17.refs_0_), channel_id=1, source_target_pairs={{0,2},{2,0},{1,3},{3,1},{4,6},{6,4},{5,7},{7,5},{8,10},{10,8},{9,1... | collective-permute-start | bytes 147464 | tf_op jit(solution)/shard_map/ppermute | solution.py:446
  19.4 13.4 %collective-permute-start.3 = (bf16[32,640]{1,0:T(8,128)(2,1)S(1)}, bf16[32,640]{1,0:T(8,128)(2,1)S(1)}, u32[]{:S(2)}, u32[]{:S(2)}) collective-permute-start(bf16[32,640]{1,0:T(8,128)(2,1)S(1)} %collective-permute-done.1.refs_2_), channel_id=1, source_target_pairs={{0,248},{4,252},{8,0},{12,4},{16,8},{20,12},{24,16},{28,20},{32,24... | collective-permute-start | bytes 122888 | tf_op jit(solution)/shard_map/ppermute | solution.py:450
  23.1 3.2 %collective-permute-start.9 = (bf16[16,896]{1,0:T(8,128)(2,1)S(1)}, bf16[16,896]{1,0:T(8,128)(2,1)S(1)}, u32[]{:S(2)}, u32[]{:S(2)}) collective-permute-start(bf16[16,896]{1,0:T(8,128)(2,1)S(1)} %get-tuple-element.19), channel_id=1, source_target_pairs={{2,4},{1,239},{0,2},{3,1},{6,8},{5,243},{4,6},{7,5},{10,12},{9,247... | collective-permute-start | bytes 86024 | tf_op jit(solution)/shard_map/ppermute | solution.py:476
  26.4 7.3 %collective-permute-start.5 = (bf16[32,768]{1,0:T(8,128)(2,1)S(1)}, bf16[32,768]{1,0:T(8,128)(2,1)S(1)}, u32[]{:S(2)}, u32[]{:S(2)}) collective-permute-start(bf16[32,768]{1,0:T(8,128)(2,1)S(1)} %collective-permute-done.refs_1_), channel_id=1, source_target_pairs={{0,2},{2,0},{1,3},{3,1},{4,6},{6,4},{5,7},{7,5},{8,10},{10,8},{9,1... | collective-permute-start | bytes 147464 | tf_op jit(solution)/shard_map/ppermute | solution.py:446
  32.3 1.7 %collective-permute-start.7 = (bf16[32,768]{1,0:T(8,128)(2,1)S(1)}, bf16[32,768]{1,0:T(8,128)(2,1)S(1)}, u32[]{:S(2)}, u32[]{:S(2)}) collective-permute-start(bf16[32,768]{1,0:T(8,128)(2,1)S(1)} %collective-permute-done.2.refs_3_), channel_id=1, source_target_pairs={{0,2},{2,0},{1,3},{3,1},{4,6},{6,4},{5,7},{7,5},{8,10},{10,8},{9,1... | collective-permute-start | bytes 147464 | tf_op jit(solution)/shard_map/ppermute | solution.py:446
  32.3 1.4 %collective-permute-start.6 = (bf16[32,640]{1,0:T(8,128)(2,1)S(1)}, bf16[32,640]{1,0:T(8,128)(2,1)S(1)}, u32[]{:S(2)}, u32[]{:S(2)}) collective-permute-start(bf16[32,640]{1,0:T(8,128)(2,1)S(1)} %collective-permute-done.1.refs_2_), channel_id=1, source_target_pairs={{0,2},{2,0},{1,3},{3,1},{4,6},{6,4},{5,7},{7,5},{8,10},{10,8},{9,1... | collective-permute-start | bytes 122888 | tf_op jit(solution)/shard_map/ppermute | solution.py:446
  32.8 1.2 %collective-permute-start.8 = (bf16[32,640]{1,0:T(8,128)(2,1)S(1)}, bf16[32,640]{1,0:T(8,128)(2,1)S(1)}, u32[]{:S(2)}, u32[]{:S(2)}) collective-permute-start(bf16[32,640]{1,0:T(8,128)(2,1)S(1)} %collective-permute-done.3.refs_4_), channel_id=1, source_target_pairs={{0,2},{2,0},{1,3},{3,1},{4,6},{6,4},{5,7},{7,5},{8,10},{10,8},{9,1... | collective-permute-start | bytes 122888 | tf_op jit(solution)/shard_map/ppermute | solution.py:446
  32.9 1.1 %copy-start.7 = (s32[2]{0:T(128)S(1)}, s32[2]{0:T(128)}, u32[]{:S(2)}) copy-start(s32[2]{0:T(128)} %rates.1) | copy-start | bytes 28
  45.0 1.4 %collective-permute-start.12 = (bf16[4,32,512]{2,1,0:T(8,128)(2,1)S(1)}, bf16[4,32,512]{2,1,0:T(8,128)(2,1)S(1)}, u32[]{:S(2)}, u32[]{:S(2)}) collective-permute-start(bf16[4,32,512]{2,1,0:T(8,128)(2,1)S(1)} %get-tuple-element.22), channel_id=1, source_target_pairs={{0,2},{2,0},{1,3},{3,1},{4,6},{6,4},{5,7},{7,5},{8,10},{10,8},{9,1... | collective-permute-start | bytes 393224 | tf_op jit(solution)/shard_map/ppermute | solution.py:446
  45.3 1.6 %collective-permute-start.11 = (f32[128,4,128]{2,1,0:T(4,128)S(1)}, f32[128,4,128]{2,1,0:T(4,128)S(1)}, u32[]{:S(2)}, u32[]{:S(2)}) collective-permute-start(f32[128,4,128]{2,1,0:T(4,128)S(1)} %select_bitcast_fusion), channel_id=1, source_target_pairs={{0,2},{2,0},{1,3},{3,1},{4,6},{6,4},{5,7},{7,5},{8,10},{10,8},{9,1... | collective-permute-start | bytes 786440 | tf_op jit(solution)/shard_map/ppermute | solution.py:446
  46.6 8.5 %collective-permute-start.13 = (bf16[5,32,256]{2,1,0:T(8,128)(2,1)S(1)}, bf16[5,32,256]{2,1,0:T(8,128)(2,1)S(1)}, u32[]{:S(2)}, u32[]{:S(2)}) collective-permute-start(bf16[5,32,256]{2,1,0:T(8,128)(2,1)S(1)} %select_convert_fusion), channel_id=1, source_target_pairs={{0,1},{1,0},{2,3},{3,2},{4,5},{5,4},{6,7},{7,6},{8,9},{9,8},{10,11... | collective-permute-start | bytes 245768 | tf_op jit(solution)/shard_map/ppermute | solution.py:446
  47.7 21.3 %all-to-all-start = ((f32[128,4,128]{2,1,0:T(4,128)}), f32[128,4,128]{2,1,0:T(4,128)S(1)}, u32[]{:S(2)}, u32[]{:S(2)}) async-start(f32[128,4,128]{2,1,0:T(4,128)} %bitcast_add_fusion), calls=%async_computation | async-start | bytes 524288 | tf_op jit(solution)/shard_map/all_to_all | solution.py:454
  55.1 14.1 %collective-permute-start.15 = (bf16[32,256]{1,0:T(8,128)(2,1)S(1)}, bf16[32,256]{1,0:T(8,128)(2,1)S(1)}, u32[]{:S(2)}, u32[]{:S(2)}) collective-permute-start(bf16[32,256]{1,0:T(8,128)(2,1)S(1)} %get-tuple-element.34), channel_id=1, source_target_pairs={{0,16},{4,20},{8,24},{12,28},{16,32},{20,36},{24,40},{28,44},{32,4... | collective-permute-start | bytes 49160 | tf_op jit(solution)/shard_map/ppermute | solution.py:450
  59.9 9.3 %collective-permute-start.14 = (bf16[32,256]{1,0:T(8,128)(2,1)S(1)}, bf16[32,256]{1,0:T(8,128)(2,1)S(1)}, u32[]{:S(2)}, u32[]{:S(2)}) collective-permute-start(bf16[32,256]{1,0:T(8,128)(2,1)S(1)} %get-tuple-element.35), channel_id=1, source_target_pairs={{0,12},{4,16},{8,20},{12,24},{16,28},{20,32},{24,36},{28,40},{32,4... | collective-permute-start | bytes 49160 | tf_op jit(solution)/shard_map/ppermute | solution.py:450
  69.8 14.6 %all-to-all-start.1 = ((f32[64,4,128]{2,1,0:T(4,128)}), f32[64,4,128]{2,1,0:T(4,128)S(1)}, u32[]{:S(2)}, u32[]{:S(2)}) async-start(f32[64,4,128]{2,1,0:T(4,128)} %broadcast_in_dim.17), calls=%async_computation.1 | async-start | bytes 262144 | tf_op jit(solution)/shard_map/all_to_all | solution.py:454
  74.5 14.1 %collective-permute-start.18 = (bf16[32,256]{1,0:T(8,128)(2,1)S(1)}, bf16[32,256]{1,0:T(8,128)(2,1)S(1)}, u32[]{:S(2)}, u32[]{:S(2)}) collective-permute-start(bf16[32,256]{1,0:T(8,128)(2,1)S(1)} %get-tuple-element.32), channel_id=1, source_target_pairs={{0,8},{4,12},{8,16},{12,20},{16,24},{20,28},{24,32},{28,36},{32,40... | collective-permute-start | bytes 49160 | tf_op jit(solution)/shard_map/ppermute | solution.py:450
  76.4 12.2 %collective-permute-start.17 = (bf16[32,256]{1,0:T(8,128)(2,1)S(1)}, bf16[32,256]{1,0:T(8,128)(2,1)S(1)}, u32[]{:S(2)}, u32[]{:S(2)}) collective-permute-start(bf16[32,256]{1,0:T(8,128)(2,1)S(1)} %get-tuple-element.33), channel_id=1, source_target_pairs={{0,4},{4,8},{8,12},{12,16},{16,20},{20,24},{24,28},{28,32},{32,36}... | collective-permute-start | bytes 49160 | tf_op jit(solution)/shard_map/ppermute | solution.py:450
  84.5 5.0 %collective-permute-start.16 = (f32[64,4,128]{2,1,0:T(4,128)S(1)}, f32[64,4,128]{2,1,0:T(4,128)S(1)}, u32[]{:S(2)}, u32[]{:S(2)}) collective-permute-start(f32[64,4,128]{2,1,0:T(4,128)S(1)} %all-to-all-done.1.own), channel_id=1, source_target_pairs={{0,2},{2,0},{1,3},{3,1},{4,6},{6,4},{5,7},{7,5},{8,10},{10,8},{9,1... | collective-permute-start | bytes 393224 | tf_op jit(solution)/shard_map/ppermute | solution.py:446

commit v5 on v4

--- a/solution.py
+++ b/solution.py
@@ -22,7 +22,7 @@
 LEAD = 32
 PACK = 96
 MARKED = EMB + 128
-SLOTS = 64
+SLOTS = 8
 TILES = 21
 AHEAD = 5
 GENOME = ("yl", "x", "z", "core")
@@ -315,12 +315,10 @@
         row = jnp.concatenate([heads, blank], 1)
         tiles += [row[:, :128], row[:, 128:]]
         for t, tile in enumerate(tiles):
-            at = half * SLOTS + t % TILES * 2
-            w_out[t // TILES, at] = tile[:4]
-            w_out[t // TILES, at + 1] = tile[4:]
+            at, row = half * SLOTS + t % TILES // 3, t % 3 * 8
+            w_out[t // TILES, at, row : row + 8, :] = tile
         for t in range(2):
-            at = half * SLOTS + 2 * TILES
-            w_out[t, at : at + SLOTS - 2 * TILES] = jnp.zeros((SLOTS - 2 * TILES, 4, 128), F32)
+            w_out[t, half * SLOTS + SLOTS - 1] = jnp.zeros((24, 128), F32)
 
 
 VMEM = pl.BlockSpec(memory_space=pltpu.VMEM)
@@ -357,7 +355,7 @@
         out_shape=(
             jax.ShapeDtypeStruct((AHEAD, BLOCK, EMB), F32),
             jax.ShapeDtypeStruct((AHEAD - 1, BLOCK, EMB), BF16),
-            jax.ShapeDtypeStruct((2, 2 * SLOTS, 4, 128), F32),
+            jax.ShapeDtypeStruct((2, 2 * SLOTS, 24, 128), F32),
         ),
         in_specs=[SMEM] * 2 + [VMEM] * (len(args) - 2),
         out_specs=(VMEM, VMEM, VMEM),
@@ -393,24 +391,18 @@
     )(*args)
 
 
-def final_kernel(place, own, other, *refs):
+def final_kernel(place, w, *refs):
     *moved, proj_out, pair_out, head_out, emb_out = refs
     total = moved[0][...]
     for block in moved[1:]:
         total = total + block[...].astype(F32)
     emb_out[...] = total
-    core = place[1]
     chan = place[2]
-    flip = jnp.full((8, 128), core, jnp.int32) == 0
     scale = 1.0 / BINS
 
     def tile(t):
-        at = t % TILES * 2
-        mine = jnp.concatenate([own[at], own[at + 1]], 0)
-        theirs = jnp.concatenate([other[at], other[at + 1]], 0)
-        if t < TILES:
-            return jnp.where(flip, mine, theirs) * scale
-        return jnp.where(flip, theirs, mine) * scale
+        at, row = t // TILES * SLOTS + t % TILES // 3, t % 3 * 8
+        return w[at, row : row + 8, :] * scale
 
     proj = [jnp.concatenate([tile(4 * a + b) for b in range(4)], 1) for a in range(4)]
     proj_out[...] = jnp.concatenate(proj, 0)
@@ -490,13 +482,12 @@
     moved = [blocks[0]]
     moved += [cycle(blocks[n].astype(BF16), CHIPS, chips, n) for n in range(1, AHEAD)]
 
-    w = jnp.where(core == 0, w[0], w[1]) + swap(jnp.where(core == 0, w[1], w[0]), "core")
-    per = SLOTS // chips
-    w = exchange(w.reshape(2 * chips, per * 4, 128), ("chan",) + CHIPS)
+    w = exchange(w.reshape(4 * SLOTS, 24, 128), ("core", "chan", "yl", "x"))
     w = jnp.sum(w, axis=0, keepdims=True)
-    w, *moved[3:] = lax.optimization_barrier((w, *moved[3:]))
-    w = exchange(jnp.broadcast_to(w, (chips, per * 4, 128)), CHIPS).reshape(SLOTS, 4, 128)
-    proj, pair, head, emb = run_final(place, w, swap(w, "core"), *moved)
+    w = exchange(jnp.broadcast_to(w, (sizes["z"], 24, 128)), "z")
+    w = jnp.sum(w, axis=0, keepdims=True)
+    w = exchange(jnp.broadcast_to(w, (2 * SLOTS, 24, 128)), ("core", "yl", "x"))
+    proj, pair, head, emb = run_final(place, w, *moved)
     return emb, proj.T, pair, head
 
 

time: 91.2 us -> 88.4 us (0.969)
  waiting for transfers between devices: 19.9 us -> 15.6 us
  starting transfers between devices: 52.5 us -> 53.7 us
  other arithmetic: 1.19 us -> 0.25 us
    all_to_all x2 -> x3, waiting for transfers between devices: 15.8 us -> 8.38 us  [exchange(): return lax.all_to_all(value, axes, 0, 0, tiled=True)]
    ppermute x10 -> x8, waiting for transfers between devices: 3.08 us -> 6.22 us  [swap(): return lax.ppermute(value, axis, [(0, 1), (1, 0)])]
    all_to_all x2 -> x3, starting transfers between devices: 11.9 us -> 13.8 us  [exchange(): return lax.all_to_all(value, axes, 0, 0, tiled=True)]
    ppermute x10 -> x8, starting transfers between devices: 15.6 us -> 13.9 us  [swap(): return lax.ppermute(value, axis, [(0, 1), (1, 0)])]
    ppermute x8, starting transfers between devices: 22.8 us -> 23.8 us  [cycle(): lax.ppermute(value, axes, [(i, (i + by) % length) for i in range(length)])]
  transfers between devices with their start and end apart: 21 -> 20, of which waited for: 8 -> 6; matrix products, arithmetic and copies ran while one was open for 1% -> 1% of each run, Pallas kernels for 0% -> 0%
where the time goes in v5:
time: 88.4 us; the launch traced here: 87.9 us
  starting transfers between devices  53.7 us (61%)
  waiting for transfers between devices  15.6 us (18%)
  Pallas kernels  13.3 us (15%)
  local copies, waits for them, and re-layouts  4.19 us (5%)
    ppermute x8, starting transfers between devices, cycle(): lax.ppermute(value, axes, [(i, (i + by) % length) for i in range(length)])  23.8 us
    ppermute x8, starting transfers between devices, swap(): return lax.ppermute(value, axis, [(0, 1), (1, 0)])  13.9 us
    all_to_all x3, starting transfers between devices, exchange(): return lax.all_to_all(value, axes, 0, 0, tiled=True)  13.8 us
    pallas_call x1, Pallas kernels, run_kernel(): pl.pallas_call(kernel, out_shape=(jax.ShapeDtypeStruct((AHEAD, BLOCK, EMB...  11.3 us
    all_to_all x3, waiting for transfers between devices, exchange(): return lax.all_to_all(value, axes, 0, 0, tiled=True)  8.38 us
    ppermute x8, waiting for transfers between devices, swap(): return lax.ppermute(value, axis, [(0, 1), (1, 0)])  6.22 us
    unnamed x16, local copies, waits for them, and re-layouts  2.83 us
    ppermute x1, starting transfers between devices, local(): rim = lax.ppermute(rim, ALL, routes)  2.23 us
  transfers between devices with their start and end apart: 20, of which 6 were waited for; matrix products, arithmetic and copies ran while one was open for 1% of the time, Pallas kernels for 0%

profile of v5, /device:TPU:1, one launch (start us, length us, event | category | flops | bytes accessed | tf_op | source)
XLA Modules:
  0.0 87.9 jit_solution(2871723287748032536)
XLA Ops:
  0.7 0.6 copy-done
  1.4 0.8 copy-done.3
  2.2 0.7 copy-done.6
  2.8 0.6 shard_map.111
  3.4 9.7 %collective-permute-start = (bf16[32,768]{1,0:T(8,128)(2,1)S(1)}, bf16[32,768]{1,0:T(8,128)(2,1)S(1)}, u32[]{:S(2)}, u32[]{:S(2)}) collective-permute-start(bf16[32,768]{1,0:T(8,128)(2,1)S(1)} %get-tuple-element.14.refs_0_), channel_id=1, source_target_pairs={{0,252},{4,0},{8,4},{12,8},{16,12},{20,16},{24,20},{28,24},{32,28}... | collective-permute-start | bytes 147464 | tf_op jit(solution)/shard_map/ppermute | solution.py:442
  13.1 1.2 %collective-permute-start.1 = (bf16[32,640]{1,0:T(8,128)(2,1)S(1)}, bf16[32,640]{1,0:T(8,128)(2,1)S(1)}, u32[]{:S(2)}, u32[]{:S(2)}) collective-permute-start(bf16[32,640]{1,0:T(8,128)(2,1)S(1)} %get-tuple-element.15), channel_id=1, source_target_pairs={{0,248},{4,252},{8,0},{12,4},{16,8},{20,12},{24,16},{28,20},{32,24... | collective-permute-start | bytes 122888 | tf_op jit(solution)/shard_map/ppermute | solution.py:442
  14.3 0.8 copy-done.2
  15.2 2.7 %collective-permute-start.10 = (bf16[96,512]{1,0:T(8,128)(2,1)S(1)}, bf16[96,512]{1,0:T(8,128)(2,1)S(1)}, u32[]{:S(2)}, u32[]{:S(2)}) collective-permute-start(bf16[96,512]{1,0:T(8,128)(2,1)S(1)} %shard_map.112.refs_11_), channel_id=1, source_target_pairs={{0,1},{1,0},{2,3},{3,2},{4,5},{5,4},{6,7},{7,6},{8,9},{9,8},{10,11... | collective-permute-start | bytes 294920 | tf_op jit(solution)/shard_map/ppermute | solution.py:438
  17.9 1.5 %collective-permute-start.4 = (bf16[32,768]{1,0:T(8,128)(2,1)S(1)}, bf16[32,768]{1,0:T(8,128)(2,1)S(1)}, u32[]{:S(2)}, u32[]{:S(2)}) collective-permute-start(bf16[32,768]{1,0:T(8,128)(2,1)S(1)} %get-tuple-element.14.refs_0_), channel_id=1, source_target_pairs={{0,2},{2,0},{1,3},{3,1},{4,6},{6,4},{5,7},{7,5},{8,10},{10,8},{9,1... | collective-permute-start | bytes 147464 | tf_op jit(solution)/shard_map/ppermute | solution.py:438
  19.4 3.7 %collective-permute-start.3 = (bf16[32,640]{1,0:T(8,128)(2,1)S(1)}, bf16[32,640]{1,0:T(8,128)(2,1)S(1)}, u32[]{:S(2)}, u32[]{:S(2)}) collective-permute-start(bf16[32,640]{1,0:T(8,128)(2,1)S(1)} %collective-permute-done.1.refs_2_), channel_id=1, source_target_pairs={{0,248},{4,252},{8,0},{12,4},{16,8},{20,12},{24,16},{28,20},{32,24... | collective-permute-start | bytes 122888 | tf_op jit(solution)/shard_map/ppermute | solution.py:442
  23.1 2.2 %collective-permute-start.9 = (bf16[16,896]{1,0:T(8,128)(2,1)S(1)}, bf16[16,896]{1,0:T(8,128)(2,1)S(1)}, u32[]{:S(2)}, u32[]{:S(2)}) collective-permute-start(bf16[16,896]{1,0:T(8,128)(2,1)S(1)} %get-tuple-element.16), channel_id=1, source_target_pairs={{2,4},{1,239},{0,2},{3,1},{6,8},{5,243},{4,6},{7,5},{10,12},{9,247... | collective-permute-start | bytes 86024 | tf_op jit(solution)/shard_map/ppermute | solution.py:468
  25.4 1.0 %collective-permute-done.9.refs_10_ = bf16[16,896]{1,0:T(8,128)(2,1)S(1)} collective-permute-done((bf16[16,896]{1,0:T(8,128)(2,1)S(1)}, bf16[16,896]{1,0:T(8,128)(2,1)S(1)}, u32[]{:S(2)}, u32[]{:S(2)}) %collective-permute-start.9) | collective-permute-done | bytes 28704 | tf_op jit(solution)/shard_map/ppermute | solution.py:468
  26.4 5.9 %collective-permute-start.5 = (bf16[32,768]{1,0:T(8,128)(2,1)S(1)}, bf16[32,768]{1,0:T(8,128)(2,1)S(1)}, u32[]{:S(2)}, u32[]{:S(2)}) collective-permute-start(bf16[32,768]{1,0:T(8,128)(2,1)S(1)} %collective-permute-done.refs_1_), channel_id=1, source_target_pairs={{0,2},{2,0},{1,3},{3,1},{4,6},{6,4},{5,7},{7,5},{8,10},{10,8},{9,1... | collective-permute-start | bytes 147464 | tf_op jit(solution)/shard_map/ppermute | solution.py:438
  32.3 0.5 collective-permute-start.6
  32.9 0.8 collective-permute-done.6.refs_7_
  33.7 0.3 collective-permute-done.8.refs_9_
  34.0 11.3 %shard_map.113 = (f32[5,32,512]{2,1,0:T(8,128)S(1)}, bf16[4,32,512]{2,1,0:T(8,128)(2,1)S(1)}, f32[2,16,24,128]{3,2,1,0:T(8,128)}) custom-call(s32[2]{0:T(128)S(1)} %copy-done.7, s32[3]{0:T(128)S(1)} %pad_add_fusion.place, bf16[32,768]{1,0:T(8,128)(2,1)S(1)} %get-tuple-element.14.refs_0_, bf16[32,768]{1,0:T(8,128)(2,1)S(1)} %collective-permute-done.refs_1_, ...), custom_call_target="tpu_custom_call" | custom-call | tf_op jit(solution)/shard_map/pallas_call | solution.py:353
  45.3 0.2 collective-permute-start.11
  45.5 4.0 %all-to-all-start = ((f32[32,24,128]{2,1,0:T(8,128)}), f32[32,24,128]{2,1,0:T(8,128)S(1)}, u32[]{:S(2)}, u32[]{:S(2)}) async-start(f32[32,24,128]{2,1,0:T(8,128)} %bitcast.5), calls=%async_computation | async-start | bytes 786432 | tf_op jit(solution)/shard_map/all_to_all | solution.py:446
  49.6 3.0 %collective-permute-start.12 = (bf16[5,32,256]{2,1,0:T(8,128)(2,1)S(1)}, bf16[5,32,256]{2,1,0:T(8,128)(2,1)S(1)}, u32[]{:S(2)}, u32[]{:S(2)}) collective-permute-start(bf16[5,32,256]{2,1,0:T(8,128)(2,1)S(1)} %select_convert_fusion), channel_id=1, source_target_pairs={{0,1},{1,0},{2,3},{3,2},{4,5},{5,4},{6,7},{7,6},{8,9},{9,8},{10,11... | collective-permute-start | bytes 245768 | tf_op jit(solution)/shard_map/ppermute | solution.py:438
  52.6 5.1 %collective-permute-done.12 = bf16[5,32,256]{2,1,0:T(8,128)(2,1)S(1)} collective-permute-done((bf16[5,32,256]{2,1,0:T(8,128)(2,1)S(1)}, bf16[5,32,256]{2,1,0:T(8,128)(2,1)S(1)}, u32[]{:S(2)}, u32[]{:S(2)}) %collective-permute-start.12) | collective-permute-done | bytes 81952 | tf_op jit(solution)/shard_map/ppermute | solution.py:438
  57.7 1.4 %all-to-all-done = f32[32,24,128]{2,1,0:T(8,128)S(1)} async-done(((f32[32,24,128]{2,1,0:T(8,128)}), f32[32,24,128]{2,1,0:T(8,128)S(1)}, u32[]{:S(2)}, u32[]{:S(2)}) %all-to-all-start) | async-done | bytes 393248 | tf_op jit(solution)/shard_map/all_to_all | solution.py:446
  59.2 0.6 broadcast_in_dim.7
  59.8 3.4 %all-to-all-start.1 = ((f32[8,24,128]{2,1,0:T(8,128)}), f32[8,24,128]{2,1,0:T(8,128)S(1)}, u32[]{:S(2)}, u32[]{:S(2)}) async-start(f32[8,24,128]{2,1,0:T(8,128)} %broadcast_in_dim.7), calls=%async_computation.1 | async-start | bytes 196608 | tf_op jit(solution)/shard_map/all_to_all | solution.py:446
  63.2 5.4 %collective-permute-start.16 = (bf16[32,256]{1,0:T(8,128)(2,1)S(1)}, bf16[32,256]{1,0:T(8,128)(2,1)S(1)}, u32[]{:S(2)}, u32[]{:S(2)}) collective-permute-start(bf16[32,256]{1,0:T(8,128)(2,1)S(1)} %get-tuple-element.26), channel_id=1, source_target_pairs={{0,16},{4,20},{8,24},{12,28},{16,32},{20,36},{24,40},{28,44},{32,4... | collective-permute-start | bytes 49160 | tf_op jit(solution)/shard_map/ppermute | solution.py:442
  68.5 0.3 collective-permute-start.15
  68.9 2.3 %collective-permute-start.14 = (bf16[32,256]{1,0:T(8,128)(2,1)S(1)}, bf16[32,256]{1,0:T(8,128)(2,1)S(1)}, u32[]{:S(2)}, u32[]{:S(2)}) collective-permute-start(bf16[32,256]{1,0:T(8,128)(2,1)S(1)} %get-tuple-element.28), channel_id=1, source_target_pairs={{0,8},{4,12},{8,16},{12,20},{16,24},{20,28},{24,32},{28,36},{32,40... | collective-permute-start | bytes 49160 | tf_op jit(solution)/shard_map/ppermute | solution.py:442
  71.2 1.2 %collective-permute-start.13 = (bf16[32,256]{1,0:T(8,128)(2,1)S(1)}, bf16[32,256]{1,0:T(8,128)(2,1)S(1)}, u32[]{:S(2)}, u32[]{:S(2)}) collective-permute-start(bf16[32,256]{1,0:T(8,128)(2,1)S(1)} %get-tuple-element.29), channel_id=1, source_target_pairs={{0,4},{4,8},{8,12},{12,16},{16,20},{20,24},{24,28},{28,32},{32,36}... | collective-permute-start | bytes 49160 | tf_op jit(solution)/shard_map/ppermute | solution.py:442
  72.4 0.7 broadcast_in_dim.8
  73.1 6.4 %all-to-all-start.2 = ((f32[16,24,128]{2,1,0:T(8,128)}), f32[16,24,128]{2,1,0:T(8,128)S(1)}, u32[]{:S(2)}, u32[]{:S(2)}) async-start(f32[16,24,128]{2,1,0:T(8,128)} %broadcast_in_dim.8), calls=%async_computation.2 | async-start | bytes 393216 | tf_op jit(solution)/shard_map/all_to_all | solution.py:446
  79.6 7.0 %all-to-all-done.2.w = f32[16,24,128]{2,1,0:T(8,128)S(1)} async-done(((f32[16,24,128]{2,1,0:T(8,128)}), f32[16,24,128]{2,1,0:T(8,128)S(1)}, u32[]{:S(2)}, u32[]{:S(2)}) %all-to-all-start.2) | async-done | bytes 196640 | tf_op jit(solution)/shard_map/all_to_all | solution.py:446
  86.6 1.3 %shard_map.114 = (f32[32,512]{1,0:T(8,128)}, f32[9,32,64]{2,1,0:T(8,128)}, f32[9,32]{1,0:T(8,128)}, f32[32,256]{1,0:T(8,128)}) custom-call(s32[3]{0:T(128)S(1)} %pad_add_fusion.place, f32[16,24,128]{2,1,0:T(8,128)S(1)} %all-to-all-done.2.w, f32[32,256]{1,0:T(8,128)S(1)} %slice_bitcast_fusion.refs_0_, bf16[32,256]{1,0:T(8,128)(2,1)S(1)} %collective-permute-done.13.refs_1_, ...), custom_call_target="tpu_custom_call" | custom-call | tf_op jit(solution)/shard_map/pallas_call | solution.py:423
  (39 shorter events, 0.5 us)
Async XLA Ops:
  0.6 0.8 copy-start
  0.6 13.7 %copy-start.1 = (bf16[9,32,64]{2,1,0:T(8,128)(2,1)S(1)}, bf16[9,32,64]{2,1,0:T(8,128)(2,1)}, u32[]{:S(2)}) copy-start(bf16[9,32,64]{2,1,0:T(8,128)(2,1)} %pair.1) | copy-start | bytes 110596
  1.4 0.8 copy-start.3
  2.1 0.7 copy-start.6
  2.8 11.5 %copy-start.4 = (bf16[32,256]{1,0:T(8,128)(2,1)S(1)}, bf16[32,256]{1,0:T(8,128)(2,1)}, u32[]{:S(2)}) copy-start(bf16[32,256]{1,0:T(8,128)(2,1)} %bias.1) | copy-start | bytes 49156
  3.4 10.9 %copy-start.5 = (bf16[9,32]{1,0:T(8,128)(2,1)S(1)}, bf16[9,32]{1,0:T(8,128)(2,1)}, u32[]{:S(2)}) copy-start(bf16[9,32]{1,0:T(8,128)(2,1)} %head.1) | copy-start | bytes 1732
  3.4 14.4 %collective-permute-start = (bf16[32,768]{1,0:T(8,128)(2,1)S(1)}, bf16[32,768]{1,0:T(8,128)(2,1)S(1)}, u32[]{:S(2)}, u32[]{:S(2)}) collective-permute-start(bf16[32,768]{1,0:T(8,128)(2,1)S(1)} %get-tuple-element.14.refs_0_), channel_id=1, source_target_pairs={{0,252},{4,0},{8,4},{12,8},{16,12},{20,16},{24,20},{28,24},{32,28}... | collective-permute-start | bytes 147464 | tf_op jit(solution)/shard_map/ppermute | solution.py:442
  13.1 6.3 %collective-permute-start.1 = (bf16[32,640]{1,0:T(8,128)(2,1)S(1)}, bf16[32,640]{1,0:T(8,128)(2,1)S(1)}, u32[]{:S(2)}, u32[]{:S(2)}) collective-permute-start(bf16[32,640]{1,0:T(8,128)(2,1)S(1)} %get-tuple-element.15), channel_id=1, source_target_pairs={{0,248},{4,252},{8,0},{12,4},{16,8},{20,12},{24,16},{28,20},{32,24... | collective-permute-start | bytes 122888 | tf_op jit(solution)/shard_map/ppermute | solution.py:442
  14.3 0.8 copy-start.2
  15.2 18.9 %copy-start.7 = (s32[2]{0:T(128)S(1)}, s32[2]{0:T(128)}, u32[]{:S(2)}) copy-start(s32[2]{0:T(128)} %rates.1) | copy-start | bytes 28
  15.2 18.5 %collective-permute-start.10 = (bf16[96,512]{1,0:T(8,128)(2,1)S(1)}, bf16[96,512]{1,0:T(8,128)(2,1)S(1)}, u32[]{:S(2)}, u32[]{:S(2)}) collective-permute-start(bf16[96,512]{1,0:T(8,128)(2,1)S(1)} %shard_map.112.refs_11_), channel_id=1, source_target_pairs={{0,1},{1,0},{2,3},{3,2},{4,5},{5,4},{6,7},{7,6},{8,9},{9,8},{10,11... | collective-permute-start | bytes 294920 | tf_op jit(solution)/shard_map/ppermute | solution.py:438
  17.9 14.4 %collective-permute-start.2 = (bf16[32,768]{1,0:T(8,128)(2,1)S(1)}, bf16[32,768]{1,0:T(8,128)(2,1)S(1)}, u32[]{:S(2)}, u32[]{:S(2)}) collective-permute-start(bf16[32,768]{1,0:T(8,128)(2,1)S(1)} %collective-permute-done.refs_1_), channel_id=1, source_target_pairs={{0,248},{4,252},{8,0},{12,4},{16,8},{20,12},{24,16},{28,20},{32,24... | collective-permute-start | bytes 147464 | tf_op jit(solution)/shard_map/ppermute | solution.py:442
  17.9 14.4 %collective-permute-start.4 = (bf16[32,768]{1,0:T(8,128)(2,1)S(1)}, bf16[32,768]{1,0:T(8,128)(2,1)S(1)}, u32[]{:S(2)}, u32[]{:S(2)}) collective-permute-start(bf16[32,768]{1,0:T(8,128)(2,1)S(1)} %get-tuple-element.14.refs_0_), channel_id=1, source_target_pairs={{0,2},{2,0},{1,3},{3,1},{4,6},{6,4},{5,7},{7,5},{8,10},{10,8},{9,1... | collective-permute-start | bytes 147464 | tf_op jit(solution)/shard_map/ppermute | solution.py:438
  19.4 13.4 %collective-permute-start.3 = (bf16[32,640]{1,0:T(8,128)(2,1)S(1)}, bf16[32,640]{1,0:T(8,128)(2,1)S(1)}, u32[]{:S(2)}, u32[]{:S(2)}) collective-permute-start(bf16[32,640]{1,0:T(8,128)(2,1)S(1)} %collective-permute-done.1.refs_2_), channel_id=1, source_target_pairs={{0,248},{4,252},{8,0},{12,4},{16,8},{20,12},{24,16},{28,20},{32,24... | collective-permute-start | bytes 122888 | tf_op jit(solution)/shard_map/ppermute | solution.py:442
  23.1 3.2 %collective-permute-start.9 = (bf16[16,896]{1,0:T(8,128)(2,1)S(1)}, bf16[16,896]{1,0:T(8,128)(2,1)S(1)}, u32[]{:S(2)}, u32[]{:S(2)}) collective-permute-start(bf16[16,896]{1,0:T(8,128)(2,1)S(1)} %get-tuple-element.16), channel_id=1, source_target_pairs={{2,4},{1,239},{0,2},{3,1},{6,8},{5,243},{4,6},{7,5},{10,12},{9,247... | collective-permute-start | bytes 86024 | tf_op jit(solution)/shard_map/ppermute | solution.py:468
  26.4 7.3 %collective-permute-start.5 = (bf16[32,768]{1,0:T(8,128)(2,1)S(1)}, bf16[32,768]{1,0:T(8,128)(2,1)S(1)}, u32[]{:S(2)}, u32[]{:S(2)}) collective-permute-start(bf16[32,768]{1,0:T(8,128)(2,1)S(1)} %collective-permute-done.refs_1_), channel_id=1, source_target_pairs={{0,2},{2,0},{1,3},{3,1},{4,6},{6,4},{5,7},{7,5},{8,10},{10,8},{9,1... | collective-permute-start | bytes 147464 | tf_op jit(solution)/shard_map/ppermute | solution.py:438
  32.3 1.7 %collective-permute-start.7 = (bf16[32,768]{1,0:T(8,128)(2,1)S(1)}, bf16[32,768]{1,0:T(8,128)(2,1)S(1)}, u32[]{:S(2)}, u32[]{:S(2)}) collective-permute-start(bf16[32,768]{1,0:T(8,128)(2,1)S(1)} %collective-permute-done.2.refs_3_), channel_id=1, source_target_pairs={{0,2},{2,0},{1,3},{3,1},{4,6},{6,4},{5,7},{7,5},{8,10},{10,8},{9,1... | collective-permute-start | bytes 147464 | tf_op jit(solution)/shard_map/ppermute | solution.py:438
  32.3 1.4 %collective-permute-start.6 = (bf16[32,640]{1,0:T(8,128)(2,1)S(1)}, bf16[32,640]{1,0:T(8,128)(2,1)S(1)}, u32[]{:S(2)}, u32[]{:S(2)}) collective-permute-start(bf16[32,640]{1,0:T(8,128)(2,1)S(1)} %collective-permute-done.1.refs_2_), channel_id=1, source_target_pairs={{0,2},{2,0},{1,3},{3,1},{4,6},{6,4},{5,7},{7,5},{8,10},{10,8},{9,1... | collective-permute-start | bytes 122888 | tf_op jit(solution)/shard_map/ppermute | solution.py:438
  32.8 1.2 %collective-permute-start.8 = (bf16[32,640]{1,0:T(8,128)(2,1)S(1)}, bf16[32,640]{1,0:T(8,128)(2,1)S(1)}, u32[]{:S(2)}, u32[]{:S(2)}) collective-permute-start(bf16[32,640]{1,0:T(8,128)(2,1)S(1)} %collective-permute-done.3.refs_4_), channel_id=1, source_target_pairs={{0,2},{2,0},{1,3},{3,1},{4,6},{6,4},{5,7},{7,5},{8,10},{10,8},{9,1... | collective-permute-start | bytes 122888 | tf_op jit(solution)/shard_map/ppermute | solution.py:438
  45.3 4.2 %collective-permute-start.11 = (bf16[4,32,512]{2,1,0:T(8,128)(2,1)S(1)}, bf16[4,32,512]{2,1,0:T(8,128)(2,1)S(1)}, u32[]{:S(2)}, u32[]{:S(2)}) collective-permute-start(bf16[4,32,512]{2,1,0:T(8,128)(2,1)S(1)} %get-tuple-element.19), channel_id=1, source_target_pairs={{0,2},{2,0},{1,3},{3,1},{4,6},{6,4},{5,7},{7,5},{8,10},{10,8},{9,1... | collective-permute-start | bytes 393224 | tf_op jit(solution)/shard_map/ppermute | solution.py:438
  45.5 13.6 %all-to-all-start = ((f32[32,24,128]{2,1,0:T(8,128)}), f32[32,24,128]{2,1,0:T(8,128)S(1)}, u32[]{:S(2)}, u32[]{:S(2)}) async-start(f32[32,24,128]{2,1,0:T(8,128)} %bitcast.5), calls=%async_computation | async-start | bytes 786432 | tf_op jit(solution)/shard_map/all_to_all | solution.py:446
  49.6 8.1 %collective-permute-start.12 = (bf16[5,32,256]{2,1,0:T(8,128)(2,1)S(1)}, bf16[5,32,256]{2,1,0:T(8,128)(2,1)S(1)}, u32[]{:S(2)}, u32[]{:S(2)}) collective-permute-start(bf16[5,32,256]{2,1,0:T(8,128)(2,1)S(1)} %select_convert_fusion), channel_id=1, source_target_pairs={{0,1},{1,0},{2,3},{3,2},{4,5},{5,4},{6,7},{7,6},{8,9},{9,8},{10,11... | collective-permute-start | bytes 245768 | tf_op jit(solution)/shard_map/ppermute | solution.py:438
  59.8 12.5 %all-to-all-start.1 = ((f32[8,24,128]{2,1,0:T(8,128)}), f32[8,24,128]{2,1,0:T(8,128)S(1)}, u32[]{:S(2)}, u32[]{:S(2)}) async-start(f32[8,24,128]{2,1,0:T(8,128)} %broadcast_in_dim.7), calls=%async_computation.1 | async-start | bytes 196608 | tf_op jit(solution)/shard_map/all_to_all | solution.py:446
  63.2 16.3 %collective-permute-start.16 = (bf16[32,256]{1,0:T(8,128)(2,1)S(1)}, bf16[32,256]{1,0:T(8,128)(2,1)S(1)}, u32[]{:S(2)}, u32[]{:S(2)}) collective-permute-start(bf16[32,256]{1,0:T(8,128)(2,1)S(1)} %get-tuple-element.26), channel_id=1, source_target_pairs={{0,16},{4,20},{8,24},{12,28},{16,32},{20,36},{24,40},{28,44},{32,4... | collective-permute-start | bytes 49160 | tf_op jit(solution)/shard_map/ppermute | solution.py:442
  68.5 11.0 %collective-permute-start.15 = (bf16[32,256]{1,0:T(8,128)(2,1)S(1)}, bf16[32,256]{1,0:T(8,128)(2,1)S(1)}, u32[]{:S(2)}, u32[]{:S(2)}) collective-permute-start(bf16[32,256]{1,0:T(8,128)(2,1)S(1)} %get-tuple-element.27), channel_id=1, source_target_pairs={{0,12},{4,16},{8,20},{12,24},{16,28},{20,32},{24,36},{28,40},{32,4... | collective-permute-start | bytes 49160 | tf_op jit(solution)/shard_map/ppermute | solution.py:442
  68.9 10.7 %collective-permute-start.14 = (bf16[32,256]{1,0:T(8,128)(2,1)S(1)}, bf16[32,256]{1,0:T(8,128)(2,1)S(1)}, u32[]{:S(2)}, u32[]{:S(2)}) collective-permute-start(bf16[32,256]{1,0:T(8,128)(2,1)S(1)} %get-tuple-element.28), channel_id=1, source_target_pairs={{0,8},{4,12},{8,16},{12,20},{16,24},{20,28},{24,32},{28,36},{32,40... | collective-permute-start | bytes 49160 | tf_op jit(solution)/shard_map/ppermute | solution.py:442
  71.2 8.4 %collective-permute-start.13 = (bf16[32,256]{1,0:T(8,128)(2,1)S(1)}, bf16[32,256]{1,0:T(8,128)(2,1)S(1)}, u32[]{:S(2)}, u32[]{:S(2)}) collective-permute-start(bf16[32,256]{1,0:T(8,128)(2,1)S(1)} %get-tuple-element.29), channel_id=1, source_target_pairs={{0,4},{4,8},{8,12},{12,16},{16,20},{20,24},{24,28},{28,32},{32,36}... | collective-permute-start | bytes 49160 | tf_op jit(solution)/shard_map/ppermute | solution.py:442
  73.1 13.5 %all-to-all-start.2 = ((f32[16,24,128]{2,1,0:T(8,128)}), f32[16,24,128]{2,1,0:T(8,128)S(1)}, u32[]{:S(2)}, u32[]{:S(2)}) async-start(f32[16,24,128]{2,1,0:T(8,128)} %broadcast_in_dim.8), calls=%async_computation.2 | async-start | bytes 393216 | tf_op jit(solution)/shard_map/all_to_all | solution.py:446

commit v6 on v5

--- a/solution.py
+++ b/solution.py
@@ -461,11 +461,10 @@
     flat = lambda chip, c, h: (chip % chips * 2 + c) * 2 + h
     routes = []
     for i in range(chips):
-        routes.append((flat(i, 1, 0), flat(i + 1, 0, 0)))
-        routes.append((flat(i, 0, 1), flat(i - AHEAD, 1, 1)))
-        routes.append((flat(i, 0, 0), flat(i, 1, 0)))
-        routes.append((flat(i, 1, 1), flat(i, 0, 1)))
-    rim = lax.ppermute(rim, ALL, routes)
+        for c in range(2):
+            routes.append((flat(i, c, 0), flat(i + 1, c, 0)))
+            routes.append((flat(i, c, 1), flat(i - AHEAD, c, 1)))
+    rim = swap(lax.ppermute(rim, ALL, routes), "core")
     sibling = [swap(value, "core") for value in same]
     keep, give, w = run_kernel(
         dilations, place, *same, *sibling, rim, packed, other_pack, target

time: 88.4 us -> 88.1 us (level)
  waiting for transfers between devices: 15.6 us -> 14.6 us
    all_to_all x3, starting transfers between devices: 13.8 us -> 17.3 us  [exchange(): return lax.all_to_all(value, axes, 0, 0, tiled=True)]
    ppermute x8 -> x9, starting transfers between devices: 13.9 us -> 12.2 us  [swap(): return lax.ppermute(value, axis, [(0, 1), (1, 0)])]
    ppermute x1, starting transfers between devices: 2.23 us -> 0.74 us  [local(): rim = swap(lax.ppermute(rim, ALL, routes), 'core')]
    ppermute x1, waiting for transfers between devices: 0.99 us -> 0.01 us  [local(): rim = swap(lax.ppermute(rim, ALL, routes), 'core')]
    ppermute x8 -> x9, waiting for transfers between devices: 6.22 us -> 5.97 us  [swap(): return lax.ppermute(value, axis, [(0, 1), (1, 0)])]
  transfers between devices with their start and end apart: 20 -> 21, of which waited for: 6 -> 5; matrix products, arithmetic and copies ran while one was open for 1% -> 1% of each run, Pallas kernels for 0% -> 0%
where the time goes in v6:
time: 88.1 us; the launch traced here: 87.6 us
  starting transfers between devices  54.4 us (62%)
  waiting for transfers between devices  14.6 us (17%)
  Pallas kernels  13.3 us (15%)
  local copies, waits for them, and re-layouts  4.18 us (5%)
    ppermute x8, starting transfers between devices, cycle(): lax.ppermute(value, axes, [(i, (i + by) % length) for i in range(length)])  24.1 us
    all_to_all x3, starting transfers between devices, exchange(): return lax.all_to_all(value, axes, 0, 0, tiled=True)  17.3 us
    ppermute x9, starting transfers between devices, swap(): return lax.ppermute(value, axis, [(0, 1), (1, 0)])  12.2 us
    pallas_call x1, Pallas kernels, run_kernel(): pl.pallas_call(kernel, out_shape=(jax.ShapeDtypeStruct((AHEAD, BLOCK, EMB...  11.3 us
    all_to_all x3, waiting for transfers between devices, exchange(): return lax.all_to_all(value, axes, 0, 0, tiled=True)  8.38 us
    ppermute x9, waiting for transfers between devices, swap(): return lax.ppermute(value, axis, [(0, 1), (1, 0)])  5.97 us
    unnamed x16, local copies, waits for them, and re-layouts  2.83 us
  transfers between devices with their start and end apart: 21, of which 5 were waited for; matrix products, arithmetic and copies ran while one was open for 1% of the time, Pallas kernels for 0%

profile of v6, /device:TPU:1, one launch (start us, length us, event | category | flops | bytes accessed | tf_op | source)
XLA Modules:
  0.0 87.6 jit_solution(2457420054727961513)
XLA Ops:
  0.7 0.6 copy-done
  1.4 0.8 copy-done.3
  2.2 0.7 copy-done.6
  2.8 0.6 shard_map.111
  3.4 9.7 %collective-permute-start = (bf16[32,768]{1,0:T(8,128)(2,1)S(1)}, bf16[32,768]{1,0:T(8,128)(2,1)S(1)}, u32[]{:S(2)}, u32[]{:S(2)}) collective-permute-start(bf16[32,768]{1,0:T(8,128)(2,1)S(1)} %get-tuple-element.14.refs_0_), channel_id=1, source_target_pairs={{0,252},{4,0},{8,4},{12,8},{16,12},{20,16},{24,20},{28,24},{32,28}... | collective-permute-start | bytes 147464 | tf_op jit(solution)/shard_map/ppermute | solution.py:442
  13.1 1.2 %collective-permute-start.1 = (bf16[32,640]{1,0:T(8,128)(2,1)S(1)}, bf16[32,640]{1,0:T(8,128)(2,1)S(1)}, u32[]{:S(2)}, u32[]{:S(2)}) collective-permute-start(bf16[32,640]{1,0:T(8,128)(2,1)S(1)} %get-tuple-element.15), channel_id=1, source_target_pairs={{0,248},{4,252},{8,0},{12,4},{16,8},{20,12},{24,16},{28,20},{32,24... | collective-permute-start | bytes 122888 | tf_op jit(solution)/shard_map/ppermute | solution.py:442
  14.3 1.2 %collective-permute-start.4 = (bf16[32,768]{1,0:T(8,128)(2,1)S(1)}, bf16[32,768]{1,0:T(8,128)(2,1)S(1)}, u32[]{:S(2)}, u32[]{:S(2)}) collective-permute-start(bf16[32,768]{1,0:T(8,128)(2,1)S(1)} %get-tuple-element.14.refs_0_), channel_id=1, source_target_pairs={{0,2},{2,0},{1,3},{3,1},{4,6},{6,4},{5,7},{7,5},{8,10},{10,8},{9,1... | collective-permute-start | bytes 147464 | tf_op jit(solution)/shard_map/ppermute | solution.py:438
  15.5 0.7 collective-permute-start.9
  16.3 0.8 copy-done.2
  17.1 2.0 %collective-permute-start.11 = (bf16[96,512]{1,0:T(8,128)(2,1)S(1)}, bf16[96,512]{1,0:T(8,128)(2,1)S(1)}, u32[]{:S(2)}, u32[]{:S(2)}) collective-permute-start(bf16[96,512]{1,0:T(8,128)(2,1)S(1)} %shard_map.112.refs_11_), channel_id=1, source_target_pairs={{0,1},{1,0},{2,3},{3,2},{4,5},{5,4},{6,7},{7,6},{8,9},{9,8},{10,11... | collective-permute-start | bytes 294920 | tf_op jit(solution)/shard_map/ppermute | solution.py:438
  19.1 3.7 %collective-permute-start.2 = (bf16[32,768]{1,0:T(8,128)(2,1)S(1)}, bf16[32,768]{1,0:T(8,128)(2,1)S(1)}, u32[]{:S(2)}, u32[]{:S(2)}) collective-permute-start(bf16[32,768]{1,0:T(8,128)(2,1)S(1)} %collective-permute-done.refs_1_), channel_id=1, source_target_pairs={{0,248},{4,252},{8,0},{12,4},{16,8},{20,12},{24,16},{28,20},{32,24... | collective-permute-start | bytes 147464 | tf_op jit(solution)/shard_map/ppermute | solution.py:442
  22.8 0.3 collective-permute-start.3
  23.1 1.5 %collective-permute-start.10 = (bf16[16,896]{1,0:T(8,128)(2,1)S(1)}, bf16[16,896]{1,0:T(8,128)(2,1)S(1)}, u32[]{:S(2)}, u32[]{:S(2)}) collective-permute-start(bf16[16,896]{1,0:T(8,128)(2,1)S(1)} %collective-permute-done.9), channel_id=1, source_target_pairs={{0,2},{2,0},{1,3},{3,1},{4,6},{6,4},{5,7},{7,5},{8,10},{10,8},{9,1... | collective-permute-start | bytes 86024 | tf_op jit(solution)/shard_map/ppermute | solution.py:438
  24.8 1.6 %collective-permute-start.7 = (bf16[32,768]{1,0:T(8,128)(2,1)S(1)}, bf16[32,768]{1,0:T(8,128)(2,1)S(1)}, u32[]{:S(2)}, u32[]{:S(2)}) collective-permute-start(bf16[32,768]{1,0:T(8,128)(2,1)S(1)} %collective-permute-done.2.refs_3_), channel_id=1, source_target_pairs={{0,2},{2,0},{1,3},{3,1},{4,6},{6,4},{5,7},{7,5},{8,10},{10,8},{9,1... | collective-permute-start | bytes 147464 | tf_op jit(solution)/shard_map/ppermute | solution.py:438
  26.7 2.5 %collective-permute-start.8 = (bf16[32,640]{1,0:T(8,128)(2,1)S(1)}, bf16[32,640]{1,0:T(8,128)(2,1)S(1)}, u32[]{:S(2)}, u32[]{:S(2)}) collective-permute-start(bf16[32,640]{1,0:T(8,128)(2,1)S(1)} %collective-permute-done.3.refs_4_), channel_id=1, source_target_pairs={{0,2},{2,0},{1,3},{3,1},{4,6},{6,4},{5,7},{7,5},{8,10},{10,8},{9,1... | collective-permute-start | bytes 122888 | tf_op jit(solution)/shard_map/ppermute | solution.py:438
  29.1 0.9 collective-permute-done.8.refs_9_
  30.0 11.3 %shard_map.113 = (f32[5,32,512]{2,1,0:T(8,128)S(1)}, bf16[4,32,512]{2,1,0:T(8,128)(2,1)S(1)}, f32[2,16,24,128]{3,2,1,0:T(8,128)}) custom-call(s32[2]{0:T(128)S(1)} %copy-done.7, s32[3]{0:T(128)S(1)} %pad_add_fusion.place, bf16[32,768]{1,0:T(8,128)(2,1)S(1)} %get-tuple-element.14.refs_0_, bf16[32,768]{1,0:T(8,128)(2,1)S(1)} %collective-permute-done.refs_1_, ...), custom_call_target="tpu_custom_call" | custom-call | tf_op jit(solution)/shard_map/pallas_call | solution.py:353
  41.3 0.4 collective-permute-start.12
  41.6 3.8 %all-to-all-start = ((f32[32,24,128]{2,1,0:T(8,128)}), f32[32,24,128]{2,1,0:T(8,128)S(1)}, u32[]{:S(2)}, u32[]{:S(2)}) async-start(f32[32,24,128]{2,1,0:T(8,128)} %bitcast.5), calls=%async_computation | async-start | bytes 786432 | tf_op jit(solution)/shard_map/all_to_all | solution.py:446
  45.6 3.0 %collective-permute-start.13 = (bf16[5,32,256]{2,1,0:T(8,128)(2,1)S(1)}, bf16[5,32,256]{2,1,0:T(8,128)(2,1)S(1)}, u32[]{:S(2)}, u32[]{:S(2)}) collective-permute-start(bf16[5,32,256]{2,1,0:T(8,128)(2,1)S(1)} %select_convert_fusion), channel_id=1, source_target_pairs={{0,1},{1,0},{2,3},{3,2},{4,5},{5,4},{6,7},{7,6},{8,9},{9,8},{10,11... | collective-permute-start | bytes 245768 | tf_op jit(solution)/shard_map/ppermute | solution.py:438
  48.6 5.1 %collective-permute-done.13 = bf16[5,32,256]{2,1,0:T(8,128)(2,1)S(1)} collective-permute-done((bf16[5,32,256]{2,1,0:T(8,128)(2,1)S(1)}, bf16[5,32,256]{2,1,0:T(8,128)(2,1)S(1)}, u32[]{:S(2)}, u32[]{:S(2)}) %collective-permute-start.13) | collective-permute-done | bytes 81952 | tf_op jit(solution)/shard_map/ppermute | solution.py:438
  53.7 1.4 %all-to-all-done = f32[32,24,128]{2,1,0:T(8,128)S(1)} async-done(((f32[32,24,128]{2,1,0:T(8,128)}), f32[32,24,128]{2,1,0:T(8,128)S(1)}, u32[]{:S(2)}, u32[]{:S(2)}) %all-to-all-start) | async-done | bytes 393248 | tf_op jit(solution)/shard_map/all_to_all | solution.py:446
  55.1 0.6 broadcast_in_dim.7
  55.8 6.9 %all-to-all-start.1 = ((f32[8,24,128]{2,1,0:T(8,128)}), f32[8,24,128]{2,1,0:T(8,128)S(1)}, u32[]{:S(2)}, u32[]{:S(2)}) async-start(f32[8,24,128]{2,1,0:T(8,128)} %broadcast_in_dim.7), calls=%async_computation.1 | async-start | bytes 196608 | tf_op jit(solution)/shard_map/all_to_all | solution.py:446
  62.7 5.4 %collective-permute-start.17 = (bf16[32,256]{1,0:T(8,128)(2,1)S(1)}, bf16[32,256]{1,0:T(8,128)(2,1)S(1)}, u32[]{:S(2)}, u32[]{:S(2)}) collective-permute-start(bf16[32,256]{1,0:T(8,128)(2,1)S(1)} %get-tuple-element.26), channel_id=1, source_target_pairs={{0,16},{4,20},{8,24},{12,28},{16,32},{20,36},{24,40},{28,44},{32,4... | collective-permute-start | bytes 49160 | tf_op jit(solution)/shard_map/ppermute | solution.py:442
  68.1 0.3 collective-permute-start.16
  68.4 2.3 %collective-permute-start.15 = (bf16[32,256]{1,0:T(8,128)(2,1)S(1)}, bf16[32,256]{1,0:T(8,128)(2,1)S(1)}, u32[]{:S(2)}, u32[]{:S(2)}) collective-permute-start(bf16[32,256]{1,0:T(8,128)(2,1)S(1)} %get-tuple-element.28), channel_id=1, source_target_pairs={{0,8},{4,12},{8,16},{12,20},{16,24},{20,28},{24,32},{28,36},{32,40... | collective-permute-start | bytes 49160 | tf_op jit(solution)/shard_map/ppermute | solution.py:442
  70.7 1.2 %collective-permute-start.14 = (bf16[32,256]{1,0:T(8,128)(2,1)S(1)}, bf16[32,256]{1,0:T(8,128)(2,1)S(1)}, u32[]{:S(2)}, u32[]{:S(2)}) collective-permute-start(bf16[32,256]{1,0:T(8,128)(2,1)S(1)} %get-tuple-element.29), channel_id=1, source_target_pairs={{0,4},{4,8},{8,12},{12,16},{16,20},{20,24},{24,28},{28,32},{32,36}... | collective-permute-start | bytes 49160 | tf_op jit(solution)/shard_map/ppermute | solution.py:442
  71.9 0.7 broadcast_in_dim.8
  72.6 6.6 %all-to-all-start.2 = ((f32[16,24,128]{2,1,0:T(8,128)}), f32[16,24,128]{2,1,0:T(8,128)S(1)}, u32[]{:S(2)}, u32[]{:S(2)}) async-start(f32[16,24,128]{2,1,0:T(8,128)} %broadcast_in_dim.8), calls=%async_computation.2 | async-start | bytes 393216 | tf_op jit(solution)/shard_map/all_to_all | solution.py:446
  79.3 7.0 %all-to-all-done.2.w = f32[16,24,128]{2,1,0:T(8,128)S(1)} async-done(((f32[16,24,128]{2,1,0:T(8,128)}), f32[16,24,128]{2,1,0:T(8,128)S(1)}, u32[]{:S(2)}, u32[]{:S(2)}) %all-to-all-start.2) | async-done | bytes 196640 | tf_op jit(solution)/shard_map/all_to_all | solution.py:446
  86.3 1.3 %shard_map.114 = (f32[32,512]{1,0:T(8,128)}, f32[9,32,64]{2,1,0:T(8,128)}, f32[9,32]{1,0:T(8,128)}, f32[32,256]{1,0:T(8,128)}) custom-call(s32[3]{0:T(128)S(1)} %pad_add_fusion.place, f32[16,24,128]{2,1,0:T(8,128)S(1)} %all-to-all-done.2.w, f32[32,256]{1,0:T(8,128)S(1)} %slice_bitcast_fusion.refs_0_, bf16[32,256]{1,0:T(8,128)(2,1)S(1)} %collective-permute-done.14.refs_1_, ...), custom_call_target="tpu_custom_call" | custom-call | tf_op jit(solution)/shard_map/pallas_call | solution.py:423
  (41 shorter events, 0.8 us)
Async XLA Ops:
  0.6 0.8 copy-start
  0.6 15.6 %copy-start.1 = (bf16[9,32,64]{2,1,0:T(8,128)(2,1)S(1)}, bf16[9,32,64]{2,1,0:T(8,128)(2,1)}, u32[]{:S(2)}) copy-start(bf16[9,32,64]{2,1,0:T(8,128)(2,1)} %pair.1) | copy-start | bytes 110596
  1.4 0.8 copy-start.3
  2.1 0.7 copy-start.6
  2.8 13.5 %copy-start.4 = (bf16[32,256]{1,0:T(8,128)(2,1)S(1)}, bf16[32,256]{1,0:T(8,128)(2,1)}, u32[]{:S(2)}) copy-start(bf16[32,256]{1,0:T(8,128)(2,1)} %bias.1) | copy-start | bytes 49156
  3.4 12.8 %copy-start.5 = (bf16[9,32]{1,0:T(8,128)(2,1)S(1)}, bf16[9,32]{1,0:T(8,128)(2,1)}, u32[]{:S(2)}) copy-start(bf16[9,32]{1,0:T(8,128)(2,1)} %head.1) | copy-start | bytes 1732
  3.4 15.7 %collective-permute-start = (bf16[32,768]{1,0:T(8,128)(2,1)S(1)}, bf16[32,768]{1,0:T(8,128)(2,1)S(1)}, u32[]{:S(2)}, u32[]{:S(2)}) collective-permute-start(bf16[32,768]{1,0:T(8,128)(2,1)S(1)} %get-tuple-element.14.refs_0_), channel_id=1, source_target_pairs={{0,252},{4,0},{8,4},{12,8},{16,12},{20,16},{24,20},{28,24},{32,28}... | collective-permute-start | bytes 147464 | tf_op jit(solution)/shard_map/ppermute | solution.py:442
  13.1 9.7 %collective-permute-start.1 = (bf16[32,640]{1,0:T(8,128)(2,1)S(1)}, bf16[32,640]{1,0:T(8,128)(2,1)S(1)}, u32[]{:S(2)}, u32[]{:S(2)}) collective-permute-start(bf16[32,640]{1,0:T(8,128)(2,1)S(1)} %get-tuple-element.15), channel_id=1, source_target_pairs={{0,248},{4,252},{8,0},{12,4},{16,8},{20,12},{24,16},{28,20},{32,24... | collective-permute-start | bytes 122888 | tf_op jit(solution)/shard_map/ppermute | solution.py:442
  14.3 10.4 %collective-permute-start.4 = (bf16[32,768]{1,0:T(8,128)(2,1)S(1)}, bf16[32,768]{1,0:T(8,128)(2,1)S(1)}, u32[]{:S(2)}, u32[]{:S(2)}) collective-permute-start(bf16[32,768]{1,0:T(8,128)(2,1)S(1)} %get-tuple-element.14.refs_0_), channel_id=1, source_target_pairs={{0,2},{2,0},{1,3},{3,1},{4,6},{6,4},{5,7},{7,5},{8,10},{10,8},{9,1... | collective-permute-start | bytes 147464 | tf_op jit(solution)/shard_map/ppermute | solution.py:438
  15.5 7.6 %collective-permute-start.9 = (bf16[16,896]{1,0:T(8,128)(2,1)S(1)}, bf16[16,896]{1,0:T(8,128)(2,1)S(1)}, u32[]{:S(2)}, u32[]{:S(2)}) collective-permute-start(bf16[16,896]{1,0:T(8,128)(2,1)S(1)} %get-tuple-element.16), channel_id=1, source_target_pairs={{0,4},{1,237},{2,6},{3,239},{4,8},{5,241},{6,10},{7,243},{8,12},{9... | collective-permute-start | bytes 86024 | tf_op jit(solution)/shard_map/ppermute | solution.py:467
  16.3 0.8 copy-start.2
  17.0 12.9 %copy-start.7 = (s32[2]{0:T(128)S(1)}, s32[2]{0:T(128)}, u32[]{:S(2)}) copy-start(s32[2]{0:T(128)} %rates.1) | copy-start | bytes 28
  17.1 12.0 %collective-permute-start.11 = (bf16[96,512]{1,0:T(8,128)(2,1)S(1)}, bf16[96,512]{1,0:T(8,128)(2,1)S(1)}, u32[]{:S(2)}, u32[]{:S(2)}) collective-permute-start(bf16[96,512]{1,0:T(8,128)(2,1)S(1)} %shard_map.112.refs_11_), channel_id=1, source_target_pairs={{0,1},{1,0},{2,3},{3,2},{4,5},{5,4},{6,7},{7,6},{8,9},{9,8},{10,11... | collective-permute-start | bytes 294920 | tf_op jit(solution)/shard_map/ppermute | solution.py:438
  19.1 5.6 %collective-permute-start.2 = (bf16[32,768]{1,0:T(8,128)(2,1)S(1)}, bf16[32,768]{1,0:T(8,128)(2,1)S(1)}, u32[]{:S(2)}, u32[]{:S(2)}) collective-permute-start(bf16[32,768]{1,0:T(8,128)(2,1)S(1)} %collective-permute-done.refs_1_), channel_id=1, source_target_pairs={{0,248},{4,252},{8,0},{12,4},{16,8},{20,12},{24,16},{28,20},{32,24... | collective-permute-start | bytes 147464 | tf_op jit(solution)/shard_map/ppermute | solution.py:442
  22.8 3.9 %collective-permute-start.3 = (bf16[32,640]{1,0:T(8,128)(2,1)S(1)}, bf16[32,640]{1,0:T(8,128)(2,1)S(1)}, u32[]{:S(2)}, u32[]{:S(2)}) collective-permute-start(bf16[32,640]{1,0:T(8,128)(2,1)S(1)} %collective-permute-done.1.refs_2_), channel_id=1, source_target_pairs={{0,248},{4,252},{8,0},{12,4},{16,8},{20,12},{24,16},{28,20},{32,24... | collective-permute-start | bytes 122888 | tf_op jit(solution)/shard_map/ppermute | solution.py:442
  23.1 3.2 %collective-permute-start.10 = (bf16[16,896]{1,0:T(8,128)(2,1)S(1)}, bf16[16,896]{1,0:T(8,128)(2,1)S(1)}, u32[]{:S(2)}, u32[]{:S(2)}) collective-permute-start(bf16[16,896]{1,0:T(8,128)(2,1)S(1)} %collective-permute-done.9), channel_id=1, source_target_pairs={{0,2},{2,0},{1,3},{3,1},{4,6},{6,4},{5,7},{7,5},{8,10},{10,8},{9,1... | collective-permute-start | bytes 86024 | tf_op jit(solution)/shard_map/ppermute | solution.py:438
  24.7 4.4 %collective-permute-start.5 = (bf16[32,768]{1,0:T(8,128)(2,1)S(1)}, bf16[32,768]{1,0:T(8,128)(2,1)S(1)}, u32[]{:S(2)}, u32[]{:S(2)}) collective-permute-start(bf16[32,768]{1,0:T(8,128)(2,1)S(1)} %collective-permute-done.refs_1_), channel_id=1, source_target_pairs={{0,2},{2,0},{1,3},{3,1},{4,6},{6,4},{5,7},{7,5},{8,10},{10,8},{9,1... | collective-permute-start | bytes 147464 | tf_op jit(solution)/shard_map/ppermute | solution.py:438
  24.8 5.2 %collective-permute-start.7 = (bf16[32,768]{1,0:T(8,128)(2,1)S(1)}, bf16[32,768]{1,0:T(8,128)(2,1)S(1)}, u32[]{:S(2)}, u32[]{:S(2)}) collective-permute-start(bf16[32,768]{1,0:T(8,128)(2,1)S(1)} %collective-permute-done.2.refs_3_), channel_id=1, source_target_pairs={{0,2},{2,0},{1,3},{3,1},{4,6},{6,4},{5,7},{7,5},{8,10},{10,8},{9,1... | collective-permute-start | bytes 147464 | tf_op jit(solution)/shard_map/ppermute | solution.py:438
  26.4 2.7 %collective-permute-start.6 = (bf16[32,640]{1,0:T(8,128)(2,1)S(1)}, bf16[32,640]{1,0:T(8,128)(2,1)S(1)}, u32[]{:S(2)}, u32[]{:S(2)}) collective-permute-start(bf16[32,640]{1,0:T(8,128)(2,1)S(1)} %collective-permute-done.1.refs_2_), channel_id=1, source_target_pairs={{0,2},{2,0},{1,3},{3,1},{4,6},{6,4},{5,7},{7,5},{8,10},{10,8},{9,1... | collective-permute-start | bytes 122888 | tf_op jit(solution)/shard_map/ppermute | solution.py:438
  26.7 3.3 %collective-permute-start.8 = (bf16[32,640]{1,0:T(8,128)(2,1)S(1)}, bf16[32,640]{1,0:T(8,128)(2,1)S(1)}, u32[]{:S(2)}, u32[]{:S(2)}) collective-permute-start(bf16[32,640]{1,0:T(8,128)(2,1)S(1)} %collective-permute-done.3.refs_4_), channel_id=1, source_target_pairs={{0,2},{2,0},{1,3},{3,1},{4,6},{6,4},{5,7},{7,5},{8,10},{10,8},{9,1... | collective-permute-start | bytes 122888 | tf_op jit(solution)/shard_map/ppermute | solution.py:438
  41.3 4.2 %collective-permute-start.12 = (bf16[4,32,512]{2,1,0:T(8,128)(2,1)S(1)}, bf16[4,32,512]{2,1,0:T(8,128)(2,1)S(1)}, u32[]{:S(2)}, u32[]{:S(2)}) collective-permute-start(bf16[4,32,512]{2,1,0:T(8,128)(2,1)S(1)} %get-tuple-element.19), channel_id=1, source_target_pairs={{0,2},{2,0},{1,3},{3,1},{4,6},{6,4},{5,7},{7,5},{8,10},{10,8},{9,1... | collective-permute-start | bytes 393224 | tf_op jit(solution)/shard_map/ppermute | solution.py:438
  41.6 13.4 %all-to-all-start = ((f32[32,24,128]{2,1,0:T(8,128)}), f32[32,24,128]{2,1,0:T(8,128)S(1)}, u32[]{:S(2)}, u32[]{:S(2)}) async-start(f32[32,24,128]{2,1,0:T(8,128)} %bitcast.5), calls=%async_computation | async-start | bytes 786432 | tf_op jit(solution)/shard_map/all_to_all | solution.py:446
  45.6 8.1 %collective-permute-start.13 = (bf16[5,32,256]{2,1,0:T(8,128)(2,1)S(1)}, bf16[5,32,256]{2,1,0:T(8,128)(2,1)S(1)}, u32[]{:S(2)}, u32[]{:S(2)}) collective-permute-start(bf16[5,32,256]{2,1,0:T(8,128)(2,1)S(1)} %select_convert_fusion), channel_id=1, source_target_pairs={{0,1},{1,0},{2,3},{3,2},{4,5},{5,4},{6,7},{7,6},{8,9},{9,8},{10,11... | collective-permute-start | bytes 245768 | tf_op jit(solution)/shard_map/ppermute | solution.py:438
  55.8 16.2 %all-to-all-start.1 = ((f32[8,24,128]{2,1,0:T(8,128)}), f32[8,24,128]{2,1,0:T(8,128)S(1)}, u32[]{:S(2)}, u32[]{:S(2)}) async-start(f32[8,24,128]{2,1,0:T(8,128)} %broadcast_in_dim.7), calls=%async_computation.1 | async-start | bytes 196608 | tf_op jit(solution)/shard_map/all_to_all | solution.py:446
  62.7 16.6 %collective-permute-start.17 = (bf16[32,256]{1,0:T(8,128)(2,1)S(1)}, bf16[32,256]{1,0:T(8,128)(2,1)S(1)}, u32[]{:S(2)}, u32[]{:S(2)}) collective-permute-start(bf16[32,256]{1,0:T(8,128)(2,1)S(1)} %get-tuple-element.26), channel_id=1, source_target_pairs={{0,16},{4,20},{8,24},{12,28},{16,32},{20,36},{24,40},{28,44},{32,4... | collective-permute-start | bytes 49160 | tf_op jit(solution)/shard_map/ppermute | solution.py:442
  68.1 11.1 %collective-permute-start.16 = (bf16[32,256]{1,0:T(8,128)(2,1)S(1)}, bf16[32,256]{1,0:T(8,128)(2,1)S(1)}, u32[]{:S(2)}, u32[]{:S(2)}) collective-permute-start(bf16[32,256]{1,0:T(8,128)(2,1)S(1)} %get-tuple-element.27), channel_id=1, source_target_pairs={{0,12},{4,16},{8,20},{12,24},{16,28},{20,32},{24,36},{28,40},{32,4... | collective-permute-start | bytes 49160 | tf_op jit(solution)/shard_map/ppermute | solution.py:442
  68.4 10.9 %collective-permute-start.15 = (bf16[32,256]{1,0:T(8,128)(2,1)S(1)}, bf16[32,256]{1,0:T(8,128)(2,1)S(1)}, u32[]{:S(2)}, u32[]{:S(2)}) collective-permute-start(bf16[32,256]{1,0:T(8,128)(2,1)S(1)} %get-tuple-element.28), channel_id=1, source_target_pairs={{0,8},{4,12},{8,16},{12,20},{16,24},{20,28},{24,32},{28,36},{32,40... | collective-permute-start | bytes 49160 | tf_op jit(solution)/shard_map/ppermute | solution.py:442
  70.7 8.5 %collective-permute-start.14 = (bf16[32,256]{1,0:T(8,128)(2,1)S(1)}, bf16[32,256]{1,0:T(8,128)(2,1)S(1)}, u32[]{:S(2)}, u32[]{:S(2)}) collective-permute-start(bf16[32,256]{1,0:T(8,128)(2,1)S(1)} %get-tuple-element.29), channel_id=1, source_target_pairs={{0,4},{4,8},{8,12},{12,16},{16,20},{20,24},{24,28},{28,32},{32,36}... | collective-permute-start | bytes 49160 | tf_op jit(solution)/shard_map/ppermute | solution.py:442
  72.6 13.6 %all-to-all-start.2 = ((f32[16,24,128]{2,1,0:T(8,128)}), f32[16,24,128]{2,1,0:T(8,128)S(1)}, u32[]{:S(2)}, u32[]{:S(2)}) async-start(f32[16,24,128]{2,1,0:T(8,128)} %broadcast_in_dim.8), calls=%async_computation.2 | async-start | bytes 393216 | tf_op jit(solution)/shard_map/all_to_all | solution.py:446
